TPU v7x, 128 devices: a whole 4x4x4 slice. The times are simulated.
128 devices in a mesh: dp: 32 (over x, y, z_lo), mp: 4 (over z_hi, core).
Axes of the slice: x: 4, y: 4, z: 4 (z_hi: 2, z_lo: 2; z = z_hi * 2 + z_lo), core: 2. Of those that a mesh axis runs over, the one named last changes fastest.
Arguments:
- inputs: float32 [8192, 1024], P('dp'), may hold values from -6 to 6
- first_gain: float32 [1024], replicated, may hold values from 0.1 to 1.9
- first_shift: float32 [1024], replicated, may hold values from -3 to 3
- attend_weight: bfloat16 [3, 1024, 1024], P(None, None, 'mp'), may hold values from -0.25 to 0.25
- attend_bias: float32 [2, 1024], P(None, 'mp'), may hold values from -3 to 3
- output_weight: bfloat16 [1024, 1024], P('mp'), may hold values from -1 to 1
- output_bias: float32 [1024], replicated, may hold values from -3 to 3
- second_gain: float32 [1024], replicated, may hold values from 0.1 to 1.9
- second_shift: float32 [1024], replicated, may hold values from -3 to 3
- up_weight: bfloat16 [1024, 4096], P(None, 'mp'), may hold values from -0.1875 to 0.1875
- up_bias: float32 [4096], P('mp'), may hold values from -3 to 3
- down_weight: bfloat16 [4096, 1024], P('mp'), may hold values from -0.125 to 0.125
- down_bias: float32 [1024], replicated, may hold values from -3 to 3
- image_of: int32 [32], replicated, may hold values from 0 to 2, as said below
- cotangent: float32 [8192, 1024], P('dp'), may hold values from -6 to 6
Outputs:
- result: float32 [8192, 1024], P('dp')
- input_grad: float32 [8192, 1024], P('dp')
- first_gain_grad: float32 [1024], replicated
- first_shift_grad: float32 [1024], replicated
- attend_weight_grad: float32 [3, 1024, 1024], P(None, None, 'mp')
- attend_bias_grad: float32 [2, 1024], P(None, 'mp')
- output_weight_grad: float32 [1024, 1024], P('mp')
- output_bias_grad: float32 [1024], replicated
- second_gain_grad: float32 [1024], replicated
- second_shift_grad: float32 [1024], replicated
- up_weight_grad: float32 [1024, 4096], P(None, 'mp')
- up_bias_grad: float32 [4096], P('mp')
- down_weight_grad: float32 [4096, 1024], P('mp')
- down_bias_grad: float32 [1024], replicated
Inputs may be any that keep to these rules, and one draw needn't show every extreme that they name: `image_of`: three images: one holds the patches of 16 indices of dp, among them the first and the last index; the other two hold 8 indices each; which image is which is drawn.
All inputs are finite; a program needn't handle non-finite values.
Results may differ from a plain program's by a relative error of at most 0.035.
Values may be sent and summed in bfloat16 or wider, within the bound.
A program may use at most 128 MiB of HBM per device.

v0:
```python
import jax
import jax.numpy as jnp
from jax import lax
from jax.sharding import PartitionSpec as P

HEAD_DIM = 64


EPSILON = 1e-06


def layer_norm(values, norm_gain, norm_shift):
    row_mean = jnp.mean(values, axis=-1, keepdims=True)
    centred = values - row_mean
    variance = jnp.mean(centred * centred, axis=-1, keepdims=True)
    return centred * lax.rsqrt(variance + EPSILON) * norm_gain + norm_shift


def gelu_exact(values):
    return jax.nn.gelu(values, approximate=False)


def block_split(pieces, row_count):
    per_block = 1
    while pieces % (per_block * 2) == 0 and per_block * 2 * row_count <= 1024:
        per_block = per_block * 2
    return pieces // per_block


def contract_rows(left, right):
    return lax.dot_general(
        left, right, (((0,), (0,)), ((), ())), preferred_element_type=jnp.float32
    )


def contract_cols(left, right):
    return lax.dot_general(
        left, right, (((1,), (1,)), ((), ())), preferred_element_type=jnp.float32
    )


def per_device(
    inputs,
    first_gain,
    first_shift,
    attend_weight,
    attend_bias,
    output_weight,
    output_bias,
    second_gain,
    second_shift,
    up_weight,
    up_bias,
    down_weight,
    down_bias,
    image_of,
    cotangent,
):
    row_count = inputs.shape[0]
    local_width = attend_weight.shape[2]
    heads_here = local_width // HEAD_DIM
    factor = HEAD_DIM ** (-0.5)
    device_count = lax.axis_size("dp")
    own_image = image_of[lax.axis_index("dp")]
    blocks = block_split(device_count, row_count)
    key_image = jnp.repeat(image_of, row_count).reshape(blocks, -1)

    def touches(image_blk):
        return jnp.any(image_blk == own_image)

    normed_one, first_back = jax.vjp(layer_norm, inputs, first_gain, first_shift)
    first_low = normed_one.astype(jnp.bfloat16)
    projected = jnp.einsum(
        "td,cdf->ctf", first_low, attend_weight, preferred_element_type=jnp.float32
    )
    queries = (projected[0] + attend_bias[0]).astype(jnp.bfloat16)
    keys_low = projected[1].astype(jnp.bfloat16)
    values_low = (projected[2] + attend_bias[1]).astype(jnp.bfloat16)
    gathered = (
        lax.all_gather(keys_low, "dp", axis=0, tiled=True),
        lax.all_gather(values_low, "dp", axis=0, tiled=True),
    )

    def as_blocks(gathered_rows):
        return gathered_rows.reshape(blocks, -1, heads_here, HEAD_DIM)

    key_blocks = as_blocks(gathered[0])
    value_blocks = as_blocks(gathered[1])
    query_heads = queries.reshape(row_count, heads_here, HEAD_DIM)

    def masked_scores(keys_blk, image_blk):
        scores = (
            jnp.einsum("qhd,khd->hqk", query_heads, keys_blk, preferred_element_type=jnp.float32)
            * factor
        )
        allowed = (image_blk == own_image)[None, None, :]
        return (jnp.where(allowed, scores, -1e30), allowed)

    def stats_step(state_pair, block_item):

        def stats_work(pair):
            running_max, running_sum = pair
            scores, allowed = masked_scores(block_item[0], block_item[1])
            new_max = jnp.maximum(running_max, jnp.max(scores, axis=2))
            shifted = jnp.where(allowed, jnp.exp(scores - new_max[:, :, None]), 0.0)
            return (
                new_max,
                running_sum * jnp.exp(running_max - new_max) + jnp.sum(shifted, axis=2),
            )

        return (lax.cond(touches(block_item[1]), stats_work, lambda pair: pair, state_pair), None)

    start_max = jnp.full((heads_here, row_count), -1e30, jnp.float32)
    (final_max, final_sum), unused = lax.scan(
        stats_step, (start_max, jnp.zeros_like(start_max)), (key_blocks, key_image)
    )
    log_total = final_max + jnp.log(final_sum)

    def block_probs(keys_blk, image_blk):
        scores, allowed = masked_scores(keys_blk, image_blk)
        return jnp.where(allowed, jnp.exp(scores - log_total[:, :, None]), 0.0)

    def value_step(summed, block_item):

        def value_work(total):
            probs = block_probs(block_item[0], block_item[2])
            return total + jnp.einsum(
                "hqk,khd->qhd",
                probs.astype(jnp.bfloat16),
                block_item[1],
                preferred_element_type=jnp.float32,
            )

        return (lax.cond(touches(block_item[2]), value_work, lambda total: total, summed), None)

    attended, unused = lax.scan(
        value_step,
        jnp.zeros((row_count, heads_here, HEAD_DIM), jnp.float32),
        (key_blocks, value_blocks, key_image),
    )
    attended = attended.reshape(row_count, local_width)
    attended_low = attended.astype(jnp.bfloat16)
    head_total = lax.psum(
        jnp.dot(attended_low, output_weight, preferred_element_type=jnp.float32).astype(
            jnp.bfloat16
        ),
        "mp",
    ).astype(jnp.float32)
    hidden = inputs + head_total + output_bias
    normed_two, second_back = jax.vjp(layer_norm, hidden, second_gain, second_shift)
    second_low = normed_two.astype(jnp.bfloat16)
    pre_act = jnp.dot(second_low, up_weight, preferred_element_type=jnp.float32) + up_bias
    activated, gelu_back = jax.vjp(gelu_exact, pre_act)
    activated_low = activated.astype(jnp.bfloat16)
    unit_total = lax.psum(
        jnp.dot(activated_low, down_weight, preferred_element_type=jnp.float32).astype(
            jnp.bfloat16
        ),
        "mp",
    ).astype(jnp.float32)
    result = hidden + unit_total + down_bias
    down_grad = cotangent.astype(jnp.bfloat16)
    down_bias_grad = jnp.sum(down_grad.astype(jnp.float32), axis=0)
    down_weight_grad = contract_rows(activated_low, down_grad)
    (pre_grad,) = gelu_back(contract_cols(down_grad, down_weight))
    pre_low = pre_grad.astype(jnp.bfloat16)
    up_bias_grad = jnp.sum(pre_low.astype(jnp.float32), axis=0)
    up_weight_grad = contract_rows(second_low, pre_low)
    second_norm_grad = lax.psum(
        contract_cols(pre_low, up_weight).astype(jnp.bfloat16), "mp"
    ).astype(jnp.float32)
    hidden_part, second_gain_grad, second_shift_grad = second_back(second_norm_grad)
    hidden_grad = cotangent + hidden_part
    branch_low = hidden_grad.astype(jnp.bfloat16)
    output_bias_grad = jnp.sum(branch_low.astype(jnp.float32), axis=0)
    output_weight_grad = contract_rows(attended_low, branch_low)
    attended_grad = contract_cols(branch_low, output_weight).astype(jnp.bfloat16)
    grad_heads = attended_grad.reshape(row_count, heads_here, HEAD_DIM)
    row_delta = jnp.einsum(
        "qhd,qhd->hq",
        grad_heads.astype(jnp.float32),
        attended.reshape(row_count, heads_here, HEAD_DIM),
    )
    fresh = lax.optimization_barrier((keys_low, values_low, attended_grad))
    again = (
        lax.all_gather(fresh[0], "dp", axis=0, tiled=True),
        lax.all_gather(fresh[1], "dp", axis=0, tiled=True),
    )
    back_keys = as_blocks(again[0])
    back_values = as_blocks(again[1])

    def score_grads(keys_blk, values_blk, image_blk):
        probs = block_probs(keys_blk, image_blk)
        prob_grad = jnp.einsum(
            "qhd,khd->hqk", grad_heads, values_blk, preferred_element_type=jnp.float32
        )
        return (probs, (probs * (prob_grad - row_delta[:, :, None])).astype(jnp.bfloat16))

    zero_rows = jnp.zeros((row_count, heads_here, HEAD_DIM), jnp.float32)

    def grad_step(summed, block_item):
        keys_blk, values_blk, image_blk = block_item
        empty_part = jnp.zeros(keys_blk.shape, jnp.float32)

        def grad_work(total):
            probs, score_grad = score_grads(keys_blk, values_blk, image_blk)
            total = total + jnp.einsum(
                "hqk,khd->qhd", score_grad, keys_blk, preferred_element_type=jnp.float32
            )
            key_part = (
                jnp.einsum(
                    "hqk,qhd->khd", score_grad, query_heads, preferred_element_type=jnp.float32
                )
                * factor
            )
            value_part = jnp.einsum(
                "hqk,qhd->khd",
                probs.astype(jnp.bfloat16),
                grad_heads,
                preferred_element_type=jnp.float32,
            )
            return (total, (key_part, value_part))

        return lax.cond(
            touches(image_blk), grad_work, lambda total: (total, (empty_part, empty_part)), summed
        )

    query_sum, (key_terms, value_terms) = lax.scan(
        grad_step, zero_rows, (back_keys, back_values, key_image)
    )
    key_terms = key_terms.reshape(-1, local_width)
    value_terms = value_terms.reshape(-1, local_width)
    key_share, value_share = (
        lax.psum_scatter(
            key_terms.astype(jnp.bfloat16), "dp", scatter_dimension=0, tiled=True
        ).astype(jnp.float32),
        lax.psum_scatter(
            value_terms.astype(jnp.bfloat16), "dp", scatter_dimension=0, tiled=True
        ).astype(jnp.float32),
    )
    query_low = (query_sum.reshape(row_count, local_width) * factor).astype(jnp.bfloat16)
    key_low_grad = key_share.astype(jnp.bfloat16)
    value_low_grad = value_share.astype(jnp.bfloat16)
    stacked = jnp.stack([query_low, key_low_grad, value_low_grad])
    attend_weight_grad = jnp.einsum(
        "td,ctf->cdf", first_low, stacked, preferred_element_type=jnp.float32
    )
    attend_bias_grad = jnp.stack(
        [
            jnp.sum(query_low.astype(jnp.float32), axis=0),
            jnp.sum(value_low_grad.astype(jnp.float32), axis=0),
        ]
    )
    first_norm_grad = lax.psum(
        jnp.einsum(
            "ctf,cdf->td", stacked, attend_weight, preferred_element_type=jnp.float32
        ).astype(jnp.bfloat16),
        "mp",
    ).astype(jnp.float32)
    input_part, first_gain_grad, first_shift_grad = first_back(first_norm_grad)
    input_grad = hidden_grad + input_part
    summed_grads = (
        lax.psum(first_gain_grad.astype(jnp.bfloat16), "dp").astype(jnp.float32),
        lax.psum(first_shift_grad.astype(jnp.bfloat16), "dp").astype(jnp.float32),
        lax.psum(attend_weight_grad.astype(jnp.bfloat16), "dp").astype(jnp.float32),
        lax.psum(attend_bias_grad.astype(jnp.bfloat16), "dp").astype(jnp.float32),
        lax.psum(output_weight_grad.astype(jnp.bfloat16), "dp").astype(jnp.float32),
        lax.psum(output_bias_grad.astype(jnp.bfloat16), "dp").astype(jnp.float32),
        lax.psum(second_gain_grad.astype(jnp.bfloat16), "dp").astype(jnp.float32),
        lax.psum(second_shift_grad.astype(jnp.bfloat16), "dp").astype(jnp.float32),
        lax.psum(up_weight_grad.astype(jnp.bfloat16), "dp").astype(jnp.float32),
        lax.psum(up_bias_grad.astype(jnp.bfloat16), "dp").astype(jnp.float32),
        lax.psum(down_weight_grad.astype(jnp.bfloat16), "dp").astype(jnp.float32),
        lax.psum(down_bias_grad.astype(jnp.bfloat16), "dp").astype(jnp.float32),
    )
    return (
        result,
        input_grad,
        summed_grads[0],
        summed_grads[1],
        summed_grads[2],
        summed_grads[3],
        summed_grads[4],
        summed_grads[5],
        summed_grads[6],
        summed_grads[7],
        summed_grads[8],
        summed_grads[9],
        summed_grads[10],
        summed_grads[11],
    )


def solution(mesh):
    in_specs = (
        P("dp", None),
        P(),
        P(),
        P(None, None, "mp"),
        P(None, "mp"),
        P("mp", None),
        P(),
        P(),
        P(),
        P(None, "mp"),
        P("mp"),
        P("mp", None),
        P(),
        P(),
        P("dp", None),
    )
    out_specs = (
        P("dp", None),
        P("dp", None),
        P(),
        P(),
        P(None, None, "mp"),
        P(None, "mp"),
        P("mp", None),
        P(),
        P(),
        P(),
        P(None, "mp"),
        P("mp"),
        P("mp", None),
        P(),
    )
    return jax.shard_map(
        per_device, mesh=mesh, in_specs=in_specs, out_specs=out_specs, check_vma=False
    )
```

profile of v0, /device:TPU:0, one launch (start us, length us, event | category | flops | bytes accessed | tf_op | source)
XLA Modules:
  0.0 1711.0 jit_solution(13563888217300171599)
XLA Ops:
  16.4 157.9 %all-gather.12.cloned.1.call-done = bf16[1,8192,256]{1,2,0:T(8,128)(2,1)} async-done(((bf16[1,256,256]{1,2,0:T(8,128)(2,1)}), bf16[1,8192,256]{1,2,0:T(8,128)(2,1)}) %all-gather.12.cloned.1.call-update) | async-done | bytes 4194320 | tf_op jit(solution)/shard_map/all_gather | solution.py:80
  174.3 8.5 copy.72
  182.8 10.3 copy.45
  193.1 6.5 copy.44
  199.7 48.9 %while.42 = (s32[]{:T(128)}, f32[4,256]{1,0:T(4,128)S(1)}, f32[4,256]{1,0:T(4,128)S(1)}, s32[8,1024]{1,0:T(8,128)S(1)}, s32[]{:T(128)}, /*index=5*/bf16[8,1024,4...) while((s32[]{:T(128)}, f32[4,256]{1,0:T(4,128)S(1)}, f32[4,256]{1,0:T(4,128)S(1)}, ...), condition=%wide.region_8.9_spmd, body=%wide.region_2.8_spmd.sunk | while | flops 142611456 | bytes 9117391 | solution.py:114
  207.7 4.2 conditional.6
  213.8 4.1 conditional.6
  248.6 79.2 %all-gather.6.cloned.1.call-done = bf16[8192,256]{0,1:T(8,128)(2,1)} async-done(((bf16[256,256]{0,1:T(8,128)(2,1)}), bf16[8192,256]{0,1:T(8,128)(2,1)}) %all-gather.6.cloned.1.call-update) | async-done | bytes 4194320 | tf_op jit(solution)/shard_map/all_gather | solution.py:81
  327.7 6.5 copy.73
  334.3 4.3 copy.47
  339.2 70.1 %while.43 = (s32[]{:T(128)}, f32[256,4,64]{0,2,1:T(8,128)S(1)}, s32[8,1024]{1,0:T(8,128)}, s32[]{:T(128)}, bf16[8,1024,4,64]{3,2,1,0:T(4,128)(2,1)}, /*index=5*/...) while((s32[]{:T(128)}, f32[256,4,64]{0,2,1:T(8,128)S(1)}, ...), condition=%wide.region_13.14_spmd, body=%wide.region_9.13_spmd.sunk | while | flops 273746944 | bytes 3431107 | solution.py:136
  342.0 6.1 conditional.7
  350.8 6.1 conditional.7
  359.5 6.1 conditional.7
  368.3 6.1 conditional.7
  377.0 6.1 conditional.7
  385.8 6.1 conditional.7
  394.5 6.1 conditional.7
  403.3 6.1 conditional.7
  412.3 42.6 %all-reduce.8.cloned.1.call-done = bf16[256,1024]{1,0:T(8,128)(2,1)} async-done(((bf16[256,1024]{1,0:T(8,128)(2,1)}), bf16[256,1024]{1,0:T(8,128)(2,1)}) %all-reduce.8.cloned.1.call-update) | async-done | bytes 524304 | tf_op jit(solution)/shard_map/psum | solution.py:143
  457.2 4.6 multiply_convert_fusion.1
  467.6 39.7 %all-reduce.10.cloned.1.call-done = bf16[256,1024]{1,0:T(8,128)(2,1)} async-done(((bf16[256,1024]{1,0:T(8,128)(2,1)}), bf16[256,1024]{1,0:T(8,128)(2,1)}) %all-reduce.10.cloned.1.call-update) | async-done | bytes 524304 | tf_op jit(solution)/shard_map/psum | solution.py:169
  517.2 8.8 reduce-scatter.5.cloned.1.call-start
  526.0 145.8 %all-gather.8.cloned.1.call-done = bf16[8192,256]{0,1:T(8,128)(2,1)} async-done(((bf16[256,256]{0,1:T(8,128)(2,1)}), bf16[8192,256]{0,1:T(8,128)(2,1)}) %all-gather.8.cloned.1.call-update) | async-done | bytes 4194320 | tf_op jit(solution)/shard_map/all_gather | solution.py:186
  671.8 6.5 copy.74
  678.4 4.3 copy.48
  682.6 149.3 %all-gather.10.cloned.1.call-done = bf16[8192,256]{0,1:T(8,128)(2,1)} async-done(((bf16[256,256]{0,1:T(8,128)(2,1)}), bf16[8192,256]{0,1:T(8,128)(2,1)}) %all-gather.10.cloned.1.call-update) | async-done | bytes 4194320 | tf_op jit(solution)/shard_map/all_gather | solution.py:187
  831.9 6.5 copy.75
  838.5 4.5 copy.49
  843.0 99.9 %while.44 = (s32[]{:T(128)}, f32[256,4,64]{0,2,1:T(8,128)S(1)}, bf16[8,1024,4,64]{1,3,2,0:T(8,128)(2,1)}, bf16[8,1024,4,64]{1,3,2,0:T(8,128)(2,1)}, s32[8,1024]{...) while((s32[]{:T(128)}, f32[256,4,64]{0,2,1:T(8,128)S(1)}, ...), condition=%wide.region_25.26_spmd, body=%wide.region_21.0_spmd.sunk | while | flops 684264448 | bytes 24675584 | solution.py:228
  845.7 8.8 conditional.8
  858.2 8.8 conditional.8
  870.7 8.8 conditional.8
  883.2 8.8 conditional.8
  895.7 8.8 conditional.8
  908.1 8.8 conditional.8
  920.6 8.8 conditional.8
  933.1 8.8 conditional.8
  943.0 12.7 copy.69
  955.7 12.7 reshape.165
  968.5 12.8 copy.68
  981.2 12.7 reshape.164
  998.9 136.0 %reduce-scatter.5.cloned.1.call-done = bf16[256,256]{1,0:T(8,128)(2,1)} async-done(((bf16[8192,256]{1,0:T(8,128)(2,1)}), bf16[256,256]{1,0:T(8,128)(2,1)}) %reduce-scatter.5.cloned.1.call-update) | async-done | bytes 131088 | tf_op jit(solution)/shard_map/reduce_scatter | solution.py:237
  1134.9 168.2 %reduce-scatter.3.cloned.1.call-done = bf16[256,256]{1,0:T(8,128)(2,1)} async-done(((bf16[8192,256]{1,0:T(8,128)(2,1)}), bf16[256,256]{1,0:T(8,128)(2,1)}) %reduce-scatter.3.cloned.1.call-update) | async-done | bytes 131088 | tf_op jit(solution)/shard_map/reduce_scatter | solution.py:234
  1317.4 30.5 %all-reduce.14.cloned.1.call-done = (bf16[256,1024]{1,0:T(8,128)(2,1)}, bf16[256,1024]{1,0:T(8,128)(2,1)}) async-done(((bf16[256,1024]{1,0:T(8,128)(2,1)}, bf16[256,1024]{1,0:T(8,128)(2,1)}), (bf16[256,1024]{1,0:T(8,128)(2,1)}, bf16[256,1024]{1,0:T(8,128)(2,1)})) %all-reduce.14.cloned.1.call-update) | async-done | bytes 1048592 | tf_op jit(solution)/shard_map/psum | solution.py:155
  1352.0 158.4 %all-reduce = (bf16[1024]{0:T(1024)(128)(2,1)S(1)}, bf16[1024]{0:T(1024)(128)(2,1)S(1)}, bf16[2,256]{1,0:T(2,128)(2,1)S(1)}, bf16[1024]{0:T(1024)(128)(2,1)S(1)}...) all-reduce(bf16[1024]{0:T(1024)(128)(2,1)S(1)} %get-tuple-element.4, ...), channel_id=1, replica_groups=mesh['dp'=32,'mp'=4] {'dp'}, use_global_device_ids=true, to_apply=%region_32.33 | all-reduce | flops 7680 | bytes 30720 | tf_op jit(solution)/shard_map/psum | solution.py:263
  1518.5 174.3 %all-reduce.12.cloned.1.call-done = (bf16[3,1024,256]{1,2,0:T(8,128)(2,1)}, bf16[256,1024]{1,0:T(8,128)(2,1)}, bf16[1024,1024]{1,0:T(8,128)(2,1)}, bf16[1024,1024]{1,0:T(8,128)(2,1)}) async-done(((bf16[3,1024,256]{1,2,0:T(8,128)(2,1)}, bf16[256,1024]{1,0:T(8,128)(2,1)}, bf16[1024,1024]{1,0:T(8,128)(2,1)}, bf16[1024,1024]{1,0:T(8,128)(2,1)}), (bf16[3,1024,256]{1,2,0:T(8,128)(2,1)}, ...) | async-done | bytes 6291472 | tf_op jit(solution)/shard_map/psum | solution.py:265
  1697.0 4.2 convert_element_type.232
  (363 shorter events, 294.9 us)
Async XLA Ops:
  7.2 450.0 %copy-start = (bf16[1024,1024]{1,0:T(8,128)(2,1)S(1)}, bf16[1024,1024]{1,0:T(8,128)(2,1)}, u32[]{:S(2)}) copy-start(bf16[1024,1024]{1,0:T(8,128)(2,1)} %param.36) | copy-start | bytes 6291460
  7.2 6.5 copy-start.42
  7.2 7.4 copy-start.43
  7.2 167.1 %all-gather.12.cloned.1.call-start = ((), (), s32[]{:S(2)}) async-start(), calls=%async_computation.9 | async-start | bytes 4325376 | tf_op jit(solution)/shard_map/all_gather | solution.py:80
  10.2 5.2 copy-start.30
  12.9 169.9 %copy-start.14 = (f32[3,256,256]{1,2,0:T(8,128)}, f32[3,256,256]{1,2,0:T(8,128)S(1)}, u32[]{:S(2)}) copy-start(f32[3,256,256]{1,2,0:T(8,128)S(1)} %convolution_bitcast_fusion.2) | copy-start | bytes 2359300
  13.6 314.1 %all-gather.6.cloned.1.call-start = ((), (), s32[]{:S(2)}) async-start(), calls=%async_computation.2 | async-start | bytes 4325376 | tf_op jit(solution)/shard_map/all_gather | solution.py:81
  14.5 440.4 %all-reduce.8.cloned.1.call-start = ((), (), s32[]{:S(2)}) async-start(), calls=%async_computation.3 | async-start | bytes 1048576 | tf_op jit(solution)/shard_map/psum | solution.py:143
  248.6 85.7 %copy-start.19 = (s32[8,1024]{1,0:T(8,128)}, s32[8,1024]{1,0:T(8,128)S(1)}, u32[]{:S(2)}) copy-start(s32[8,1024]{1,0:T(8,128)S(1)} %get-tuple-element.889) | copy-start | bytes 98308
  339.2 115.7 %copy-start.2 = (f32[256,1024]{1,0:T(8,128)S(1)}, f32[256,1024]{1,0:T(8,128)}, u32[]{:S(2)}) copy-start(f32[256,1024]{1,0:T(8,128)} %param.27) | copy-start | bytes 3145732
  339.2 115.7 %copy-start.36 = (f32[1024]{0:T(1024)S(1)}, f32[1024]{0:T(1024)}, u32[]{:S(2)}) copy-start(f32[1024]{0:T(1024)} %param.33) | copy-start | bytes 12292
  409.4 47.7 %copy-start.22 = (f32[1024]{0:T(1024)S(1)}, f32[1024]{0:T(1024)}, u32[]{:S(2)}) copy-start(f32[1024]{0:T(1024)} %param.34) | copy-start | bytes 12292
  412.3 95.1 %all-reduce.10.cloned.1.call-start = ((), (), s32[]{:S(2)}) async-start(), calls=%async_computation.4 | async-start | bytes 1048576 | tf_op jit(solution)/shard_map/psum | solution.py:169
  456.2 5.6 copy-start.3
  457.1 53.3 %copy-start.24 = (f32[256]{0:T(256)}, f32[256]{0:T(256)S(1)}, u32[]{:S(2)}) copy-start(f32[256]{0:T(256)S(1)} %fusion.64) | copy-start | bytes 3076
  457.1 4.7 copy-start.5
  457.2 4.7 copy-start.44
  465.9 46.4 %copy-start.6 = (f32[256,1024]{1,0:T(8,128)S(1)}, f32[256,1024]{1,0:T(8,128)}, u32[]{:S(2)}) copy-start(f32[256,1024]{1,0:T(8,128)} %param.41) | copy-start | bytes 3145732
  465.9 205.9 %all-gather.8.cloned.1.call-start = ((), (), s32[]{:S(2)}) async-start(), calls=%async_computation.5 | async-start | bytes 4325376 | tf_op jit(solution)/shard_map/all_gather | solution.py:186
  512.2 166.1 %copy-start.8 = (f32[256,1024]{1,0:T(8,128)}, f32[256,1024]{1,0:T(8,128)S(1)}, u32[]{:S(2)}) copy-start(f32[256,1024]{1,0:T(8,128)S(1)} %get-tuple-element.529) | copy-start | bytes 3145732
  512.2 166.1 %copy-start.28 = (f32[256]{0:T(256)}, f32[256]{0:T(256)S(1)}, u32[]{:S(2)}) copy-start(f32[256]{0:T(256)S(1)} %negate_multiply_fusion.2) | copy-start | bytes 3076
  516.6 315.3 %all-gather.10.cloned.1.call-start = ((), (), s32[]{:S(2)}) async-start(), calls=%async_computation.6 | async-start | bytes 4325376 | tf_op jit(solution)/shard_map/all_gather | solution.py:187
  517.2 617.7 %reduce-scatter.5.cloned.1.call-start = ((), (), s32[]{:S(2)}) async-start(), calls=%async_computation.8 | async-start | bytes 4325376 | tf_op jit(solution)/shard_map/reduce_scatter | solution.py:237
  838.4 4.6 copy-start.21
  838.4 4.6 copy-start.38
  968.4 334.6 %reduce-scatter.3.cloned.1.call-start = ((), (), s32[]{:S(2)}) async-start(), calls=%async_computation.7 | async-start | bytes 4325376 | tf_op jit(solution)/shard_map/reduce_scatter | solution.py:234
  994.0 353.9 %all-reduce.14.cloned.1.call-start = ((), (), s32[]{:S(2)}) async-start(), calls=%async_computation.11 | async-start | bytes 2097152 | tf_op jit(solution)/shard_map/psum | solution.py:155
  998.1 311.8 %copy-start.4 = (f32[256,1024]{1,0:T(8,128)S(1)}, f32[256,1024]{1,0:T(8,128)}, u32[]{:S(2)}) copy-start(f32[256,1024]{1,0:T(8,128)} %copy-done.3) | copy-start | bytes 3145732
  998.1 311.8 %copy-start.16 = (bf16[256,1024]{1,0:T(8,128)(2,1)S(1)}, bf16[256,1024]{1,0:T(8,128)(2,1)}, u32[]{:S(2)}) copy-start(bf16[256,1024]{1,0:T(8,128)(2,1)} %copy-done.15) | copy-start | bytes 1572868
  1306.0 6.8 copy-start.10
  1306.0 6.8 copy-start.13
  1306.1 7.8 copy-start.20
  1306.1 7.8 copy-start.23
  1306.1 386.7 %all-reduce.12.cloned.1.call-start = ((), (), s32[]{:S(2)}) async-start(), calls=%async_computation.10 | async-start | bytes 12582912 | tf_op jit(solution)/shard_map/psum | solution.py:265
  1306.4 7.5 copy-start.26
  1306.4 7.5 copy-start.45
  1306.4 7.5 copy-start.46
  1315.8 34.5 %copy-start.31 = (f32[256]{0:T(256)S(1)}, f32[256]{0:T(256)}, u32[]{:S(2)}) copy-start(f32[256]{0:T(256)} %copy-done.30) | copy-start | bytes 3076
  1315.9 34.6 %copy-start.27 = (f32[256]{0:T(256)S(1)}, f32[256]{0:T(256)}, u32[]{:S(2)}) copy-start(f32[256]{0:T(256)} %copy-done.25) | copy-start | bytes 3076
  1315.9 36.2 %copy-start.33 = (bf16[1024]{0:T(1024)(128)(2,1)S(1)}, bf16[1024]{0:T(1024)(128)(2,1)}, u32[]{:S(2)}) copy-start(bf16[1024]{0:T(1024)(128)(2,1)} %get-tuple-element.454) | copy-start | bytes 6148
  1315.9 36.2 %copy-start.34 = (bf16[1024]{0:T(1024)(128)(2,1)S(1)}, bf16[1024]{0:T(1024)(128)(2,1)}, u32[]{:S(2)}) copy-start(bf16[1024]{0:T(1024)(128)(2,1)} %get-tuple-element.524) | copy-start | bytes 6148
  1315.9 36.2 %copy-start.35 = (bf16[1024]{0:T(1024)(128)(2,1)S(1)}, bf16[1024]{0:T(1024)(128)(2,1)}, u32[]{:S(2)}) copy-start(bf16[1024]{0:T(1024)(128)(2,1)} %get-tuple-element.538) | copy-start | bytes 6148
  1315.9 36.2 %copy-start.41 = (bf16[1024]{0:T(1024)(128)(2,1)S(1)}, bf16[1024]{0:T(1024)(128)(2,1)}, u32[]{:S(2)}) copy-start(bf16[1024]{0:T(1024)(128)(2,1)} %get-tuple-element.544) | copy-start | bytes 6148
  1315.9 199.3 %copy-start.7 = (f32[256,1024]{1,0:T(8,128)S(1)}, f32[256,1024]{1,0:T(8,128)}, u32[]{:S(2)}) copy-start(f32[256,1024]{1,0:T(8,128)} %param.41) | copy-start | bytes 3145732
  1315.9 199.3 %copy-start.29 = (f32[256]{0:T(256)S(1)}, f32[256]{0:T(256)}, u32[]{:S(2)}) copy-start(f32[256]{0:T(256)} %copy-done.28) | copy-start | bytes 3076
  1315.9 199.3 %copy-start.37 = (f32[1024]{0:T(1024)S(1)}, f32[1024]{0:T(1024)}, u32[]{:S(2)}) copy-start(f32[1024]{0:T(1024)} %param.39) | copy-start | bytes 12292
  1695.9 5.3 copy-start.11
  1697.0 6.7 copy-start.1
  (9 other events, 17.3 us)
Sparse Core Ops, SparseCore 0:
  13.8 160.4 all-gather.11
  175.9 151.8 all-gather.5
  412.4 42.5 all-reduce.7
  466.0 41.2 all-reduce.9
  516.7 155.0 all-gather.7
  673.3 158.6 all-gather.9
  968.5 166.3 reduce-scatter.4
  1137.9 165.1 reduce-scatter.2
  1306.2 41.6 all-reduce.13
  1351.9 340.8 all-reduce.11
where the time goes:
time: 1730 us; the launch traced here: 1710 us
  waiting for transfers between devices  1120 us (65%)
  local copies, waits for them, and re-layouts  162 us (9%)
  blocking collectives  158 us (9%)
  matrix products  135 us (8%)
  other arithmetic  89.2 us (5%)
  loops' own time  17.4 us (1%)
    psum x1, waiting for transfers between devices, per_device(): lax.psum(attend_weight_grad.astype(jnp.bfloat16), 'dp').astype(jnp.float32)  174 us
    reduce_scatter x1, waiting for transfers between devices, per_device(): lax.psum_scatter(key_terms.astype(jnp.bfloat16), 'dp', scatter_dimension=...  168 us
    psum x1, blocking collectives, per_device(): lax.psum(first_gain_grad.astype(jnp.bfloat16), 'dp').astype(jnp.float32)  158 us
    all_gather x1, waiting for transfers between devices, per_device(): lax.all_gather(keys_low, 'dp', axis=0, tiled=True)  158 us
    all_gather x1, waiting for transfers between devices, per_device(): lax.all_gather(fresh[1], 'dp', axis=0, tiled=True)  149 us
    all_gather x1, waiting for transfers between devices, per_device(): lax.all_gather(fresh[0], 'dp', axis=0, tiled=True)  146 us
    reduce_scatter x1, waiting for transfers between devices, per_device(): lax.psum_scatter(value_terms.astype(jnp.bfloat16), 'dp', scatter_dimensio...  136 us
    all_gather x1, waiting for transfers between devices, per_device(): lax.all_gather(values_low, 'dp', axis=0, tiled=True)  79.2 us
  transfers between devices with their start and end apart: 10, of which 10 were waited for; matrix products, arithmetic and copies ran while one was open for 8% of the time, Pallas kernels for 0%

commit v1 on v0

--- a/solution.py
+++ b/solution.py
@@ -1,12 +1,356 @@
+import functools
+
 import jax
 import jax.numpy as jnp
 from jax import lax
+from jax.experimental import pallas as pl
+from jax.experimental.pallas import tpu as pltpu
 from jax.sharding import PartitionSpec as P
 
 HEAD_DIM = 64
-
-
 EPSILON = 1e-06
+LOWEST = -1e30
+HIGHEST = 1e30
+MESH = pl.DeviceIdType.MESH
+F32 = jnp.float32
+BF16 = jnp.bfloat16
+VMEM_BYTES = 60 * 2**20
+
+
+def dot_nn(left, right):
+    return lax.dot_general(left, right, (((1,), (0,)), ((), ())), preferred_element_type=F32)
+
+
+def dot_nt(left, right):
+    return lax.dot_general(left, right, (((1,), (1,)), ((), ())), preferred_element_type=F32)
+
+
+def dot_tn(left, right):
+    return lax.dot_general(left, right, (((0,), (0,)), ((), ())), preferred_element_type=F32)
+
+
+class Place:
+    def __init__(self):
+        data, model = lax.axis_index("dp"), lax.axis_index("mp")
+        self.x = lax.div(data, 8)
+        self.y = lax.rem(lax.div(data, 2), 4)
+        self.z = lax.rem(data, 2)
+        self.high = lax.div(model, 2)
+        self.core = lax.rem(model, 2)
+        self.group = self.y * 2 + self.z
+
+    def at(self, dx=0, dy=0, dz=0, dhigh=0, dcore=0):
+        x = lax.rem(self.x + dx, 4)
+        y = lax.rem(self.y + dy, 4)
+        z = lax.rem(self.z + dz, 2)
+        high = lax.rem(self.high + dhigh, 2)
+        core = lax.rem(self.core + dcore, 2)
+        return (x * 8 + y * 2 + z, high * 2 + core)
+
+
+class Links:
+    def __init__(self, send_sem, recv_sem):
+        self.send_sem, self.recv_sem = send_sem, recv_sem
+        self.used = 0
+        self.sent = []
+
+    def copy(self, source, target, device):
+        at = self.used
+        self.used += 1
+        made = pltpu.make_async_remote_copy(
+            src_ref=source,
+            dst_ref=target,
+            send_sem=self.send_sem.at[at],
+            recv_sem=self.recv_sem.at[at],
+            device_id=device,
+            device_id_type=MESH,
+        )
+        self.sent.append(made)
+        return made
+
+    def send(self, source, target, device):
+        made = self.copy(source, target, device)
+        made.start()
+        return made
+
+    def finish(self):
+        for made in self.sent:
+            made.wait_send()
+        self.sent = []
+
+
+def greet(partners):
+    barrier = pltpu.get_barrier_semaphore()
+    for device in partners:
+        pl.semaphore_signal(barrier, inc=1, device_id=device, device_id_type=MESH)
+    return lambda: pl.semaphore_wait(barrier, len(partners))
+
+
+def all_partners(me):
+    return [
+        me.at(dx=1), me.at(dx=3), me.at(dx=2), me.at(dy=1), me.at(dy=3),
+        me.at(dz=1), me.at(dhigh=1), me.at(dcore=1),
+    ]
+
+
+def row_norm(values):
+    mean = jnp.mean(values, axis=-1, keepdims=True)
+    centred = values - mean
+    variance = jnp.mean(centred * centred, axis=-1, keepdims=True)
+    inverse = lax.rsqrt(variance + EPSILON)
+    return centred * inverse, inverse
+
+
+def spread(column):
+    return jnp.broadcast_to(column, (column.shape[0], 128))
+
+
+class Gather:
+    def __init__(self, me, links, slots, rows):
+        self.me, self.links, self.slots = me, links, slots
+        self.low = pl.ds(0, rows // 2)
+        self.high = pl.ds(rows // 2, rows // 2)
+        self.other = 1 - me.z
+
+    def slot(self, dy, z):
+        return lax.rem(self.me.y + dy, 4) * 2 + z
+
+    def send(self, slot, device):
+        return self.links.send(self.slots.at[slot], self.slots.at[slot], device)
+
+    def begin(self):
+        me = self.me
+        own = me.group
+        self.from_z = self.send(own, me.at(dz=1))
+        self.own_y = [self.send(own, me.at(dy=1)), self.send(own, me.at(dy=3))]
+
+    def pass_z(self):
+        me = self.me
+        self.from_z.wait_recv()
+        slot = self.slot(0, self.other)
+        self.other_y = [self.send(slot, me.at(dy=1)), self.send(slot, me.at(dy=3))]
+
+    def forward(self, pair, z):
+        me = self.me
+        pair[0].wait_recv()
+        below = self.slot(3, z)
+        up = self.links.send(
+            self.slots.at[below, self.low], self.slots.at[below, self.low], me.at(dy=1)
+        )
+        pair[1].wait_recv()
+        above = self.slot(1, z)
+        down = self.links.send(
+            self.slots.at[above, self.high], self.slots.at[above, self.high], me.at(dy=3)
+        )
+        return [up, down]
+
+    def pass_own(self):
+        self.far_own = self.forward(self.own_y, self.me.z)
+
+    def pass_other(self):
+        self.far_other = self.forward(self.other_y, self.other)
+
+    def end_own(self):
+        for made in self.far_own:
+            made.wait_recv()
+
+    def end_other(self):
+        for made in self.far_other:
+            made.wait_recv()
+
+
+def attention_kernel(
+    x_ref, gain_ref, shift_ref, weight_ref, bias_ref, output_ref, image_ref,
+    first_out, kv_out, query_out, mixed_out, stats_out, attended_out, output_out,
+    kv, query_pair, kv_send, query_send, query_own, top, total, mixed,
+    head_send, head_recv, attended, output_all, send_sem, recv_sem,
+):
+    me = Place()
+    links = Links(send_sem, recv_sem)
+    wait_all = greet(all_partners(me))
+
+    normed, _ = row_norm(x_ref[...])
+    first_low = (normed * gain_ref[...] + shift_ref[...]).astype(BF16)
+    first_out[...] = first_low
+    keys = dot_nn(first_low, weight_ref[1])
+    values = dot_nn(first_low, weight_ref[2]) + bias_ref[1:2, :]
+    for head in range(4):
+        part = slice(head * HEAD_DIM, (head + 1) * HEAD_DIM)
+        kv_send[head] = jnp.concatenate([keys[:, part], values[:, part]], axis=1).astype(BF16)
+    queries = dot_nn(first_low, weight_ref[0]) + bias_ref[0:1, :]
+    queries = queries.astype(BF16).astype(F32) * (HEAD_DIM**-0.5)
+    for head in range(4):
+        part = slice(head * HEAD_DIM, (head + 1) * HEAD_DIM)
+        query_send[head] = jnp.concatenate(
+            [queries[:128, part], queries[128:, part]], axis=1
+        ).astype(BF16)
+
+    wait_all()
+    own = me.group
+    kv_moves, query_moves = [], []
+    for step in (1, 3, 2):
+        head = lax.rem(me.x + step, 4)
+        kv_moves.append(
+            links.send(kv_send.at[head], kv.at[own, pl.ds(me.x * 256, 256)], me.at(dx=step))
+        )
+    for step in (1, 3, 2):
+        head = lax.rem(me.x + step, 4)
+        query_moves.append(
+            links.send(
+                query_send.at[head], query_pair.at[own, pl.ds(me.x * 128, 128)], me.at(dx=step)
+            )
+        )
+    kv[own, pl.ds(me.x * 256, 256), :] = kv_send[me.x]
+    query_pair[own, pl.ds(me.x * 128, 128), :] = query_send[me.x]
+    attended_at = me.high * 2 + me.core
+
+    for made in kv_moves:
+        made.wait_recv()
+    gather = Gather(me, links, kv, 1024)
+    gather.begin()
+    output_all[attended_at] = output_ref[...]
+    output_high = links.send(output_ref, output_all.at[attended_at], me.at(dhigh=1))
+    output_core = links.send(output_ref, output_all.at[attended_at], me.at(dcore=1))
+    for made in query_moves:
+        made.wait_recv()
+    for block in range(4):
+        pair = query_pair[own, block * 128 : (block + 1) * 128, :].astype(F32)
+        both = jnp.concatenate([pair, pltpu.roll(pair, 64, 1)], axis=0)
+        lane = lax.broadcasted_iota(jnp.int32, both.shape, 1)
+        query_own[block * 256 : (block + 1) * 256, :] = jnp.where(
+            lane < HEAD_DIM, both, 0.0
+        ).astype(BF16)
+    query_gather = Gather(me, links, query_pair, 512)
+    top[...] = jnp.full(top.shape, LOWEST, F32)
+    total[...] = jnp.zeros(total.shape, F32)
+    mixed[...] = jnp.zeros(mixed.shape, F32)
+
+    def attend(slot):
+        @pl.loop(0, 4)
+        def _(block):
+            rows = pl.ds(pl.multiple_of(block * 256, 256), 256)
+            query = query_own[rows, :]
+            mine = image_ref[block * 8 + own]
+            scores, shut = [], []
+            highest = None
+            for part in range(4):
+                same = image_ref[part * 8 + slot] == mine
+                shut.append(jnp.where(same, -3e38, HIGHEST))
+                score = dot_nt(query, kv[slot, part * 256 : (part + 1) * 256, :])
+                scores.append(score)
+                peak = jnp.maximum(score[:, :128], score[:, 128:])
+                peak = jnp.minimum(peak, jnp.where(same, 3e38, LOWEST))
+                highest = peak if highest is None else jnp.maximum(highest, peak)
+            before = top[rows, :]
+            now = jnp.maximum(before, spread(jnp.max(highest, axis=1, keepdims=True)))
+            fade = jnp.exp(before - now)
+            top[rows, :] = now
+            sums = total[rows, :] * fade
+            acc = mixed[rows, :] * fade
+            for part in range(4):
+                level = jnp.maximum(now, shut[part])
+                prob = jnp.exp(scores[part] - jnp.concatenate([level, level], axis=1))
+                sums = sums + prob[:, :128] + prob[:, 128:]
+                acc = acc + dot_nn(prob.astype(BF16), kv[slot, part * 256 : (part + 1) * 256, :])
+            total[rows, :] = sums
+            mixed[rows, :] = acc
+
+    attend(own)
+    gather.pass_z()
+    attend(gather.slot(0, gather.other))
+    gather.pass_own()
+    query_gather.begin()
+    attend(gather.slot(3, me.z))
+    attend(gather.slot(1, me.z))
+    gather.pass_other()
+    query_gather.pass_z()
+    attend(gather.slot(3, gather.other))
+    attend(gather.slot(1, gather.other))
+    output_high.wait_recv()
+    across = lax.rem(me.high + 1, 2) * 2 + me.core
+    output_pass = links.send(output_all.at[across], output_all.at[across], me.at(dcore=1))
+    gather.end_own()
+    attend(gather.slot(2, me.z))
+    gather.end_other()
+    attend(gather.slot(2, gather.other))
+
+    for block in range(4):
+        rows = slice(block * 256, (block + 1) * 256)
+        sums = spread(jnp.sum(total[rows, :], axis=1, keepdims=True))
+        out = mixed[rows, :] / sums
+        mixed[rows, :] = out
+        log_total = top[rows, :] + jnp.log(sums)
+        stats_out[block : block + 1, :] = log_total.T[0:1, :]
+        back = pltpu.roll(out[:128, :], 64, 1)
+        lane = lax.broadcasted_iota(jnp.int32, back.shape, 1)
+        head_send[block] = jnp.where(lane < HEAD_DIM, back, out[128:, :]).astype(BF16)
+    stats_out[4:, :] = jnp.zeros((4, 256), F32)
+    head_moves = []
+    for step in (1, 3, 2):
+        to = lax.rem(me.x + step, 4)
+        head_moves.append(links.send(head_send.at[to], head_recv.at[me.x], me.at(dx=step)))
+    head_recv[me.x] = head_send[me.x]
+    query_gather.pass_own()
+    for made in head_moves:
+        made.wait_recv()
+    upper = jnp.concatenate([head_recv[head].astype(F32)[:, :64] for head in range(4)], axis=1)
+    lower = jnp.concatenate([head_recv[head].astype(F32)[:, 64:] for head in range(4)], axis=1)
+    attended[attended_at] = jnp.concatenate([upper, lower], axis=0).astype(BF16)
+    here = attended.at[attended_at]
+    attended_high = links.send(here, here, me.at(dhigh=1))
+    attended_core = links.send(here, here, me.at(dcore=1))
+    query_gather.pass_other()
+    mixed_out[...] = mixed[...]
+    kv_out[...] = kv[...]
+    output_core.wait_recv()
+    output_pass.wait_recv()
+    output_out[...] = output_all[...]
+    attended_high.wait_recv()
+    attended_pass = links.send(attended.at[across], attended.at[across], me.at(dcore=1))
+    query_gather.end_own()
+    query_gather.end_other()
+    query_out[...] = query_pair[...]
+    attended_core.wait_recv()
+    attended_pass.wait_recv()
+    attended_out[...] = attended[...]
+    links.finish()
+
+
+def attention(x, gain, shift, weight, bias, output_weight, image_of):
+    vmem = pl.BlockSpec(memory_space=pltpu.VMEM)
+    return pl.pallas_call(
+        attention_kernel,
+        out_shape=[
+            jax.ShapeDtypeStruct((256, 1024), BF16),
+            jax.ShapeDtypeStruct((8, 1024, 128), BF16),
+            jax.ShapeDtypeStruct((8, 512, 128), BF16),
+            jax.ShapeDtypeStruct((1024, 128), F32),
+            jax.ShapeDtypeStruct((8, 256), F32),
+            jax.ShapeDtypeStruct((4, 256, 256), BF16),
+            jax.ShapeDtypeStruct((4, 256, 1024), BF16),
+        ],
+        in_specs=[vmem] * 6 + [pl.BlockSpec(memory_space=pltpu.SMEM)],
+        out_specs=[vmem] * 7,
+        scratch_shapes=[
+            pltpu.VMEM((8, 1024, 128), BF16),
+            pltpu.VMEM((8, 512, 128), BF16),
+            pltpu.VMEM((4, 256, 128), BF16),
+            pltpu.VMEM((4, 128, 128), BF16),
+            pltpu.VMEM((1024, 128), BF16),
+            pltpu.VMEM((1024, 128), F32),
+            pltpu.VMEM((1024, 128), F32),
+            pltpu.VMEM((1024, 128), F32),
+            pltpu.VMEM((4, 128, 128), BF16),
+            pltpu.VMEM((4, 128, 128), BF16),
+            pltpu.VMEM((4, 256, 256), BF16),
+            pltpu.VMEM((4, 256, 1024), BF16),
+            pltpu.SemaphoreType.DMA((40,)),
+            pltpu.SemaphoreType.DMA((40,)),
+        ],
+        compiler_params=pltpu.CompilerParams(
+            collective_id=0, has_side_effects=True, vmem_limit_bytes=VMEM_BYTES
+        ),
+    )(x, gain, shift, weight, bias, output_weight, image_of)
 
 
 def layer_norm(values, norm_gain, norm_shift):
@@ -140,13 +484,14 @@
     )
     attended = attended.reshape(row_count, local_width)
     attended_low = attended.astype(jnp.bfloat16)
-    head_total = lax.psum(
-        jnp.dot(attended_low, output_weight, preferred_element_type=jnp.float32).astype(
-            jnp.bfloat16
-        ),
-        "mp",
-    ).astype(jnp.float32)
-    hidden = inputs + head_total + output_bias
+    _, _, _, _, _, attended_all, output_all = attention(
+        inputs, first_gain[None], first_shift[None], attend_weight, attend_bias, output_weight, image_of
+    )
+    hidden = (
+        inputs
+        + jnp.einsum("stf,sfd->td", attended_all, output_all, preferred_element_type=jnp.float32)
+        + output_bias
+    )
     normed_two, second_back = jax.vjp(layer_norm, hidden, second_gain, second_shift)
     second_low = normed_two.astype(jnp.bfloat16)
     pre_act = jnp.dot(second_low, up_weight, preferred_element_type=jnp.float32) + up_bias

time: 1730 us -> 1700 us (0.983)
  Pallas kernels: 0 us -> 57.8 us
  waiting for transfers between devices: 1120 us -> 1090 us
  local copies, waits for them, and re-layouts: 162 us -> 137 us
    pallas_call x0 -> x1, Pallas kernels: none -> 57.8 us  [attention(): pl.pallas_call(attention_kernel, out_shape=[jax.ShapeDtypeStruct((256, 10...]
    all_gather x1, waiting for transfers between devices: 158 us -> 103 us  [per_device(): lax.all_gather(keys_low, 'dp', axis=0, tiled=True)]
    all_gather x1, waiting for transfers between devices: 79.2 us -> 128 us  [per_device(): lax.all_gather(values_low, 'dp', axis=0, tiled=True)]
    psum x1 -> x0, waiting for transfers between devices: 42.6 us -> none  [per_device(): lax.psum(jnp.dot(attended_low, output_weight, preferred_element_type=jnp....]
    unnamed x99 -> x87, local copies, waits for them, and re-layouts: 35.3 us -> 34 us
  transfers between devices with their start and end apart: 10 -> 9, of which waited for: 10 -> 9; matrix products, arithmetic and copies ran while one was open for 8% -> 6% of each run, Pallas kernels for 0% -> 0%
where the time goes in v1:
time: 1700 us; the launch traced here: 1680 us
  waiting for transfers between devices  1090 us (64%)
  blocking collectives  158 us (9%)
  local copies, waits for them, and re-layouts  137 us (8%)
  matrix products  118 us (7%)
  other arithmetic  87.3 us (5%)
  Pallas kernels  57.8 us (3%)
  loops' own time  17.2 us (1%)
    psum x1, waiting for transfers between devices, per_device(): lax.psum(attend_weight_grad.astype(jnp.bfloat16), 'dp').astype(jnp.float32)  174 us
    reduce_scatter x1, waiting for transfers between devices, per_device(): lax.psum_scatter(key_terms.astype(jnp.bfloat16), 'dp', scatter_dimension=...  168 us
    psum x1, blocking collectives, per_device(): lax.psum(first_gain_grad.astype(jnp.bfloat16), 'dp').astype(jnp.float32)  158 us
    all_gather x1, waiting for transfers between devices, per_device(): lax.all_gather(fresh[0], 'dp', axis=0, tiled=True)  157 us
    all_gather x1, waiting for transfers between devices, per_device(): lax.all_gather(fresh[1], 'dp', axis=0, tiled=True)  145 us
    reduce_scatter x1, waiting for transfers between devices, per_device(): lax.psum_scatter(value_terms.astype(jnp.bfloat16), 'dp', scatter_dimensio...  139 us
    all_gather x1, waiting for transfers between devices, per_device(): lax.all_gather(values_low, 'dp', axis=0, tiled=True)  128 us
    all_gather x1, waiting for transfers between devices, per_device(): lax.all_gather(keys_low, 'dp', axis=0, tiled=True)  103 us
  transfers between devices with their start and end apart: 9, of which 9 were waited for; matrix products, arithmetic and copies ran while one was open for 6% of the time, Pallas kernels for 0%

profile of v1, /device:TPU:0, one launch (start us, length us, event | category | flops | bytes accessed | tf_op | source)
XLA Modules:
  0.0 1680.1 jit_solution(18408249048568468675)
XLA Ops:
  8.1 57.8 %shard_map.254 = (bf16[256,1024]{1,0:T(8,128)(2,1)}, bf16[8,1024,128]{2,1,0:T(8,128)(2,1)}, bf16[8,512,128]{2,1,0:T(8,128)(2,1)}, f32[1024,128]{1,0:T(8,128)}, f...) custom-call(f32[256,1024]{1,0:T(8,128)} %x_ref.1, f32[1,1024]{1,0:T(1,128)} %bitcast.160, ...), custom_call_target="tpu_custom_call" | custom-call | tf_op jit(solution)/shard_map/pallas_call | solution.py:321
  85.4 40.2 %all-reduce.7.cloned.1.call-done = bf16[256,1024]{1,0:T(8,128)(2,1)} async-done(((bf16[256,1024]{1,0:T(8,128)(2,1)}), bf16[256,1024]{1,0:T(8,128)(2,1)}) %all-reduce.7.cloned.1.call-update) | async-done | bytes 524304 | tf_op jit(solution)/shard_map/psum | solution.py:514
  132.5 102.8 %all-gather.12.cloned.1.call-done = bf16[1,8192,256]{1,2,0:T(8,128)(2,1)} async-done(((bf16[1,256,256]{1,2,0:T(8,128)(2,1)}), bf16[1,8192,256]{1,2,0:T(8,128)(2,1)}) %all-gather.12.cloned.1.call-update) | async-done | bytes 4194320 | tf_op jit(solution)/shard_map/all_gather | solution.py:424
  235.4 6.5 copy.73
  243.9 4.3 copy.44
  248.3 10.6 copy.45
  258.9 128.4 %all-gather.10.cloned.1.call-done = bf16[8192,256]{0,1:T(8,128)(2,1)} async-done(((bf16[256,256]{0,1:T(8,128)(2,1)}), bf16[8192,256]{0,1:T(8,128)(2,1)}) %all-gather.10.cloned.1.call-update) | async-done | bytes 4194320 | tf_op jit(solution)/shard_map/all_gather | solution.py:425
  387.2 6.5 copy.75
  393.8 4.3 copy.47
  398.2 46.4 %while.42 = (s32[]{:T(128)}, f32[4,256]{1,0:T(4,128)S(1)}, f32[4,256]{1,0:T(4,128)S(1)}, s32[8,1024]{1,0:T(8,128)S(1)}, s32[]{:T(128)}, /*index=5*/bf16[8,1024,4...) while((s32[]{:T(128)}, f32[4,256]{1,0:T(4,128)S(1)}, f32[4,256]{1,0:T(4,128)S(1)}, ...), condition=%wide.region_14.15_spmd, body=%wide.region_8.14_spmd.sunk | while | flops 142611456 | bytes 9117391 | solution.py:458
  400.3 4.2 conditional.6
  406.6 4.2 conditional.6
  412.9 4.2 conditional.6
  419.3 4.2 conditional.6
  425.6 4.2 conditional.6
  434.0 4.2 conditional.6
  440.4 4.2 conditional.6
  444.6 49.9 %while.43 = (s32[]{:T(128)}, f32[256,4,64]{0,2,1:T(8,128)S(1)}, s32[8,1024]{1,0:T(8,128)S(1)}, s32[]{:T(128)}, bf16[8,1024,4,64]{3,2,1,0:T(4,128)(2,1)}, /*index...) while((s32[]{:T(128)}, f32[256,4,64]{0,2,1:T(8,128)S(1)}, ...), condition=%wide.region_19.20_spmd, body=%wide.region_15.0_spmd.sunk | while | flops 273746944 | bytes 2775747 | solution.py:480
  446.7 4.8 conditional.7
  453.5 4.8 conditional.7
  460.3 4.8 conditional.7
  467.2 4.8 conditional.7
  474.0 4.8 conditional.7
  482.9 4.8 conditional.7
  489.7 4.8 conditional.7
  497.0 157.1 %all-gather.6.cloned.1.call-done = bf16[8192,256]{0,1:T(8,128)(2,1)} async-done(((bf16[256,256]{0,1:T(8,128)(2,1)}), bf16[8192,256]{0,1:T(8,128)(2,1)}) %all-gather.6.cloned.1.call-update) | async-done | bytes 4194320 | tf_op jit(solution)/shard_map/all_gather | solution.py:531
  654.1 6.5 copy.72
  660.6 4.3 copy.48
  664.9 145.4 %all-gather.8.cloned.1.call-done = bf16[8192,256]{0,1:T(8,128)(2,1)} async-done(((bf16[256,256]{0,1:T(8,128)(2,1)}), bf16[8192,256]{0,1:T(8,128)(2,1)}) %all-gather.8.cloned.1.call-update) | async-done | bytes 4194320 | tf_op jit(solution)/shard_map/all_gather | solution.py:532
  810.2 6.5 copy.74
  816.8 4.5 copy.49
  821.3 86.6 %while.44 = (s32[]{:T(128)}, f32[256,4,64]{0,2,1:T(8,128)S(1)}, bf16[8,1024,4,64]{1,3,2,0:T(8,128)(2,1)}, bf16[8,1024,4,64]{1,3,2,0:T(8,128)(2,1)}, s32[8,1024]{...) while((s32[]{:T(128)}, f32[256,4,64]{0,2,1:T(8,128)S(1)}, ...), condition=%wide.region_24.25_spmd, body=%wide.region_20.0_spmd.sunk | while | flops 684264448 | bytes 24675584 | solution.py:573
  823.3 8.9 conditional.8
  835.2 8.9 conditional.8
  847.2 8.9 conditional.8
  859.1 8.9 conditional.8
  871.0 8.9 conditional.8
  886.1 8.9 conditional.8
  898.0 8.9 conditional.8
  907.9 12.7 copy.69
  920.6 12.7 reshape.166
  933.4 12.7 copy.68
  946.1 12.7 reshape.165
  963.8 139.1 %reduce-scatter.5.cloned.1.call-done = bf16[256,256]{1,0:T(8,128)(2,1)} async-done(((bf16[8192,256]{1,0:T(8,128)(2,1)}), bf16[256,256]{1,0:T(8,128)(2,1)}) %reduce-scatter.5.cloned.1.call-update) | async-done | bytes 131088 | tf_op jit(solution)/shard_map/reduce_scatter | solution.py:582
  1102.9 168.0 %reduce-scatter.3.cloned.1.call-done = bf16[256,256]{1,0:T(8,128)(2,1)} async-done(((bf16[8192,256]{1,0:T(8,128)(2,1)}), bf16[256,256]{1,0:T(8,128)(2,1)}) %reduce-scatter.3.cloned.1.call-update) | async-done | bytes 131088 | tf_op jit(solution)/shard_map/reduce_scatter | solution.py:579
  1285.4 30.7 %all-reduce.11.cloned.1.call-done = (bf16[256,1024]{1,0:T(8,128)(2,1)}, bf16[256,1024]{1,0:T(8,128)(2,1)}) async-done(((bf16[256,1024]{1,0:T(8,128)(2,1)}, bf16[256,1024]{1,0:T(8,128)(2,1)}), (bf16[256,1024]{1,0:T(8,128)(2,1)}, bf16[256,1024]{1,0:T(8,128)(2,1)})) %all-reduce.11.cloned.1.call-update) | async-done | bytes 1048592 | tf_op jit(solution)/shard_map/psum | solution.py:500
  1320.3 158.2 %all-reduce = (bf16[1024]{0:T(1024)(128)(2,1)S(1)}, bf16[1024]{0:T(1024)(128)(2,1)S(1)}, bf16[2,256]{1,0:T(2,128)(2,1)S(1)}, bf16[1024]{0:T(1024)(128)(2,1)S(1)}...) all-reduce(bf16[1024]{0:T(1024)(128)(2,1)S(1)} %get-tuple-element.4, ...), channel_id=1, replica_groups=mesh['dp'=32,'mp'=4] {'dp'}, use_global_device_ids=true, to_apply=%region_31.32 | all-reduce | flops 7680 | bytes 30720 | tf_op jit(solution)/shard_map/psum | solution.py:608
  1486.5 174.1 %all-reduce.9.cloned.1.call-done = (bf16[3,1024,256]{1,2,0:T(8,128)(2,1)}, bf16[256,1024]{1,0:T(8,128)(2,1)}, bf16[1024,1024]{1,0:T(8,128)(2,1)}, bf16[1024,1024]{1,0:T(8,128)(2,1)}) async-done(((bf16[3,1024,256]{1,2,0:T(8,128)(2,1)}, bf16[256,1024]{1,0:T(8,128)(2,1)}, bf16[1024,1024]{1,0:T(8,128)(2,1)}, bf16[1024,1024]{1,0:T(8,128)(2,1)}), (bf16[3,1024,256]{1,2,0:T(8,128)(2,1)}, ...) | async-done | bytes 6291472 | tf_op jit(solution)/shard_map/psum | solution.py:610
  (335 shorter events, 240.0 us)
Async XLA Ops:
  8.0 61.0 %copy-start = (bf16[1024,1024]{1,0:T(8,128)(2,1)S(1)}, bf16[1024,1024]{1,0:T(8,128)(2,1)}, u32[]{:S(2)}) copy-start(bf16[1024,1024]{1,0:T(8,128)(2,1)} %param.36) | copy-start | bytes 6291460
  8.0 117.6 %all-reduce.7.cloned.1.call-start = ((), (), s32[]{:S(2)}) async-start(), calls=%async_computation.2 | async-start | bytes 1048576 | tf_op jit(solution)/shard_map/psum | solution.py:514
  8.1 61.0 %copy-start.16 = (f32[1024]{0:T(1024)S(1)}, f32[1024]{0:T(1024)}, u32[]{:S(2)}) copy-start(f32[1024]{0:T(1024)} %param.34) | copy-start | bytes 12292
  8.1 61.0 %copy-start.30 = (f32[1024]{0:T(1024)S(1)}, f32[1024]{0:T(1024)}, u32[]{:S(2)}) copy-start(f32[1024]{0:T(1024)} %param.35) | copy-start | bytes 12292
  8.1 61.0 %copy-start.40 = (f32[1024]{0:T(1024)S(1)}, f32[1024]{0:T(1024)}, u32[]{:S(2)}) copy-start(f32[1024]{0:T(1024)} %param.37) | copy-start | bytes 12292
  68.7 4.1 copy-start.4
  69.1 58.6 %copy-start.17 = (f32[256]{0:T(256)}, f32[256]{0:T(256)S(1)}, u32[]{:S(2)}) copy-start(f32[256]{0:T(256)S(1)} %fusion.65) | copy-start | bytes 3076
  69.1 3.8 copy-start.7
  69.1 3.8 copy-start.38
  72.9 4.4 copy-start.2
  74.6 3.1 copy-start.15
  74.6 3.1 copy-start.32
  75.4 5.4 copy-start.29
  76.9 4.7 copy-start.36
  77.0 48.6 %copy-start.5 = (f32[256,1024]{1,0:T(8,128)S(1)}, f32[256,1024]{1,0:T(8,128)}, u32[]{:S(2)}) copy-start(f32[256,1024]{1,0:T(8,128)} %copy-done.4) | copy-start | bytes 3145732
  77.0 158.4 %all-gather.12.cloned.1.call-start = ((), (), s32[]{:S(2)}) async-start(), calls=%async_computation.8 | async-start | bytes 4325376 | tf_op jit(solution)/shard_map/all_gather | solution.py:424
  77.6 5.9 copy-start.24
  77.7 3.9 copy-start.19
  80.0 1.7 copy-start.11
  80.7 306.5 %all-gather.10.cloned.1.call-start = ((), (), s32[]{:S(2)}) async-start(), calls=%async_computation.5 | async-start | bytes 4325376 | tf_op jit(solution)/shard_map/all_gather | solution.py:425
  81.6 572.5 %all-gather.6.cloned.1.call-start = ((), (), s32[]{:S(2)}) async-start(), calls=%async_computation.3 | async-start | bytes 4325376 | tf_op jit(solution)/shard_map/all_gather | solution.py:531
  129.1 112.7 %copy-start.22 = (f32[256]{0:T(256)}, f32[256]{0:T(256)S(1)}, u32[]{:S(2)}) copy-start(f32[256]{0:T(256)S(1)} %negate_multiply_fusion.2) | copy-start | bytes 3076
  241.9 2.0 copy-start.3
  496.0 314.3 %all-gather.8.cloned.1.call-start = ((), (), s32[]{:S(2)}) async-start(), calls=%async_computation.4 | async-start | bytes 4325376 | tf_op jit(solution)/shard_map/all_gather | solution.py:532
  496.7 606.1 %reduce-scatter.5.cloned.1.call-start = ((), (), s32[]{:S(2)}) async-start(), calls=%async_computation.7 | async-start | bytes 4325376 | tf_op jit(solution)/shard_map/reduce_scatter | solution.py:582
  933.4 337.5 %reduce-scatter.3.cloned.1.call-start = ((), (), s32[]{:S(2)}) async-start(), calls=%async_computation.6 | async-start | bytes 4325376 | tf_op jit(solution)/shard_map/reduce_scatter | solution.py:579
  958.9 1.0 copy-start.13
  958.9 357.3 %all-reduce.11.cloned.1.call-start = ((), (), s32[]{:S(2)}) async-start(), calls=%async_computation.10 | async-start | bytes 2097152 | tf_op jit(solution)/shard_map/psum | solution.py:500
  963.0 314.6 %copy-start.6 = (f32[256,1024]{1,0:T(8,128)S(1)}, f32[256,1024]{1,0:T(8,128)}, u32[]{:S(2)}) copy-start(f32[256,1024]{1,0:T(8,128)} %copy-done.4) | copy-start | bytes 3145732
  963.0 314.6 %copy-start.18 = (f32[256]{0:T(256)S(1)}, f32[256]{0:T(256)}, u32[]{:S(2)}) copy-start(f32[256]{0:T(256)} %copy-done.17) | copy-start | bytes 3076
  963.0 314.6 %copy-start.31 = (f32[1024]{0:T(1024)S(1)}, f32[1024]{0:T(1024)}, u32[]{:S(2)}) copy-start(f32[1024]{0:T(1024)} %param.35) | copy-start | bytes 12292
  1273.8 8.2 copy-start.14
  1273.8 8.2 copy-start.20
  1273.8 8.1 copy-start.33
  1273.8 8.1 copy-start.39
  1273.8 386.8 %all-reduce.9.cloned.1.call-start = ((), (), s32[]{:S(2)}) async-start(), calls=%async_computation.9 | async-start | bytes 12582912 | tf_op jit(solution)/shard_map/psum | solution.py:610
  1283.9 1.4 copy-start.35
  1283.9 34.7 %copy-start.25 = (f32[256]{0:T(256)S(1)}, f32[256]{0:T(256)}, u32[]{:S(2)}) copy-start(f32[256]{0:T(256)} %copy-done.24) | copy-start | bytes 3076
  1283.9 34.7 %copy-start.21 = (f32[256]{0:T(256)S(1)}, f32[256]{0:T(256)}, u32[]{:S(2)}) copy-start(f32[256]{0:T(256)} %copy-done.19) | copy-start | bytes 3076
  1283.9 36.3 %copy-start.26 = (bf16[1024]{0:T(1024)(128)(2,1)S(1)}, bf16[1024]{0:T(1024)(128)(2,1)}, u32[]{:S(2)}) copy-start(bf16[1024]{0:T(1024)(128)(2,1)} %get-tuple-element.458) | copy-start | bytes 6148
  1283.9 36.3 %copy-start.27 = (bf16[1024]{0:T(1024)(128)(2,1)S(1)}, bf16[1024]{0:T(1024)(128)(2,1)}, u32[]{:S(2)}) copy-start(bf16[1024]{0:T(1024)(128)(2,1)} %get-tuple-element.528) | copy-start | bytes 6148
  1283.9 36.3 %copy-start.28 = (bf16[1024]{0:T(1024)(128)(2,1)S(1)}, bf16[1024]{0:T(1024)(128)(2,1)}, u32[]{:S(2)}) copy-start(bf16[1024]{0:T(1024)(128)(2,1)} %get-tuple-element.540) | copy-start | bytes 6148
  1283.9 36.3 %copy-start.37 = (bf16[1024]{0:T(1024)(128)(2,1)S(1)}, bf16[1024]{0:T(1024)(128)(2,1)}, u32[]{:S(2)}) copy-start(bf16[1024]{0:T(1024)(128)(2,1)} %get-tuple-element.548) | copy-start | bytes 6148
  1283.9 199.3 %copy-start.8 = (f32[256,1024]{1,0:T(8,128)S(1)}, f32[256,1024]{1,0:T(8,128)}, u32[]{:S(2)}) copy-start(f32[256,1024]{1,0:T(8,128)} %param.41) | copy-start | bytes 3145732
  1284.0 199.2 %copy-start.23 = (f32[256]{0:T(256)S(1)}, f32[256]{0:T(256)}, u32[]{:S(2)}) copy-start(f32[256]{0:T(256)} %copy-done.22) | copy-start | bytes 3076
  1284.0 199.2 %copy-start.34 = (f32[1024]{0:T(1024)S(1)}, f32[1024]{0:T(1024)}, u32[]{:S(2)}) copy-start(f32[1024]{0:T(1024)} %param.39) | copy-start | bytes 12292
  1665.8 4.2 copy-start.10
  1665.8 6.7 copy-start.1
  (2 other events, 1.8 us)
Sparse Core Ops, SparseCore 0:
  77.1 48.4 all-reduce.6
  1273.9 42.1 all-reduce.10
  1320.3 340.2 all-reduce.8
Sparse Core Ops, SparseCore 1:
  80.8 154.5 all-gather.11
  236.8 150.4 all-gather.9
  496.1 157.9 all-gather.5
  655.7 154.5 all-gather.7
  933.5 169.3 reduce-scatter.4
  1105.8 164.9 reduce-scatter.2

commit v2 on v1

--- a/solution.py
+++ b/solution.py
@@ -353,34 +353,548 @@
     )(x, gain, shift, weight, bias, output_weight, image_of)
 
 
-def layer_norm(values, norm_gain, norm_shift):
-    row_mean = jnp.mean(values, axis=-1, keepdims=True)
-    centred = values - row_mean
-    variance = jnp.mean(centred * centred, axis=-1, keepdims=True)
-    return centred * lax.rsqrt(variance + EPSILON) * norm_gain + norm_shift
-
-
-def gelu_exact(values):
-    return jax.nn.gelu(values, approximate=False)
-
-
-def block_split(pieces, row_count):
-    per_block = 1
-    while pieces % (per_block * 2) == 0 and per_block * 2 * row_count <= 1024:
-        per_block = per_block * 2
-    return pieces // per_block
-
-
-def contract_rows(left, right):
-    return lax.dot_general(
-        left, right, (((0,), (0,)), ((), ())), preferred_element_type=jnp.float32
+class ModelSum:
+    def __init__(self, me, links, part, pair, half, far, full):
+        self.me, self.links = me, links
+        self.part, self.pair, self.half, self.far, self.full = part, pair, half, far, full
+        self.own = pl.ds(pl.multiple_of(me.core * 128, 128), 128)
+        self.other = pl.ds(pl.multiple_of((1 - me.core) * 128, 128), 128)
+
+    def fill(self, rows, tile):
+        @pl.loop(0, 4)
+        def _(step):
+            cols = pl.ds(pl.multiple_of(step * 256, 256), 256)
+            self.part[rows, cols] = tile(rows, cols).astype(BF16)
+
+    def begin(self, tile):
+        self.fill(self.other, tile)
+        self.first = self.links.send(self.part.at[self.other], self.pair, self.me.at(dcore=1))
+        self.fill(self.own, tile)
+
+    def cross(self):
+        self.first.wait_recv()
+        self.half[...] = (self.part[self.own, :].astype(F32) + self.pair[...].astype(F32)).astype(BF16)
+        self.second = self.links.send(self.half, self.far, self.me.at(dhigh=1))
+
+    def back(self):
+        self.second.wait_recv()
+        self.full[self.own, :] = (self.half[...].astype(F32) + self.far[...].astype(F32)).astype(BF16)
+        self.third = self.links.send(
+            self.full.at[self.own], self.full.at[self.own], self.me.at(dcore=1)
+        )
+
+    def end(self):
+        self.third.wait_recv()
+
+
+def ring(me, axis):
+    if axis == "x":
+        return me.x, me.at(dx=1), me.at(dx=3)
+    return me.y, me.at(dy=1), me.at(dy=3)
+
+
+def add_rows(target, rows, cols, count, sources):
+    step = min(count, 64)
+
+    @pl.loop(0, count // step)
+    def _(index):
+        here = pl.ds(pl.multiple_of(index * step, step), step)
+        there = pl.ds(pl.multiple_of(rows + index * step, step), step)
+        value = target[there, cols].astype(F32)
+        for source in sources:
+            value = value + source[here, :].astype(F32)
+        target[there, cols] = value.astype(BF16)
+
+
+def weight_sum(me, links, axes, parts, whole, stages, cross, result, done_sem):
+    height, width = parts.shape
+    low, high = pl.ds(0, width // 2), pl.ds(width // 2, width // 2)
+    base, count = 0, height
+    bases = []
+    for axis, (side_up, side_down, main_up, main_down) in zip(axes, stages):
+        spot, up, down = ring(me, axis)
+        count = count // 4
+        bases.append((base, count))
+
+        def chunk(step, base=base, spot=spot, count=count):
+            return pl.multiple_of(base + lax.rem(spot + step, 4) * count, 16)
+
+        def rows(step, count=count, chunk=chunk):
+            return pl.ds(chunk(step), count)
+
+        far_up = links.send(parts.at[rows(2), low], side_up, up)
+        far_down = links.send(parts.at[rows(2), high], side_down, down)
+        near = [
+            links.send(parts.at[rows(1), high], main_up.at[:, high], up),
+            links.send(parts.at[rows(3), low], main_down.at[:, low], down),
+        ]
+        yield
+        far_up.wait_recv()
+        add_rows(parts, chunk(1), low, count, [side_up])
+        near.append(links.send(parts.at[rows(1), low], main_up.at[:, low], up))
+        far_down.wait_recv()
+        add_rows(parts, chunk(3), high, count, [side_down])
+        near.append(links.send(parts.at[rows(3), high], main_down.at[:, high], down))
+        yield
+        for made in near:
+            made.wait_recv()
+        base = chunk(0)
+        add_rows(parts, base, slice(None), count, [main_up, main_down])
+    rows = pl.ds(base, count)
+    own = pl.ds(pl.multiple_of(me.z * (width // 2), 128), width // 2)
+    other = pl.ds(pl.multiple_of((1 - me.z) * (width // 2), 128), width // 2)
+    made = links.send(parts.at[rows, other], cross, me.at(dz=1))
+    yield
+    made.wait_recv()
+    whole[rows, own] = (parts[rows, own].astype(F32) + cross[...].astype(F32)).astype(BF16)
+    made = links.send(whole.at[rows, own], whole.at[rows, own], me.at(dz=1))
+    yield
+    made.wait_recv()
+    for axis, (base, count) in zip(axes[::-1], bases[::-1]):
+        spot, up, down = ring(me, axis)
+
+        def rows(step, base=base, spot=spot, count=count):
+            return pl.ds(pl.multiple_of(base + lax.rem(spot + step, 4) * count, 16), count)
+
+        mine = whole.at[rows(0)]
+        above = links.send(mine, mine, up)
+        below = links.send(mine, mine, down)
+        yield
+        above.wait_recv()
+        piece = whole.at[rows(3), low]
+        far = [links.send(piece, piece, up)]
+        below.wait_recv()
+        piece = whole.at[rows(1), high]
+        far.append(links.send(piece, piece, down))
+        yield
+        for made in far:
+            made.wait_recv()
+    copy = pltpu.make_async_copy(whole, result, done_sem)
+    copy.start()
+    yield
+    copy.wait()
+
+
+def vector_sum(me, links, values, from_z, along_x, along_y):
+    made = links.send(values, from_z, me.at(dz=1))
+    yield
+    made.wait_recv()
+    for slots, spot, name in ((along_x, me.x, "dx"), (along_y, me.y, "dy")):
+        if name == "dx":
+            slots[spot] = values[...] + from_z[...]
+        else:
+            slots[spot] = along_x[0] + along_x[1] + along_x[2] + along_x[3]
+        here = slots.at[spot]
+        moves = [links.send(here, here, me.at(**{name: step})) for step in (1, 3, 2)]
+        yield
+        for made in moves:
+            made.wait_recv()
+
+
+def advance(jobs):
+    for job in list(jobs):
+        try:
+            next(job)
+        except StopIteration:
+            jobs.remove(job)
+
+
+def lanes_below(shape):
+    return lax.broadcasted_iota(jnp.int32, shape, 1) < HEAD_DIM
+
+
+def pack_rows(values):
+    return jnp.where(lanes_below((128, 128)), values[:128, :], pltpu.roll(values[128:, :], 64, 1))
+
+
+def backward_kernel(
+    x_ref, cot_ref, gain_one_ref, first_ref, kv_ref, query_ref, mixed_ref, stats_ref,
+    attended_ref, output_ref, output_bias_ref, gain_two_ref, shift_two_ref,
+    up_ref, up_bias_ref, down_ref, down_bias_ref, weight_ref, mates_ref, count_ref,
+    result_out, input_out, vector_out, up_out, down_out, qk_out, v_out, o_out,
+    hidden, xhat_two, inverse_two, second_low, down_grad, activated, pre_grad,
+    branch_low, sums, units, lows,
+    grad_send, grad_pair, stats_all, query_own, grad_own, levels, rows_all, query_grad_all,
+    acc_one, acc_two, qg_send, qg_recv, kvg_send, kvg_recv, stacked,
+    vector, from_z, along_x, along_y,
+    jobs_up, jobs_down, jobs_qk, jobs_v, jobs_o,
+    send_sem, recv_sem, done_sem,
+):
+    me = Place()
+    links = Links(send_sem, recv_sem)
+    wait_all = greet(all_partners(me))
+    own = me.group
+    column_tiles = 4
+
+    def cols_of(step):
+        return pl.ds(pl.multiple_of(step * 256, 256), 256)
+
+    @pl.loop(0, column_tiles)
+    def _(step):
+        cols = cols_of(step)
+        value = x_ref[:, cols] + output_bias_ref[:, cols]
+        for part in range(4):
+            value = value + dot_nn(attended_ref[part], output_ref[part, :, cols])
+        hidden[:, cols] = value
+
+    normed, inverse = row_norm(hidden[...])
+    xhat_two[...] = normed
+    inverse_two[...] = spread(inverse)
+    second_low[...] = (normed * gain_two_ref[...] + shift_two_ref[...]).astype(BF16)
+    down_grad[...] = cot_ref[...].astype(BF16)
+
+    @pl.loop(0, column_tiles)
+    def _(step):
+        cols = cols_of(step)
+        pre = dot_nn(second_low[...], up_ref[:, cols]) + up_bias_ref[:, cols]
+        back = dot_nt(down_grad[...], down_ref[cols, :])
+        spread_of = 0.5 + 0.5 * lax.erf(pre * (0.5**0.5))
+        density = jnp.exp(-0.5 * pre * pre) * 0.3989422804014327
+        activated[:, cols] = (pre * spread_of).astype(BF16)
+        low = (back * (spread_of + pre * density)).astype(BF16)
+        pre_grad[:, cols] = low
+        vector[4:5, cols] = jnp.sum(low.astype(F32), axis=0, keepdims=True)
+
+    wait_all()
+    norm_sum = ModelSum(me, links, *sums)
+    norm_sum.begin(lambda rows, cols: dot_nt(pre_grad[rows, :], up_ref[cols, :]))
+    norm_sum.cross()
+
+    up_parts, down_parts = jobs_up[0], jobs_down[0]
+
+    @pl.loop(0, column_tiles)
+    def _(step):
+        cols = cols_of(step)
+        up_parts[cols, :] = dot_tn(second_low[:, cols], pre_grad[...]).astype(BF16)
+
+    jobs = []
+    jobs.append(weight_sum(me, links, "xy", *jobs_up, up_out, done_sem.at[0]))
+
+    @pl.loop(0, column_tiles)
+    def _(step):
+        cols = cols_of(step)
+        down_parts[cols, :] = dot_tn(activated[:, cols], down_grad[...]).astype(BF16)
+
+    jobs.append(weight_sum(me, links, "yx", *jobs_down, down_out, done_sem.at[1]))
+    advance(jobs)
+    unit_sum = ModelSum(me, links, *units)
+    unit_sum.begin(lambda rows, cols: dot_nn(activated[rows, :], down_ref[:, cols]))
+    vector[3:4, :] = jnp.sum(down_grad[...].astype(F32), axis=0, keepdims=True)
+    norm_sum.back()
+    unit_sum.cross()
+    norm_sum.end()
+
+    grad = norm_sum.full[...].astype(F32)
+    xhat = xhat_two[...]
+    vector[0:1, :] = jnp.sum(grad * xhat, axis=0, keepdims=True)
+    vector[1:2, :] = jnp.sum(grad, axis=0, keepdims=True)
+    scaled = grad * gain_two_ref[...]
+    hidden_grad = cot_ref[...] + (
+        scaled
+        - jnp.mean(scaled, axis=-1, keepdims=True)
+        - xhat * jnp.mean(scaled * xhat, axis=-1, keepdims=True)
+    ) * inverse_two[:, 0:1]
+    input_out[...] = hidden_grad
+    low = hidden_grad.astype(BF16)
+    branch_low[...] = low
+    vector[2:3, :] = jnp.sum(low.astype(F32), axis=0, keepdims=True)
+
+    at = me.high * 2 + me.core
+    attended_grad = dot_nt(branch_low[...], output_ref[at]).astype(BF16).astype(F32)
+    for head in range(4):
+        part = slice(head * HEAD_DIM, (head + 1) * HEAD_DIM)
+        grad_send[head] = jnp.concatenate(
+            [attended_grad[:128, part], attended_grad[128:, part]], axis=1
+        ).astype(BF16)
+    moves = []
+    for step in (1, 3, 2):
+        head = lax.rem(me.x + step, 4)
+        moves.append(links.send(grad_send.at[head], grad_pair.at[own, me.x], me.at(dx=step)))
+    grad_pair[own, me.x] = grad_send[me.x]
+
+    o_parts = jobs_o[0]
+
+    @pl.loop(0, column_tiles)
+    def _(step):
+        cols = cols_of(step)
+        o_parts[:, cols] = dot_tn(attended_ref[at], branch_low[:, cols]).astype(BF16)
+
+    for made in moves:
+        made.wait_recv()
+    gather = Gather(me, links, grad_pair, 4)
+    gather.begin()
+    stats_all[own] = stats_ref[...]
+
+    @pl.loop(0, 4)
+    def _(block):
+        pair = query_ref[own * 4 + block].astype(F32)
+        both = jnp.concatenate([pair, pltpu.roll(pair, 64, 1)], axis=0)
+        keep = lanes_below(both.shape)
+        query_own[block] = jnp.where(keep, both, 0.0).astype(BF16)
+        pair = grad_pair[own, block].astype(F32)
+        both = jnp.concatenate([pltpu.roll(pair, 64, 1), pair], axis=0)
+        both = jnp.where(keep, 0.0, both)
+        grad_own[block] = both.astype(BF16)
+        delta = spread(jnp.sum(both * mixed_ref[block], axis=1, keepdims=True))
+        levels[block, 1] = delta
+        stats_all[own, pl.ds(block + 4, 1), :] = delta.T[0:1, :]
+        line = stats_ref[pl.ds(block, 1), :]
+        levels[block, 0] = jnp.broadcast_to(line, (128, 256)).T
+
+    stats_gather = Gather(me, links, stats_all, 8)
+    stats_gather.begin()
+
+    def wide(value):
+        return jnp.concatenate([value, value], axis=1)
+
+    def query_pass(block):
+        query, grad_out = query_own[block], grad_own[block]
+        line = block * 8 + own
+        acc_one[...] = jnp.zeros(acc_one.shape, F32)
+
+        @pl.loop(0, 4)
+        def _(step):
+            acc = acc_one[...]
+            for part in range(4):
+                index = step * 4 + part
+                shut = jnp.where(index < count_ref[line], -3e38, HIGHEST)
+                keys = kv_ref[mates_ref[line * 16 + index]]
+                level = jnp.maximum(levels[block, 0], shut)
+                prob = jnp.exp(dot_nt(query, keys) - wide(level))
+                change = prob * (dot_nt(grad_out, keys) - wide(levels[block, 1]))
+                acc = acc + dot_nn(change.astype(BF16), keys)
+            acc_one[...] = acc
+
+        qg_send[block] = pack_rows(acc_one[...] * (HEAD_DIM**-0.5)).astype(BF16)
+
+    query_moves = []
+
+    def send_query(step):
+        block = lax.rem(me.x + step, 4)
+        query_pass(block)
+        if step:
+            query_moves.append(
+                links.send(qg_send.at[block], qg_recv.at[me.x], me.at(dx=step))
+            )
+
+    send_query(2)
+    gather.pass_z()
+    stats_gather.pass_z()
+    advance(jobs)
+    send_query(1)
+    gather.pass_own()
+    stats_gather.pass_own()
+    unit_sum.back()
+    advance(jobs)
+    send_query(3)
+    gather.pass_other()
+    stats_gather.pass_other()
+    unit_sum.end()
+    result_out[...] = hidden[...] + unit_sum.full[...].astype(F32) + down_bias_ref[...]
+    advance(jobs)
+    jobs.append(weight_sum(me, links, "yx", *jobs_o, o_out, done_sem.at[4]))
+    send_query(0)
+    qg_recv[me.x] = qg_send[me.x]
+    advance(jobs)
+    gather.end_own()
+    gather.end_other()
+    stats_gather.end_own()
+    stats_gather.end_other()
+
+    @pl.loop(0, 32)
+    def _(spot):
+        slot, block = lax.div(spot, 4), lax.rem(spot, 4)
+        pair = query_ref[spot].astype(F32)
+        other = grad_pair[slot, block].astype(F32)
+        keep = lanes_below(pair.shape)
+        upper = jnp.where(keep, pair, pltpu.roll(other, 64, 1))
+        lower = jnp.where(keep, pltpu.roll(pair, 64, 1), other)
+        query_grad_all[spot] = jnp.concatenate([upper, lower], axis=0).astype(BF16)
+        rows_all[spot, 0:1, :] = stats_all[slot, pl.ds(block, 1), :]
+        rows_all[spot, 1:2, :] = stats_all[slot, pl.ds(block + 4, 1), :]
+
+    def key_pass(block):
+        both = kv_ref[own * 4 + block].astype(F32)
+        keep = lanes_below(both.shape)
+        key = jnp.where(keep, both, 0.0).astype(BF16)
+        value = jnp.where(keep, 0.0, both).astype(BF16)
+        line = block * 8 + own
+        acc_one[...] = jnp.zeros(acc_one.shape, F32)
+        acc_two[...] = jnp.zeros(acc_two.shape, F32)
+
+        @pl.loop(0, 4)
+        def _(step):
+            key_acc, value_acc = acc_one[...], acc_two[...]
+            for part in range(4):
+                index = step * 4 + part
+                shut = jnp.where(index < count_ref[line], -3e38, HIGHEST)
+                spot = mates_ref[line * 16 + index]
+                pair = query_grad_all[spot]
+                lines = rows_all[spot]
+                prob = jnp.exp(dot_nt(key, pair) - jnp.maximum(lines[0:1, :], shut))
+                change = prob * (dot_nt(value, pair) - lines[1:2, :])
+                value_acc = value_acc + dot_nn(prob.astype(BF16), pair)
+                key_acc = key_acc + dot_nn(change.astype(BF16), pair)
+            acc_one[...] = key_acc
+            acc_two[...] = value_acc
+
+        kvg_send[block] = jnp.where(keep, acc_one[...], acc_two[...]).astype(BF16)
+
+    key_moves = []
+    for step in (2, 1, 3, 0):
+        block = lax.rem(me.x + step, 4)
+        key_pass(block)
+        if step:
+            key_moves.append(links.send(kvg_send.at[block], kvg_recv.at[me.x], me.at(dx=step)))
+        advance(jobs)
+    kvg_recv[me.x] = kvg_send[me.x]
+    for made in query_moves + key_moves:
+        made.wait_recv()
+
+    heads = [qg_recv[head].astype(F32) for head in range(4)]
+    upper = jnp.concatenate([value[:, :64] for value in heads], axis=1)
+    lower = jnp.concatenate([value[:, 64:] for value in heads], axis=1)
+    stacked[:, 0:256] = jnp.concatenate([upper, lower], axis=0).astype(BF16)
+    heads = [kvg_recv[head].astype(F32) for head in range(4)]
+    stacked[:, 256:512] = jnp.concatenate([value[:, :64] for value in heads], axis=1).astype(BF16)
+    stacked[:, 512:768] = jnp.concatenate([value[:, 64:] for value in heads], axis=1).astype(BF16)
+    vector[5:6, 0:256] = jnp.sum(stacked[:, 0:256].astype(F32), axis=0, keepdims=True)
+    vector[5:6, 256:512] = jnp.sum(stacked[:, 512:768].astype(F32), axis=0, keepdims=True)
+    vector[5:6, 512:1024] = jnp.zeros((1, 512), F32)
+    low_sum = ModelSum(me, links, *lows)
+    low_sum.begin(
+        lambda rows, cols: dot_nt(stacked[rows, 0:256], weight_ref[0, cols, :])
+        + dot_nt(stacked[rows, 256:512], weight_ref[1, cols, :])
+        + dot_nt(stacked[rows, 512:768], weight_ref[2, cols, :])
     )
-
-
-def contract_cols(left, right):
-    return lax.dot_general(
-        left, right, (((1,), (1,)), ((), ())), preferred_element_type=jnp.float32
-    )
+    low_sum.cross()
+    qk_parts, v_parts = jobs_qk[0], jobs_v[0]
+
+    @pl.loop(0, column_tiles)
+    def _(step):
+        cols = cols_of(step)
+        value = dot_tn(first_ref[:, cols], stacked[...]).astype(BF16)
+        qk_parts[cols, :] = value[:, 0:512]
+        v_parts[cols, :] = value[:, 512:768]
+
+    jobs.append(weight_sum(me, links, "xy", *jobs_qk, qk_out, done_sem.at[2]))
+    jobs.append(weight_sum(me, links, "yx", *jobs_v, v_out, done_sem.at[3]))
+    advance(jobs)
+    low_sum.back()
+    advance(jobs)
+    low_sum.end()
+    grad = low_sum.full[...].astype(F32)
+    xhat, inverse = row_norm(x_ref[...])
+    vector[6:7, :] = jnp.sum(grad * xhat, axis=0, keepdims=True)
+    vector[7:8, :] = jnp.sum(grad, axis=0, keepdims=True)
+    jobs.append(vector_sum(me, links, vector, from_z, along_x, along_y))
+    advance(jobs)
+    scaled = grad * gain_one_ref[...]
+    input_out[...] = input_out[...] + (
+        scaled
+        - jnp.mean(scaled, axis=-1, keepdims=True)
+        - xhat * jnp.mean(scaled * xhat, axis=-1, keepdims=True)
+    ) * inverse
+    while jobs:
+        advance(jobs)
+    vector_out[...] = along_y[0] + along_y[1] + along_y[2] + along_y[3]
+    links.finish()
+
+
+def job_scratch(height, width):
+    shapes = []
+    stages = []
+    count = height
+    for _ in range(2):
+        count = count // 4
+        stages.append(
+            [
+                pltpu.VMEM((count, width // 2), BF16),
+                pltpu.VMEM((count, width // 2), BF16),
+                pltpu.VMEM((count, width), BF16),
+                pltpu.VMEM((count, width), BF16),
+            ]
+        )
+    return [
+        pltpu.VMEM((height, width), BF16),
+        pltpu.VMEM((height, width), BF16),
+        stages,
+        pltpu.VMEM((count, width // 2), BF16),
+    ]
+
+
+def sum_scratch():
+    return [
+        pltpu.VMEM((256, 1024), BF16),
+        pltpu.VMEM((128, 1024), BF16),
+        pltpu.VMEM((128, 1024), BF16),
+        pltpu.VMEM((128, 1024), BF16),
+        pltpu.VMEM((256, 1024), BF16),
+    ]
+
+
+def backward(*args):
+    vmem = pl.BlockSpec(memory_space=pltpu.VMEM)
+    smem = pl.BlockSpec(memory_space=pltpu.SMEM)
+    hbm = pl.BlockSpec(memory_space=pl.ANY)
+    return pl.pallas_call(
+        backward_kernel,
+        out_shape=[
+            jax.ShapeDtypeStruct((256, 1024), F32),
+            jax.ShapeDtypeStruct((256, 1024), F32),
+            jax.ShapeDtypeStruct((8, 1024), F32),
+            jax.ShapeDtypeStruct((1024, 1024), BF16),
+            jax.ShapeDtypeStruct((1024, 1024), BF16),
+            jax.ShapeDtypeStruct((1024, 512), BF16),
+            jax.ShapeDtypeStruct((1024, 256), BF16),
+            jax.ShapeDtypeStruct((256, 1024), BF16),
+        ],
+        in_specs=[vmem] * 18 + [smem] * 2,
+        out_specs=[vmem] * 3 + [hbm] * 5,
+        scratch_shapes=[
+            pltpu.VMEM((256, 1024), F32),
+            pltpu.VMEM((256, 1024), F32),
+            pltpu.VMEM((256, 128), F32),
+            pltpu.VMEM((256, 1024), BF16),
+            pltpu.VMEM((256, 1024), BF16),
+            pltpu.VMEM((256, 1024), BF16),
+            pltpu.VMEM((256, 1024), BF16),
+            pltpu.VMEM((256, 1024), BF16),
+            sum_scratch(),
+            sum_scratch(),
+            sum_scratch(),
+            pltpu.VMEM((4, 128, 128), BF16),
+            pltpu.VMEM((8, 4, 128, 128), BF16),
+            pltpu.VMEM((8, 8, 256), F32),
+            pltpu.VMEM((4, 256, 128), BF16),
+            pltpu.VMEM((4, 256, 128), BF16),
+            pltpu.VMEM((4, 2, 256, 128), F32),
+            pltpu.VMEM((32, 8, 256), F32),
+            pltpu.VMEM((32, 256, 128), BF16),
+            pltpu.VMEM((256, 128), F32),
+            pltpu.VMEM((256, 128), F32),
+            pltpu.VMEM((4, 128, 128), BF16),
+            pltpu.VMEM((4, 128, 128), BF16),
+            pltpu.VMEM((4, 256, 128), BF16),
+            pltpu.VMEM((4, 256, 128), BF16),
+            pltpu.VMEM((256, 768), BF16),
+            pltpu.VMEM((8, 1024), F32),
+            pltpu.VMEM((8, 1024), F32),
+            pltpu.VMEM((4, 8, 1024), F32),
+            pltpu.VMEM((4, 8, 1024), F32),
+            job_scratch(1024, 1024),
+            job_scratch(1024, 1024),
+            job_scratch(1024, 512),
+            job_scratch(1024, 256),
+            job_scratch(256, 1024),
+            pltpu.SemaphoreType.DMA((170,)),
+            pltpu.SemaphoreType.DMA((170,)),
+            pltpu.SemaphoreType.DMA((5,)),
+        ],
+        compiler_params=pltpu.CompilerParams(
+            collective_id=1, has_side_effects=True, vmem_limit_bytes=VMEM_BYTES
+        ),
+    )(*args)
 
 
 def per_device(
@@ -400,275 +914,39 @@
     image_of,
     cotangent,
 ):
-    row_count = inputs.shape[0]
-    local_width = attend_weight.shape[2]
-    heads_here = local_width // HEAD_DIM
-    factor = HEAD_DIM ** (-0.5)
-    device_count = lax.axis_size("dp")
-    own_image = image_of[lax.axis_index("dp")]
-    blocks = block_split(device_count, row_count)
-    key_image = jnp.repeat(image_of, row_count).reshape(blocks, -1)
-
-    def touches(image_blk):
-        return jnp.any(image_blk == own_image)
-
-    normed_one, first_back = jax.vjp(layer_norm, inputs, first_gain, first_shift)
-    first_low = normed_one.astype(jnp.bfloat16)
-    projected = jnp.einsum(
-        "td,cdf->ctf", first_low, attend_weight, preferred_element_type=jnp.float32
-    )
-    queries = (projected[0] + attend_bias[0]).astype(jnp.bfloat16)
-    keys_low = projected[1].astype(jnp.bfloat16)
-    values_low = (projected[2] + attend_bias[1]).astype(jnp.bfloat16)
-    gathered = (
-        lax.all_gather(keys_low, "dp", axis=0, tiled=True),
-        lax.all_gather(values_low, "dp", axis=0, tiled=True),
-    )
-
-    def as_blocks(gathered_rows):
-        return gathered_rows.reshape(blocks, -1, heads_here, HEAD_DIM)
-
-    key_blocks = as_blocks(gathered[0])
-    value_blocks = as_blocks(gathered[1])
-    query_heads = queries.reshape(row_count, heads_here, HEAD_DIM)
-
-    def masked_scores(keys_blk, image_blk):
-        scores = (
-            jnp.einsum("qhd,khd->hqk", query_heads, keys_blk, preferred_element_type=jnp.float32)
-            * factor
-        )
-        allowed = (image_blk == own_image)[None, None, :]
-        return (jnp.where(allowed, scores, -1e30), allowed)
-
-    def stats_step(state_pair, block_item):
-
-        def stats_work(pair):
-            running_max, running_sum = pair
-            scores, allowed = masked_scores(block_item[0], block_item[1])
-            new_max = jnp.maximum(running_max, jnp.max(scores, axis=2))
-            shifted = jnp.where(allowed, jnp.exp(scores - new_max[:, :, None]), 0.0)
-            return (
-                new_max,
-                running_sum * jnp.exp(running_max - new_max) + jnp.sum(shifted, axis=2),
-            )
-
-        return (lax.cond(touches(block_item[1]), stats_work, lambda pair: pair, state_pair), None)
-
-    start_max = jnp.full((heads_here, row_count), -1e30, jnp.float32)
-    (final_max, final_sum), unused = lax.scan(
-        stats_step, (start_max, jnp.zeros_like(start_max)), (key_blocks, key_image)
-    )
-    log_total = final_max + jnp.log(final_sum)
-
-    def block_probs(keys_blk, image_blk):
-        scores, allowed = masked_scores(keys_blk, image_blk)
-        return jnp.where(allowed, jnp.exp(scores - log_total[:, :, None]), 0.0)
-
-    def value_step(summed, block_item):
-
-        def value_work(total):
-            probs = block_probs(block_item[0], block_item[2])
-            return total + jnp.einsum(
-                "hqk,khd->qhd",
-                probs.astype(jnp.bfloat16),
-                block_item[1],
-                preferred_element_type=jnp.float32,
-            )
-
-        return (lax.cond(touches(block_item[2]), value_work, lambda total: total, summed), None)
-
-    attended, unused = lax.scan(
-        value_step,
-        jnp.zeros((row_count, heads_here, HEAD_DIM), jnp.float32),
-        (key_blocks, value_blocks, key_image),
-    )
-    attended = attended.reshape(row_count, local_width)
-    attended_low = attended.astype(jnp.bfloat16)
-    _, _, _, _, _, attended_all, output_all = attention(
+    first_low, kv, query_pair, mixed, stats, attended, output_all = attention(
         inputs, first_gain[None], first_shift[None], attend_weight, attend_bias, output_weight, image_of
     )
-    hidden = (
-        inputs
-        + jnp.einsum("stf,sfd->td", attended_all, output_all, preferred_element_type=jnp.float32)
-        + output_bias
+    same = image_of[:, None] == image_of[None, :]
+    index = jnp.arange(32)
+    rank = jnp.sum(same[:, None, :] & (index[None, :] < index[:, None])[None], axis=2)
+    place = (index % 8) * 4 + index // 8
+    chosen = same[:, None, :] & (rank[:, None, :] == jnp.arange(16)[None, :, None])
+    mates = jnp.sum(jnp.where(chosen, place[None, None, :], 0), axis=2).astype(jnp.int32)
+    count = jnp.sum(same, axis=1).astype(jnp.int32)
+    result, input_grad, vector, up, down, qk, v, o = backward(
+        inputs, cotangent, first_gain[None], first_low, kv.reshape(32, 256, 128),
+        query_pair.reshape(32, 128, 128), mixed.reshape(4, 256, 128), stats,
+        attended, output_all, output_bias[None], second_gain[None], second_shift[None],
+        up_weight, up_bias[None], down_weight, down_bias[None], attend_weight,
+        mates.reshape(512), count,
     )
-    normed_two, second_back = jax.vjp(layer_norm, hidden, second_gain, second_shift)
-    second_low = normed_two.astype(jnp.bfloat16)
-    pre_act = jnp.dot(second_low, up_weight, preferred_element_type=jnp.float32) + up_bias
-    activated, gelu_back = jax.vjp(gelu_exact, pre_act)
-    activated_low = activated.astype(jnp.bfloat16)
-    unit_total = lax.psum(
-        jnp.dot(activated_low, down_weight, preferred_element_type=jnp.float32).astype(
-            jnp.bfloat16
-        ),
-        "mp",
-    ).astype(jnp.float32)
-    result = hidden + unit_total + down_bias
-    down_grad = cotangent.astype(jnp.bfloat16)
-    down_bias_grad = jnp.sum(down_grad.astype(jnp.float32), axis=0)
-    down_weight_grad = contract_rows(activated_low, down_grad)
-    (pre_grad,) = gelu_back(contract_cols(down_grad, down_weight))
-    pre_low = pre_grad.astype(jnp.bfloat16)
-    up_bias_grad = jnp.sum(pre_low.astype(jnp.float32), axis=0)
-    up_weight_grad = contract_rows(second_low, pre_low)
-    second_norm_grad = lax.psum(
-        contract_cols(pre_low, up_weight).astype(jnp.bfloat16), "mp"
-    ).astype(jnp.float32)
-    hidden_part, second_gain_grad, second_shift_grad = second_back(second_norm_grad)
-    hidden_grad = cotangent + hidden_part
-    branch_low = hidden_grad.astype(jnp.bfloat16)
-    output_bias_grad = jnp.sum(branch_low.astype(jnp.float32), axis=0)
-    output_weight_grad = contract_rows(attended_low, branch_low)
-    attended_grad = contract_cols(branch_low, output_weight).astype(jnp.bfloat16)
-    grad_heads = attended_grad.reshape(row_count, heads_here, HEAD_DIM)
-    row_delta = jnp.einsum(
-        "qhd,qhd->hq",
-        grad_heads.astype(jnp.float32),
-        attended.reshape(row_count, heads_here, HEAD_DIM),
-    )
-    fresh = lax.optimization_barrier((keys_low, values_low, attended_grad))
-    again = (
-        lax.all_gather(fresh[0], "dp", axis=0, tiled=True),
-        lax.all_gather(fresh[1], "dp", axis=0, tiled=True),
-    )
-    back_keys = as_blocks(again[0])
-    back_values = as_blocks(again[1])
-
-    def score_grads(keys_blk, values_blk, image_blk):
-        probs = block_probs(keys_blk, image_blk)
-        prob_grad = jnp.einsum(
-            "qhd,khd->hqk", grad_heads, values_blk, preferred_element_type=jnp.float32
-        )
-        return (probs, (probs * (prob_grad - row_delta[:, :, None])).astype(jnp.bfloat16))
-
-    zero_rows = jnp.zeros((row_count, heads_here, HEAD_DIM), jnp.float32)
-
-    def grad_step(summed, block_item):
-        keys_blk, values_blk, image_blk = block_item
-        empty_part = jnp.zeros(keys_blk.shape, jnp.float32)
-
-        def grad_work(total):
-            probs, score_grad = score_grads(keys_blk, values_blk, image_blk)
-            total = total + jnp.einsum(
-                "hqk,khd->qhd", score_grad, keys_blk, preferred_element_type=jnp.float32
-            )
-            key_part = (
-                jnp.einsum(
-                    "hqk,qhd->khd", score_grad, query_heads, preferred_element_type=jnp.float32
-                )
-                * factor
-            )
-            value_part = jnp.einsum(
-                "hqk,qhd->khd",
-                probs.astype(jnp.bfloat16),
-                grad_heads,
-                preferred_element_type=jnp.float32,
-            )
-            return (total, (key_part, value_part))
-
-        return lax.cond(
-            touches(image_blk), grad_work, lambda total: (total, (empty_part, empty_part)), summed
-        )
-
-    query_sum, (key_terms, value_terms) = lax.scan(
-        grad_step, zero_rows, (back_keys, back_values, key_image)
-    )
-    key_terms = key_terms.reshape(-1, local_width)
-    value_terms = value_terms.reshape(-1, local_width)
-    key_share, value_share = (
-        lax.psum_scatter(
-            key_terms.astype(jnp.bfloat16), "dp", scatter_dimension=0, tiled=True
-        ).astype(jnp.float32),
-        lax.psum_scatter(
-            value_terms.astype(jnp.bfloat16), "dp", scatter_dimension=0, tiled=True
-        ).astype(jnp.float32),
-    )
-    query_low = (query_sum.reshape(row_count, local_width) * factor).astype(jnp.bfloat16)
-    key_low_grad = key_share.astype(jnp.bfloat16)
-    value_low_grad = value_share.astype(jnp.bfloat16)
-    stacked = jnp.stack([query_low, key_low_grad, value_low_grad])
-    attend_weight_grad = jnp.einsum(
-        "td,ctf->cdf", first_low, stacked, preferred_element_type=jnp.float32
-    )
-    attend_bias_grad = jnp.stack(
-        [
-            jnp.sum(query_low.astype(jnp.float32), axis=0),
-            jnp.sum(value_low_grad.astype(jnp.float32), axis=0),
-        ]
-    )
-    first_norm_grad = lax.psum(
-        jnp.einsum(
-            "ctf,cdf->td", stacked, attend_weight, preferred_element_type=jnp.float32
-        ).astype(jnp.bfloat16),
-        "mp",
-    ).astype(jnp.float32)
-    input_part, first_gain_grad, first_shift_grad = first_back(first_norm_grad)
-    input_grad = hidden_grad + input_part
-    summed_grads = (
-        lax.psum(first_gain_grad.astype(jnp.bfloat16), "dp").astype(jnp.float32),
-        lax.psum(first_shift_grad.astype(jnp.bfloat16), "dp").astype(jnp.float32),
-        lax.psum(attend_weight_grad.astype(jnp.bfloat16), "dp").astype(jnp.float32),
-        lax.psum(attend_bias_grad.astype(jnp.bfloat16), "dp").astype(jnp.float32),
-        lax.psum(output_weight_grad.astype(jnp.bfloat16), "dp").astype(jnp.float32),
-        lax.psum(output_bias_grad.astype(jnp.bfloat16), "dp").astype(jnp.float32),
-        lax.psum(second_gain_grad.astype(jnp.bfloat16), "dp").astype(jnp.float32),
-        lax.psum(second_shift_grad.astype(jnp.bfloat16), "dp").astype(jnp.float32),
-        lax.psum(up_weight_grad.astype(jnp.bfloat16), "dp").astype(jnp.float32),
-        lax.psum(up_bias_grad.astype(jnp.bfloat16), "dp").astype(jnp.float32),
-        lax.psum(down_weight_grad.astype(jnp.bfloat16), "dp").astype(jnp.float32),
-        lax.psum(down_bias_grad.astype(jnp.bfloat16), "dp").astype(jnp.float32),
-    )
+    weight_grad = jnp.stack([qk[:, :256], qk[:, 256:], v]).astype(F32)
     return (
-        result,
-        input_grad,
-        summed_grads[0],
-        summed_grads[1],
-        summed_grads[2],
-        summed_grads[3],
-        summed_grads[4],
-        summed_grads[5],
-        summed_grads[6],
-        summed_grads[7],
-        summed_grads[8],
-        summed_grads[9],
-        summed_grads[10],
-        summed_grads[11],
+        result, input_grad, vector[6], vector[7], weight_grad,
+        vector[5, :512].reshape(2, 256), o.astype(F32), vector[2], vector[0], vector[1],
+        up.astype(F32), vector[4], down.astype(F32), vector[3],
     )
 
 
 def solution(mesh):
     in_specs = (
-        P("dp", None),
-        P(),
-        P(),
-        P(None, None, "mp"),
-        P(None, "mp"),
-        P("mp", None),
-        P(),
-        P(),
-        P(),
-        P(None, "mp"),
-        P("mp"),
-        P("mp", None),
-        P(),
-        P(),
-        P("dp", None),
+        P("dp", None), P(), P(), P(None, None, "mp"), P(None, "mp"), P("mp", None), P(), P(), P(),
+        P(None, "mp"), P("mp"), P("mp", None), P(), P(), P("dp", None),
     )
     out_specs = (
-        P("dp", None),
-        P("dp", None),
-        P(),
-        P(),
-        P(None, None, "mp"),
-        P(None, "mp"),
-        P("mp", None),
-        P(),
-        P(),
-        P(),
-        P(None, "mp"),
-        P("mp"),
-        P("mp", None),
-        P(),
+        P("dp", None), P("dp", None), P(), P(), P(None, None, "mp"), P(None, "mp"), P("mp", None),
+        P(), P(), P(), P(None, "mp"), P("mp"), P("mp", None), P(),
     )
     return jax.shard_map(
         per_device, mesh=mesh, in_specs=in_specs, out_specs=out_specs, check_vma=False

time: 1700 us -> 215 us (0.13); the launches traced: 1680 us -> 214 us
  waiting for transfers between devices: 1090 us -> 0 us
  blocking collectives: 158 us -> 0 us
  Pallas kernels: 57.8 us -> 199 us
  local copies, waits for them, and re-layouts: 137 us -> 5.22 us
  matrix products: 118 us -> 0 us
  other arithmetic: 87.3 us -> 9.96 us
  loops' own time: 17.2 us -> 0 us
    all_gather x4 -> x0, waiting for transfers between devices: 534 us -> none  [the longest x1 157 us: per_device(): lax.all_gather(fresh[0], 'dp', axis=0, tiled=True)]
    reduce_scatter x2 -> x0, waiting for transfers between devices: 307 us -> none  [the longest x1 168 us: per_device(): lax.psum_scatter(key_terms.astype(jnp.bfloat16), 'dp', scatter_dimension=...]
    psum x3 -> x0, waiting for transfers between devices: 245 us -> none  [the longest x1 174 us: per_device(): lax.psum(attend_weight_grad.astype(jnp.bfloat16), 'dp').astype(jnp.float32)]
    psum x1 -> x0, blocking collectives: 158 us -> none  [per_device(): lax.psum(first_gain_grad.astype(jnp.bfloat16), 'dp').astype(jnp.float32)]
    pallas_call x0 -> x1, Pallas kernels: none -> 141 us  [backward(): pl.pallas_call(backward_kernel, out_shape=[jax.ShapeDtypeStruct((256, 102...]
    dot_general x61 -> x0, matrix products: 118 us -> none  [the longest x14 27.1 us: masked_scores(): jnp.einsum('qhd,khd->hqk', query_heads, keys_blk, preferred_element_type=...]
    convert_element_type x6 -> x0, local copies, waits for them, and re-layouts: 52.5 us -> none  [the longest x2 25.4 us: per_device(): key_terms.astype(jnp.bfloat16)]
    reduce_or x24 -> x0, other arithmetic: 32.4 us -> none  [touches(): return jnp.any(image_blk == own_image)]
  transfers between devices with their start and end apart: 9 -> 0, of which waited for: 9 -> 0; matrix products, arithmetic and copies ran while one was open for 6% -> 0% of each run, Pallas kernels for 0% -> 0%
where the time goes in v2:
time: 215 us; the launch traced here: 214 us
  Pallas kernels  199 us (93%)
  other arithmetic  9.96 us (5%)
  local copies, waits for them, and re-layouts  5.22 us (2%)
    pallas_call x1, Pallas kernels, backward(): pl.pallas_call(backward_kernel, out_shape=[jax.ShapeDtypeStruct((256, 102...  141 us
    pallas_call x1, Pallas kernels, attention(): pl.pallas_call(attention_kernel, out_shape=[jax.ShapeDtypeStruct((256, 10...  57.7 us

profile of v2, /device:TPU:0, one launch (start us, length us, event | category | flops | bytes accessed | tf_op | source)
XLA Modules:
  0.0 214.5 jit_solution(17092969944310023838)
XLA Ops:
  0.6 0.0 copy-start.7
  0.7 57.7 %shard_map.254 = (bf16[256,1024]{1,0:T(8,128)(2,1)}, bf16[8,1024,128]{2,1,0:T(8,128)(2,1)}, bf16[8,512,128]{2,1,0:T(8,128)(2,1)}, f32[1024,128]{1,0:T(8,128)}, f...) custom-call(f32[256,1024]{1,0:T(8,128)} %x_ref.3, f32[1,1024]{1,0:T(1,128)} %bitcast.26, ...), custom_call_target="tpu_custom_call" | custom-call | tf_op jit(solution)/shard_map/pallas_call | solution.py:321
  58.4 0.0 copy-done.7
  58.4 0.1 iota_compare_fusion.1
  58.5 0.6 convert_reduce_fusion
  59.1 0.6 select_reduce_fusion
  59.8 0.7 reshape.101.mates_ref
  60.4 0.7 convert_reduce_fusion.1.count_ref
  61.1 140.8 %shard_map.255 = (f32[256,1024]{1,0:T(8,128)}, f32[256,1024]{1,0:T(8,128)}, f32[8,1024]{1,0:T(8,128)}, bf16[1024,1024]{1,0:T(8,128)(2,1)}, bf16[1024,1024]{1,0:T...) custom-call(f32[256,1024]{1,0:T(8,128)} %x_ref.3, ...), custom_call_target="tpu_custom_call" | custom-call | tf_op jit(solution)/shard_map/pallas_call | solution.py:840
  201.9 0.0 copy-start.5
  201.9 1.3 slice_bitcast_fusion.1
  203.3 0.0 copy-done.5
  203.3 0.0 copy-start.6
  203.3 0.0 copy-start.1
  203.3 1.9 maximum_convert_fusion
  205.2 0.0 copy-done.6
  205.2 0.6 fusion.3
  205.9 0.6 reshape_squeeze.3
  206.5 0.0 copy-done.1
  206.5 0.0 copy-start
  206.5 2.5 %convert_element_type.22 = f32[1024,1024]{1,0:T(8,128)} convert(bf16[1024,1024]{1,0:T(8,128)(2,1)S(1)} %copy-done.1) | non-fusion elementwise | flops 1048576 | bytes 6291456 | tf_op jit(solution)/shard_map/convert_element_type | solution.py:938
  208.9 0.0 copy-done
  208.9 0.0 copy-start.4
  208.9 0.0 copy-start.3
  208.9 2.5 %convert_element_type.23 = f32[1024,1024]{1,0:T(8,128)} convert(bf16[1024,1024]{1,0:T(8,128)(2,1)S(1)} %copy-done) | non-fusion elementwise | flops 1048576 | bytes 6291456 | tf_op jit(solution)/shard_map/convert_element_type | solution.py:938
  211.4 0.0 copy-start.2
  211.4 0.0 copy-done.4
  211.4 1.1 convert_element_type.21
  212.5 0.0 copy-done.3
  212.5 1.0 copy.31
  213.5 0.0 copy-done.2
  213.5 1.0 copy.32
  (2 shorter events, 0.0 us)
Async XLA Ops:
  0.6 57.8 %copy-start.7 = (s32[32]{0:T(128)S(1)}, s32[32]{0:T(128)}, u32[]{:S(2)}) copy-start(s32[32]{0:T(128)} %image_ref.1) | copy-start | bytes 388
  201.9 1.4 copy-start.5
  203.3 1.9 copy-start.6
  203.3 3.2 %copy-start.1 = (bf16[1024,1024]{1,0:T(8,128)(2,1)S(1)}, bf16[1024,1024]{1,0:T(8,128)(2,1)}, u32[]{:S(2)}) copy-start(bf16[1024,1024]{1,0:T(8,128)(2,1)} %get-tuple-element.42) | copy-start | bytes 6291460
  206.5 2.5 %copy-start = (bf16[1024,1024]{1,0:T(8,128)(2,1)S(1)}, bf16[1024,1024]{1,0:T(8,128)(2,1)}, u32[]{:S(2)}) copy-start(bf16[1024,1024]{1,0:T(8,128)(2,1)} %get-tuple-element.43) | copy-start | bytes 6291460
  208.9 2.5 %copy-start.4 = (bf16[256,1024]{1,0:T(8,128)(2,1)S(1)}, bf16[256,1024]{1,0:T(8,128)(2,1)}, u32[]{:S(2)}) copy-start(bf16[256,1024]{1,0:T(8,128)(2,1)} %get-tuple-element.41) | copy-start | bytes 1572868
  208.9 3.6 %copy-start.3 = (f32[256,1024]{1,0:T(8,128)S(1)}, f32[256,1024]{1,0:T(8,128)}, u32[]{:S(2)}) copy-start(f32[256,1024]{1,0:T(8,128)} %get-tuple-element.69) | copy-start | bytes 3145732
  211.4 2.1 copy-start.2

commit v3 on v1

v3 whole, which is shorter than its diff:
```python
import functools

import jax
import jax.numpy as jnp
from jax import lax
from jax.experimental import pallas as pl
from jax.experimental.pallas import tpu as pltpu
from jax.sharding import PartitionSpec as P

HEAD_DIM = 64
EPSILON = 1e-06
LOWEST = -1e30
HIGHEST = 1e30
MESH = pl.DeviceIdType.MESH
F32 = jnp.float32
BF16 = jnp.bfloat16
VMEM_BYTES = 60 * 2**20


def dot_nn(left, right):
    return lax.dot_general(left, right, (((1,), (0,)), ((), ())), preferred_element_type=F32)


def dot_nt(left, right):
    return lax.dot_general(left, right, (((1,), (1,)), ((), ())), preferred_element_type=F32)


def dot_tn(left, right):
    return lax.dot_general(left, right, (((0,), (0,)), ((), ())), preferred_element_type=F32)


class Place:
    def __init__(self):
        data, model = lax.axis_index("dp"), lax.axis_index("mp")
        self.x = lax.div(data, 8)
        self.y = lax.rem(lax.div(data, 2), 4)
        self.z = lax.rem(data, 2)
        self.high = lax.div(model, 2)
        self.core = lax.rem(model, 2)
        self.group = self.y * 2 + self.z

    def at(self, dx=0, dy=0, dz=0, dhigh=0, dcore=0):
        x = lax.rem(self.x + dx, 4)
        y = lax.rem(self.y + dy, 4)
        z = lax.rem(self.z + dz, 2)
        high = lax.rem(self.high + dhigh, 2)
        core = lax.rem(self.core + dcore, 2)
        return (x * 8 + y * 2 + z, high * 2 + core)


class Links:
    def __init__(self, send_sem, recv_sem):
        self.send_sem, self.recv_sem = send_sem, recv_sem
        self.used = 0
        self.sent = []

    def copy(self, source, target, device):
        at = self.used
        self.used += 1
        made = pltpu.make_async_remote_copy(
            src_ref=source,
            dst_ref=target,
            send_sem=self.send_sem.at[at],
            recv_sem=self.recv_sem.at[at],
            device_id=device,
            device_id_type=MESH,
        )
        self.sent.append(made)
        return made

    def send(self, source, target, device):
        made = self.copy(source, target, device)
        made.start()
        return made

    def finish(self):
        for made in self.sent:
            made.wait_send()
        self.sent = []


def greet(partners):
    barrier = pltpu.get_barrier_semaphore()
    for device in partners:
        pl.semaphore_signal(barrier, inc=1, device_id=device, device_id_type=MESH)
    return lambda: pl.semaphore_wait(barrier, len(partners))


def all_partners(me):
    near = [me.at(dx=step) for step in (1, 2, 3)]
    near += [me.at(dx=step, dz=1) for step in (1, 2, 3)]
    near += [me.at(dy=step) for step in (1, 2, 3)]
    near += [me.at(dy=step, dz=1) for step in (1, 2, 3)]
    return near + [me.at(dz=1), me.at(dhigh=1), me.at(dcore=1)]


def row_norm(values):
    mean = jnp.mean(values, axis=-1, keepdims=True)
    centred = values - mean
    variance = jnp.mean(centred * centred, axis=-1, keepdims=True)
    inverse = lax.rsqrt(variance + EPSILON)
    return centred * inverse, inverse


def spread(column):
    return jnp.broadcast_to(column, (column.shape[0], 128))


def wide(value):
    return jnp.concatenate([value, value], axis=1)


def lanes_below(shape):
    return lax.broadcasted_iota(jnp.int32, shape, 1) < HEAD_DIM


def pack_rows(values):
    return jnp.where(lanes_below((128, 128)), values[:128, :], pltpu.roll(values[128:, :], 64, 1))


def pack_heads(values, target):
    for head in range(4):
        part = slice(head * HEAD_DIM, (head + 1) * HEAD_DIM)
        target[head] = jnp.concatenate([values[:128, part], values[128:, part]], axis=1).astype(BF16)


def unpack_heads(source):
    heads = [source[head].astype(F32) for head in range(4)]
    upper = jnp.concatenate([value[:, :HEAD_DIM] for value in heads], axis=1)
    lower = jnp.concatenate([value[:, HEAD_DIM:] for value in heads], axis=1)
    return jnp.concatenate([upper, lower], axis=0).astype(BF16)


class Gather:
    def __init__(self, me, links, blocks):
        self.me, self.links, self.blocks = me, links, blocks
        self.other = 1 - me.z

    def slot(self, dy, z):
        return lax.rem(self.me.y + dy, 4) * 2 + z

    def send(self, slot, first, count, device):
        piece = self.blocks.at[pl.ds(slot * 4 + first, count)]
        return self.links.send(piece, piece, device)

    def begin(self):
        me = self.me
        self.up, self.down, self.across = me.at(dy=1), me.at(dy=3), me.at(dz=1)
        own = me.group
        self.own_y = [self.send(own, 0, 4, self.up), self.send(own, 0, 4, self.down)]
        self.from_z = self.send(own, 0, 4, self.across)

    def pass_z(self):
        self.from_z.wait_recv()
        slot = self.slot(0, self.other)
        self.other_y = [self.send(slot, 0, 2, self.up), self.send(slot, 0, 2, self.down)]

    def pass_own(self):
        below, above = self.slot(3, self.me.z), self.slot(1, self.me.z)
        self.own_y[0].wait_recv()
        self.far_own = [self.send(below, 0, 2, self.up)]
        self.rest = [self.send(below, 2, 2, self.across)]
        self.own_y[1].wait_recv()
        self.far_own.append(self.send(above, 2, 2, self.down))
        self.rest.append(self.send(above, 2, 2, self.across))

    def pass_other(self):
        below, above = self.slot(3, self.other), self.slot(1, self.other)
        self.other_y[0].wait_recv()
        self.far_other = [self.send(below, 0, 1, self.up)]
        self.other_y[1].wait_recv()
        self.far_other.append(self.send(above, 1, 1, self.down))

    def end_near(self):
        for made in self.rest:
            made.wait_recv()

    def end_own(self):
        self.far_own[1].wait_recv()
        self.last = self.send(self.slot(2, self.me.z), 2, 2, self.across)
        self.far_own[0].wait_recv()

    def end_other(self):
        for made in self.far_other + [self.last]:
            made.wait_recv()


class ModelSum:
    def __init__(self, me, links, part, pair, half, far, full):
        self.me, self.links = me, links
        self.part, self.pair, self.half, self.far, self.full = part, pair, half, far, full
        self.own = pl.ds(pl.multiple_of(me.core * 128, 128), 128)
        self.other = pl.ds(pl.multiple_of((1 - me.core) * 128, 128), 128)

    def begin(self, tile):
        @pl.loop(0, 4)
        def _(step):
            cols = cols_of(step)
            self.part[:, cols] = tile(cols).astype(BF16)

        self.first = self.links.send(self.part.at[self.other], self.pair, self.me.at(dcore=1))

    def cross(self):
        self.first.wait_recv()
        self.half[...] = (self.part[self.own, :].astype(F32) + self.pair[...].astype(F32)).astype(BF16)
        self.second = self.links.send(self.half, self.far, self.me.at(dhigh=1))

    def back(self):
        self.second.wait_recv()
        self.full[self.own, :] = (self.half[...].astype(F32) + self.far[...].astype(F32)).astype(BF16)
        self.third = self.links.send(
            self.full.at[self.own], self.full.at[self.own], self.me.at(dcore=1)
        )

    def end(self):
        self.third.wait_recv()


def cols_of(step):
    return pl.ds(pl.multiple_of(step * 256, 256), 256)


def ring(me, axis):
    if axis == "x":
        return me.x, lambda step, dz=0: me.at(dx=step, dz=dz)
    return me.y, lambda step, dz=0: me.at(dy=step, dz=dz)


def add_rows(target, base, rows, cols, sources):
    step = min(rows.size, 64)

    @pl.loop(0, rows.size // step)
    def _(index):
        here = pl.ds(pl.multiple_of(index * step, step), step)
        there = pl.ds(pl.multiple_of(rows.start + index * step, 8), step)
        value = base[there, cols].astype(F32)
        for source in sources:
            value = value + source[here, :].astype(F32)
        target[there, cols] = value.astype(BF16)


def weight_sum(me, links, stages, parts, whole, slots, result, done_sem):
    row, rows, col, cols = 0, parts.shape[0], 0, parts.shape[1]
    pieces = []
    for index, ((kind, axis), slot) in enumerate(zip(stages, slots)):
        target = whole if index == len(stages) - 1 else parts
        across = pl.ds(col, cols)

        if kind == "pair":
            here = pl.ds(row, rows)
            cols = cols // 2
            own = pl.ds(pl.multiple_of(col + me.z * cols, 128), cols)
            other = pl.ds(pl.multiple_of(col + (1 - me.z) * cols, 128), cols)
            made = links.send(parts.at[here, other], slot, me.at(dz=1))
            pieces.append((here, own))
            yield
            made.wait_recv()
            add_rows(target, parts, here, own, [slot])
            col = own.start
            continue
        spot, to = ring(me, axis)
        if kind == "columns":
            here = pl.ds(row, rows)
            cols = cols // 8

            def strip(step, z, col=col, cols=cols, spot=spot):
                place = lax.rem(spot + step, 4) * 2 + z
                return pl.ds(pl.multiple_of(col + place * cols, 128), cols)

            pieces.append((here, strip))
            moves = []
            for step, dz in PLANE:
                piece = parts.at[here, strip(step, lax.rem(me.z + dz, 2))]
                moves.append(links.send(piece, slot.at[step * 2 + dz - 1], to(step, dz)))
            yield
            for made in moves:
                made.wait_recv()
            mine = strip(0, me.z)
            add_rows(target, parts, here, mine, [slot.at[index] for index in range(7)])
            continue
        rows = rows // (8 if kind == "plane" else 4)

        def chunk(step, z=None, row=row, rows=rows, spot=spot):
            place = lax.rem(spot + step, 4)
            place = place if z is None else place * 2 + z
            return pl.ds(pl.multiple_of(row + place * rows, 8), rows)

        pieces.append((chunk, across))
        if kind == "ring":
            low = pl.ds(col, cols // 2)
            high = pl.ds(col + cols // 2, cols // 2)
            first, second = pl.ds(0, cols // 2), pl.ds(cols // 2, cols // 2)
            side_up, side_down, main_up, main_down = slot
            far_up = links.send(parts.at[chunk(2), low], side_up, to(1))
            far_down = links.send(parts.at[chunk(2), high], side_down, to(3))
            near = [
                links.send(parts.at[chunk(1), high], main_up.at[:, second], to(1)),
                links.send(parts.at[chunk(3), low], main_down.at[:, first], to(3)),
            ]
            yield
            far_up.wait_recv()
            add_rows(parts, parts, chunk(1), low, [side_up])
            near.append(links.send(parts.at[chunk(1), low], main_up.at[:, first], to(1)))
            far_down.wait_recv()
            add_rows(parts, parts, chunk(3), high, [side_down])
            near.append(links.send(parts.at[chunk(3), high], main_down.at[:, second], to(3)))
            yield
            for made in near:
                made.wait_recv()
            add_rows(target, parts, chunk(0), across, [main_up, main_down])
            row = chunk(0).start
        elif kind == "direct":
            moves = [
                links.send(parts.at[chunk(step), across], slot.at[step - 1], to(step))
                for step in (1, 3, 2)
            ]
            yield
            for made in moves:
                made.wait_recv()
            add_rows(target, parts, chunk(0), across, [slot.at[step] for step in range(3)])
            row = chunk(0).start
        else:
            moves = []
            for step, dz in PLANE:
                piece = parts.at[chunk(step, lax.rem(me.z + dz, 2)), across]
                moves.append(links.send(piece, slot.at[step * 2 + dz - 1], to(step, dz)))
            yield
            for made in moves:
                made.wait_recv()
            mine = chunk(0, me.z)
            add_rows(target, parts, mine, across, [slot.at[index] for index in range(7)])
            row = mine.start
    for (kind, axis), (place, across) in zip(stages[::-1], pieces[::-1]):
        if kind == "pair":
            piece = whole.at[place, across]
            moves = [links.send(piece, piece, me.at(dz=1))]
            yield
        elif kind in ("plane", "columns"):
            _, to = ring(me, axis)
            piece = whole.at[place, across(0, me.z)] if kind == "columns" else whole.at[place(0, me.z), across]
            moves = [links.send(piece, piece, to(step, dz)) for step, dz in PLANE]
            yield
        elif kind == "direct":
            _, to = ring(me, axis)
            piece = whole.at[place(0), across]
            moves = [links.send(piece, piece, to(step)) for step in (1, 3, 2)]
            yield
        else:
            _, to = ring(me, axis)
            half = across.size // 2
            piece = whole.at[place(0), across]
            above = links.send(piece, piece, to(1))
            below = links.send(piece, piece, to(3))
            yield
            above.wait_recv()
            piece = whole.at[place(3), pl.ds(across.start, half)]
            moves = [links.send(piece, piece, to(1))]
            below.wait_recv()
            piece = whole.at[place(1), pl.ds(across.start + half, half)]
            moves.append(links.send(piece, piece, to(3)))
            yield
        for made in moves:
            made.wait_recv()
    copy = pltpu.make_async_copy(whole, result, done_sem)
    copy.start()
    yield
    copy.wait()


PLANE = [(1, 0), (3, 0), (0, 1), (1, 1), (3, 1), (2, 0), (2, 1)]


def vector_sum(me, links, values, plane, line, total):
    own = me.group
    plane[own] = values[...]
    here = plane.at[own]
    moves = [links.send(here, here, me.at(dy=step, dz=dz)) for step, dz in PLANE]
    yield
    for made in moves:
        made.wait_recv()
    value = plane[0]
    for slot in range(1, 8):
        value = value + plane[slot]
    line[me.x] = value
    here = line.at[me.x]
    moves = [links.send(here, here, me.at(dx=step)) for step in (1, 3, 2)]
    yield
    for made in moves:
        made.wait_recv()
    total[...] = line[0] + line[1] + line[2] + line[3]


def advance(jobs):
    for job in list(jobs):
        if next(job, "done") == "done":
            jobs.remove(job)


def list_mates(image_ref, next_of, mates, own):
    last = [jnp.int32(-1)] * 3
    for block in range(31, -1, -1):
        image = image_ref[block]
        next_of[block] = jnp.where(image == 0, last[0], jnp.where(image == 1, last[1], last[2]))
        last = [jnp.where(image == index, block, last[index]) for index in range(3)]
    for line in range(4):
        image = image_ref[line * 8 + own]
        first = jnp.where(image == 0, last[0], jnp.where(image == 1, last[1], last[2]))

        def list_one(index, block, line=line):
            known = jnp.maximum(block, 0)
            place = lax.rem(known, 8) * 4 + lax.div(known, 8)
            mates[line * 16 + index] = jnp.where(block < 0, -1, place)
            return jnp.where(block < 0, -1, next_of[known])

        lax.fori_loop(0, 16, list_one, first)


UP_STAGES = [("ring", "x"), ("direct", "y"), ("pair", None)]
DOWN_STAGES = [("ring", "y"), ("direct", "x"), ("pair", None)]
O_STAGES = [("direct", "x"), ("columns", "y")]
Q_STAGES = [("direct", "y"), ("plane", "x")]
K_STAGES = [("direct", "x"), ("plane", "y")]
V_STAGES = [("direct", "y"), ("plane", "x")]


def layer_kernel(
    x_hbm, cot_hbm, gain_one_ref, shift_one_ref, weight_hbm, attend_bias_ref, output_hbm,
    output_bias_ref, gain_two_ref, shift_two_ref, up_hbm, up_bias_ref, down_hbm, down_bias_ref,
    image_ref,
    result_out, input_out, vector_out, last_out, up_out, down_out, qkv_out, o_out,
    x_ref, cot_ref, weight_ref, up_ref, down_ref,
    first_low, kv, query_pair, kv_send, query_send, query_own, top, total, mixed,
    head_send, head_recv, attended, output_all, next_of, mates,
    hidden, xhat_two, inverse_two, second_low, down_grad, activated, pre_grad,
    branch_low, norm_parts, unit_parts, low_parts,
    grad_send, grad_pair, stats_all, grad_own, rows_all, query_grad_all,
    qg_send, qg_recv, kvg_send, kvg_recv, stacked,
    vector, plane_one, line_one, last, plane_two, line_two,
    job_up, job_down, job_q, job_k, job_v, job_o,
    send_sem, recv_sem, load_sem, done_sem,
):
    me = Place()
    links = Links(send_sem, recv_sem)
    at = me.high * 2 + me.core
    loads = []
    for source, target in (
        (x_hbm, x_ref), (weight_hbm, weight_ref), (output_hbm, output_all.at[at]), (up_hbm, up_ref),
        (down_hbm, down_ref), (cot_hbm, cot_ref),
    ):
        load = pltpu.make_async_copy(source, target, load_sem.at[len(loads)])
        load.start()
        loads.append(load)
    wait_all = greet(all_partners(me))
    own = me.group
    loads[0].wait()
    normed, _ = row_norm(x_ref[...])
    first_low[...] = (normed * gain_one_ref[...] + shift_one_ref[...]).astype(BF16)
    loads[1].wait()
    keys = dot_nn(first_low[...], weight_ref[1])
    values = dot_nn(first_low[...], weight_ref[2]) + attend_bias_ref[1:2, :]
    for head in range(4):
        part = slice(head * HEAD_DIM, (head + 1) * HEAD_DIM)
        kv_send[head] = jnp.concatenate([keys[:, part], values[:, part]], axis=1).astype(BF16)
    wait_all()
    kv_moves, query_moves = [], []
    for step in (1, 3, 2):
        head = lax.rem(me.x + step, 4)
        kv_moves.append(links.send(kv_send.at[head], kv.at[own * 4 + me.x], me.at(dx=step)))
    queries = dot_nn(first_low[...], weight_ref[0]) + attend_bias_ref[0:1, :]
    pack_heads(queries.astype(BF16).astype(F32) * (HEAD_DIM**-0.5), query_send)
    for step in (1, 3, 2):
        head = lax.rem(me.x + step, 4)
        query_moves.append(
            links.send(query_send.at[head], query_pair.at[own * 4 + me.x], me.at(dx=step))
        )
    kv[own * 4 + me.x] = kv_send[me.x]
    query_pair[own * 4 + me.x] = query_send[me.x]
    for made in kv_moves:
        made.wait_recv()
    gather = Gather(me, links, kv)
    gather.begin()
    top[...] = jnp.full(top.shape, LOWEST, F32)
    total[...] = jnp.zeros(total.shape, F32)
    mixed[...] = jnp.zeros(mixed.shape, F32)
    list_mates(image_ref, next_of, mates, own)
    for made in query_moves:
        made.wait_recv()
    for block in range(4):
        pair = query_pair[own * 4 + block].astype(F32)
        both = jnp.concatenate([pair, pltpu.roll(pair, 64, 1)], axis=0)
        query_own[block] = jnp.where(lanes_below(both.shape), both, 0.0).astype(BF16)

    def attend(slot):
        keys = [kv[slot * 4 + part] for part in range(4)]
        images = [image_ref[part * 8 + slot] for part in range(4)]
        scores = [[dot_nt(query_own[block], key) for key in keys] for block in range(4)]
        joined = jnp.concatenate(keys, axis=0)
        state = []
        for block in range(4):
            mine = image_ref[block * 8 + own]
            highest, shut = None, []
            for part in range(4):
                same = images[part] == mine
                shut.append(jnp.where(same, -3e38, HIGHEST))
                score = scores[block][part]
                peak = jnp.maximum(score[:, :128], score[:, 128:])
                peak = jnp.minimum(peak, jnp.where(same, 3e38, LOWEST))
                highest = peak if highest is None else jnp.maximum(highest, peak)
            before = top[block]
            now = jnp.maximum(before, spread(jnp.max(highest, axis=1, keepdims=True)))
            top[block] = now
            state.append((now, jnp.exp(before - now), shut))
        for block, (now, fade, shut) in enumerate(state):
            sums = total[block] * fade
            probs = []
            for part in range(4):
                level = jnp.maximum(now, shut[part])
                prob = jnp.exp(scores[block][part] - wide(level))
                sums = sums + prob[:, :128] + prob[:, 128:]
                probs.append(prob.astype(BF16))
            total[block] = sums
            mixed[block] = mixed[block] * fade + dot_nn(jnp.concatenate(probs, axis=1), joined)

    def attend_near(z):
        @pl.loop(0, 2)
        def _(side):
            attend(gather.slot(3 - 2 * side, z))

    attend(own)
    gather.pass_z()
    attend(gather.slot(0, gather.other))
    gather.pass_own()
    attend_near(me.z)
    gather.pass_other()
    gather.end_near()
    attend_near(gather.other)
    gather.end_own()
    loads[2].wait()
    quarter = pl.ds(pl.multiple_of(me.x * 64, 64), 64)
    piece = output_all.at[at, quarter]
    output_high = links.send(piece, piece, me.at(dhigh=1))
    output_core = links.send(output_all.at[at], output_all.at[at], me.at(dcore=1))
    attend(gather.slot(2, me.z))
    gather.end_other()
    across = (1 - me.high) * 2 + me.core
    output_high.wait_recv()
    piece = output_all.at[across, quarter]
    output_moves = [links.send(piece, piece, me.at(dx=step)) for step in (1, 3, 2)]
    query_gather = Gather(me, links, query_pair)
    query_gather.begin()
    attend(gather.slot(2, gather.other))
    for block in range(4):
        sums = spread(jnp.sum(total[block], axis=1, keepdims=True))
        out = mixed[block] / sums
        mixed[block] = out
        top[block] = top[block] + jnp.log(sums)
        back = pltpu.roll(out[:128, :], 64, 1)
        head_send[block] = jnp.where(lanes_below(back.shape), back, out[128:, :]).astype(BF16)
    head_moves = []
    for step in (1, 3, 2):
        to = lax.rem(me.x + step, 4)
        head_moves.append(links.send(head_send.at[to], head_recv.at[me.x], me.at(dx=step)))
    head_recv[me.x] = head_send[me.x]
    for made in output_moves:
        made.wait_recv()
    output_pass = links.send(output_all.at[across], output_all.at[across], me.at(dcore=1))
    for block in range(4):
        stats_all[own, block : block + 1, :] = top[block].T[0:1, :]
    for made in head_moves:
        made.wait_recv()
    attended[at] = unpack_heads(head_recv)
    here = attended.at[at]
    attended_high = links.send(here, here, me.at(dhigh=1))
    attended_core = links.send(here, here, me.at(dcore=1))
    query_gather.pass_z()
    query_gather.pass_own()
    output_core.wait_recv()
    output_pass.wait_recv()
    attended_high.wait_recv()
    attended_pass = links.send(attended.at[across], attended.at[across], me.at(dcore=1))
    query_gather.pass_other()
    attended_core.wait_recv()
    attended_pass.wait_recv()

    @pl.loop(0, 4)
    def _(step):
        cols = cols_of(step)
        value = x_ref[:, cols] + output_bias_ref[:, cols]
        for part in range(4):
            value = value + dot_nn(attended[part], output_all[part, :, cols])
        hidden[:, cols] = value

    normed, inverse = row_norm(hidden[...])
    xhat_two[...] = normed
    inverse_two[...] = spread(inverse)
    second_low[...] = (normed * gain_two_ref[...] + shift_two_ref[...]).astype(BF16)
    loads[5].wait()
    down_grad[...] = cot_ref[...].astype(BF16)
    loads[3].wait()
    loads[4].wait()

    @pl.loop(0, 4)
    def _(step):
        cols = cols_of(step)
        pre = dot_nn(second_low[...], up_ref[:, cols]) + up_bias_ref[:, cols]
        back = dot_nt(down_grad[...], down_ref[cols, :])
        chance = 0.5 + 0.5 * lax.erf(pre * (0.5**0.5))
        density = jnp.exp(-0.5 * pre * pre) * 0.3989422804014327
        activated[:, cols] = (pre * chance).astype(BF16)
        low = (back * (chance + pre * density)).astype(BF16)
        pre_grad[:, cols] = low
        vector[4:5, cols] = jnp.sum(low.astype(F32), axis=0, keepdims=True)

    norm_sum = ModelSum(me, links, *norm_parts)
    norm_sum.begin(lambda cols: dot_nt(pre_grad[...], up_ref[cols, :]))

    @pl.loop(0, 4)
    def _(step):
        cols = cols_of(step)
        job_down[0][cols, :] = dot_tn(activated[:, cols], down_grad[...]).astype(BF16)

    downs = [weight_sum(me, links, DOWN_STAGES, *job_down, down_out, done_sem.at[1])]
    norm_sum.cross()
    query_gather.end_near()
    query_gather.end_own()
    query_gather.end_other()
    advance(downs)

    @pl.loop(0, 4)
    def _(step):
        cols = cols_of(step)
        job_up[0][cols, :] = dot_tn(second_low[:, cols], pre_grad[...]).astype(BF16)

    ups = [weight_sum(me, links, UP_STAGES, *job_up, up_out, done_sem.at[0])]
    advance(ups)
    unit_sum = ModelSum(me, links, *unit_parts)
    unit_sum.begin(lambda cols: dot_nn(activated[...], down_ref[:, cols]))
    vector[3:4, :] = jnp.sum(down_grad[...].astype(F32), axis=0, keepdims=True)
    advance(downs)
    norm_sum.back()
    norm_sum.end()
    grad = norm_sum.full[...].astype(F32)
    xhat = xhat_two[...]
    vector[0:1, :] = jnp.sum(grad * xhat, axis=0, keepdims=True)
    vector[1:2, :] = jnp.sum(grad, axis=0, keepdims=True)
    scaled = grad * gain_two_ref[...]
    hidden_grad = cot_ref[...] + (
        scaled
        - jnp.mean(scaled, axis=-1, keepdims=True)
        - xhat * jnp.mean(scaled * xhat, axis=-1, keepdims=True)
    ) * inverse_two[:, 0:1]
    cot_ref[...] = hidden_grad
    low = hidden_grad.astype(BF16)
    branch_low[...] = low
    vector[2:3, :] = jnp.sum(low.astype(F32), axis=0, keepdims=True)
    pack_heads(dot_nt(branch_low[...], output_all[at]).astype(BF16).astype(F32), grad_send)
    moves = []
    for step in (1, 3, 2):
        head = lax.rem(me.x + step, 4)
        moves.append(links.send(grad_send.at[head], grad_pair.at[own * 4 + me.x], me.at(dx=step)))
    grad_pair[own * 4 + me.x] = grad_send[me.x]
    advance(ups)

    @pl.loop(0, 4)
    def _(step):
        cols = cols_of(step)
        job_o[0][:, cols] = dot_tn(attended[at], branch_low[:, cols]).astype(BF16)

    for made in moves:
        made.wait_recv()
    gather = Gather(me, links, grad_pair)
    gather.begin()

    @pl.loop(0, 4)
    def _(block):
        pair = grad_pair[own * 4 + block].astype(F32)
        both = jnp.concatenate([pltpu.roll(pair, 64, 1), pair], axis=0)
        both = jnp.where(lanes_below(both.shape), 0.0, both)
        grad_own[block] = both.astype(BF16)
        delta = spread(jnp.sum(both * mixed[block], axis=1, keepdims=True))
        total[block] = delta
        stats_all[own, pl.ds(block + 4, 1), :] = delta.T[0:1, :]

    here = stats_all.at[own]
    stats_moves = [links.send(here, here, me.at(dy=step, dz=dz)) for step, dz in PLANE]

    def query_pass(block):
        query, grad_out = query_own[block], grad_own[block]
        level, delta = top[block], wide(total[block])

        def some(step, acc):
            keys, changes = [], []
            for part in range(8):
                place = mates[block * 16 + step * 8 + part]
                key = kv[jnp.maximum(place, 0)]
                shut = jnp.where(place < 0, HIGHEST, -3e38)
                prob = jnp.exp(dot_nt(query, key) - wide(jnp.maximum(level, shut)))
                changes.append((prob * (dot_nt(grad_out, key) - delta)).astype(BF16))
                keys.append(key)
            return acc + dot_nn(jnp.concatenate(changes, axis=1), jnp.concatenate(keys, axis=0))

        acc = lax.fori_loop(0, 2, some, jnp.zeros((256, 128), F32))
        qg_send[block] = pack_rows(acc * (HEAD_DIM**-0.5)).astype(BF16)

    query_moves = []

    def send_query(step):
        block = lax.rem(me.x + step, 4)
        query_pass(block)
        if step:
            query_moves.append(links.send(qg_send.at[block], qg_recv.at[me.x], me.at(dx=step)))
        else:
            qg_recv[me.x] = qg_send[me.x]

    def pair_up(slot):
        @pl.loop(0, 4)
        def _(block):
            spot = slot * 4 + block
            pair = query_pair[spot].astype(F32)
            other = grad_pair[spot].astype(F32)
            keep = lanes_below(pair.shape)
            upper = jnp.where(keep, pair, pltpu.roll(other, 64, 1))
            lower = jnp.where(keep, pltpu.roll(pair, 64, 1), other)
            query_grad_all[spot] = jnp.concatenate([upper, lower], axis=0).astype(BF16)
            rows_all[spot, 0:1, :] = stats_all[slot, pl.ds(block, 1), :]
            rows_all[spot, 1:2, :] = stats_all[slot, pl.ds(block + 4, 1), :]

    send_query(2)
    gather.pass_z()
    advance(downs)
    send_query(1)
    gather.pass_own()
    outs = [weight_sum(me, links, O_STAGES, *job_o, o_out, done_sem.at[5])]
    advance(outs)
    advance(ups)
    for made in stats_moves:
        made.wait_recv()
    pair_up(own)
    pair_up(gather.slot(0, gather.other))
    send_query(3)
    gather.pass_other()
    pair_up(gather.slot(1, me.z))
    pair_up(gather.slot(3, me.z))
    send_query(0)
    gather.end_own()
    advance(downs)
    gather.end_near()
    pair_up(gather.slot(2, me.z))
    pair_up(gather.slot(1, gather.other))
    pair_up(gather.slot(3, gather.other))
    gather.end_other()
    pair_up(gather.slot(2, gather.other))
    advance(ups)
    advance(downs)
    advance(outs)

    def key_pass(block):
        both = kv[own * 4 + block].astype(F32)
        keep = lanes_below(both.shape)
        key = jnp.where(keep, both, 0.0).astype(BF16)
        value = jnp.where(keep, 0.0, both).astype(BF16)

        def some(step, accs):
            pairs, probs, changes = [], [], []
            for part in range(8):
                place = mates[block * 16 + step * 8 + part]
                spot = jnp.maximum(place, 0)
                shut = jnp.where(place < 0, HIGHEST, -3e38)
                pair, lines = query_grad_all[spot], rows_all[spot]
                prob = jnp.exp(dot_nt(key, pair) - jnp.maximum(lines[0:1, :], shut))
                probs.append(prob.astype(BF16))
                changes.append((prob * (dot_nt(value, pair) - lines[1:2, :])).astype(BF16))
                pairs.append(pair)
            joined = jnp.concatenate(pairs, axis=0)
            return (
                accs[0] + dot_nn(jnp.concatenate(changes, axis=1), joined),
                accs[1] + dot_nn(jnp.concatenate(probs, axis=1), joined),
            )

        zero = jnp.zeros((256, 128), F32)
        of_key, of_value = lax.fori_loop(0, 2, some, (zero, zero))
        kvg_send[block] = jnp.where(keep, of_key, of_value).astype(BF16)

    key_moves = []

    def send_key(step):
        block = lax.rem(me.x + step, 4)
        key_pass(block)
        if step:
            key_moves.append(links.send(kvg_send.at[block], kvg_recv.at[me.x], me.at(dx=step)))
        else:
            kvg_recv[me.x] = kvg_send[me.x]

    send_key(2)
    advance(ups)
    for made in query_moves:
        made.wait_recv()
    stacked[:, 0:256] = unpack_heads(qg_recv)
    job_q[0][...] = dot_tn(first_low[...], stacked[:, 0:256]).astype(BF16)
    jobs = [weight_sum(me, links, Q_STAGES, *job_q, qkv_out.at[0], done_sem.at[2])]
    advance(jobs)
    advance(outs)
    send_key(1)
    advance(downs)
    send_key(3)
    advance(ups)
    send_key(0)
    advance(jobs)
    advance(outs)
    for made in key_moves:
        made.wait_recv()

    heads = [kvg_recv[head].astype(F32) for head in range(4)]
    stacked[:, 256:512] = jnp.concatenate([value[:, :64] for value in heads], axis=1).astype(BF16)
    stacked[:, 512:768] = jnp.concatenate([value[:, 64:] for value in heads], axis=1).astype(BF16)
    low_sum = ModelSum(me, links, *low_parts)
    low_sum.begin(
        lambda cols: dot_nt(stacked[:, 0:256], weight_ref[0, cols, :])
        + dot_nt(stacked[:, 256:512], weight_ref[1, cols, :])
        + dot_nt(stacked[:, 512:768], weight_ref[2, cols, :])
    )
    job_k[0][...] = dot_tn(first_low[...], stacked[:, 256:512]).astype(BF16)
    job_v[0][...] = dot_tn(first_low[...], stacked[:, 512:768]).astype(BF16)
    pairs = [
        weight_sum(me, links, K_STAGES, *job_k, qkv_out.at[1], done_sem.at[3]),
        weight_sum(me, links, V_STAGES, *job_v, qkv_out.at[2], done_sem.at[4]),
    ]
    advance(pairs)
    low_sum.cross()
    unit_sum.cross()
    vector[5:6, 0:256] = jnp.sum(stacked[:, 0:256].astype(F32), axis=0, keepdims=True)
    vector[5:6, 256:512] = jnp.sum(stacked[:, 512:768].astype(F32), axis=0, keepdims=True)
    vector[5:6, 512:1024] = jnp.zeros((1, 512), F32)
    vector[6:8, :] = jnp.zeros((2, 1024), F32)
    vectors = [vector_sum(me, links, vector, plane_one, line_one, vector_out)]
    advance(vectors)
    advance(jobs)
    advance(downs)
    advance(ups)
    xhat, inverse = row_norm(x_ref[...])
    low_sum.back()
    advance(pairs)
    low_sum.end()
    grad = low_sum.full[...].astype(F32)
    gain_grad = jnp.sum(grad * xhat, axis=0, keepdims=True)
    shift_grad = jnp.sum(grad, axis=0, keepdims=True)
    for part in range(4):
        cols = slice(part * 256, (part + 1) * 256)
        last[part : part + 1, :] = gain_grad[:, cols]
        last[part + 4 : part + 5, :] = shift_grad[:, cols]
    vectors.append(vector_sum(me, links, last, plane_two, line_two, last_out))
    advance(vectors)
    scaled = grad * gain_one_ref[...]
    cot_ref[...] = cot_ref[...] + (
        scaled
        - jnp.mean(scaled, axis=-1, keepdims=True)
        - xhat * jnp.mean(scaled * xhat, axis=-1, keepdims=True)
    ) * inverse
    input_done = pltpu.make_async_copy(cot_ref, input_out, done_sem.at[6])
    input_done.start()
    unit_sum.back()
    unit_sum.end()
    hidden[...] = hidden[...] + unit_sum.full[...].astype(F32) + down_bias_ref[...]
    result_done = pltpu.make_async_copy(hidden, result_out, done_sem.at[7])
    result_done.start()
    jobs = pairs + vectors + jobs + ups + downs + outs
    while jobs:
        advance(jobs)
    input_done.wait()
    result_done.wait()
    links.finish()


def job_scratch(height, width, stages):
    slots = []
    rows, cols = height, width
    for kind, _ in stages:
        if kind == "ring":
            rows = rows // 4
            side, main = pltpu.VMEM((rows, cols // 2), BF16), pltpu.VMEM((rows, cols), BF16)
            slots.append([side, side, main, main])
        elif kind == "direct":
            rows = rows // 4
            slots.append(pltpu.VMEM((3, rows, cols), BF16))
        elif kind == "plane":
            rows = rows // 8
            slots.append(pltpu.VMEM((7, rows, cols), BF16))
        elif kind == "columns":
            cols = cols // 8
            slots.append(pltpu.VMEM((7, rows, cols), BF16))
        else:
            cols = cols // 2
            slots.append(pltpu.VMEM((rows, cols), BF16))
    return [pltpu.VMEM((height, width), BF16), pltpu.VMEM((height, width), BF16), slots]


def sum_scratch():
    half = pltpu.VMEM((128, 1024), BF16)
    whole = pltpu.VMEM((256, 1024), BF16)
    return [whole, half, half, half, whole]


def layer(*args):
    vmem = pl.BlockSpec(memory_space=pltpu.VMEM)
    smem = pl.BlockSpec(memory_space=pltpu.SMEM)
    hbm = pl.BlockSpec(memory_space=pl.ANY)
    low_rows = pltpu.VMEM((256, 1024), BF16)
    wide_rows = pltpu.VMEM((256, 1024), F32)
    return pl.pallas_call(
        layer_kernel,
        out_shape=[
            jax.ShapeDtypeStruct((256, 1024), F32),
            jax.ShapeDtypeStruct((256, 1024), F32),
            jax.ShapeDtypeStruct((8, 1024), F32),
            jax.ShapeDtypeStruct((8, 256), F32),
            jax.ShapeDtypeStruct((1024, 1024), BF16),
            jax.ShapeDtypeStruct((1024, 1024), BF16),
            jax.ShapeDtypeStruct((3, 1024, 256), BF16),
            jax.ShapeDtypeStruct((256, 1024), BF16),
        ],
        in_specs=[hbm, hbm, vmem, vmem, hbm, vmem, hbm, vmem, vmem, vmem, hbm, vmem, hbm, vmem, smem],
        out_specs=[hbm] * 2 + [vmem] * 2 + [hbm] * 4,
        scratch_shapes=[
            wide_rows, wide_rows,
            pltpu.VMEM((3, 1024, 256), BF16),
            pltpu.VMEM((1024, 1024), BF16), pltpu.VMEM((1024, 1024), BF16),
            low_rows,
            pltpu.VMEM((32, 256, 128), BF16),
            pltpu.VMEM((32, 128, 128), BF16),
            pltpu.VMEM((4, 256, 128), BF16),
            pltpu.VMEM((4, 128, 128), BF16),
            pltpu.VMEM((4, 256, 128), BF16),
            pltpu.VMEM((4, 256, 128), F32),
            pltpu.VMEM((4, 256, 128), F32),
            pltpu.VMEM((4, 256, 128), F32),
            pltpu.VMEM((4, 128, 128), BF16),
            pltpu.VMEM((4, 128, 128), BF16),
            pltpu.VMEM((4, 256, 256), BF16),
            pltpu.VMEM((4, 256, 1024), BF16),
            pltpu.SMEM((32,), jnp.int32),
            pltpu.SMEM((64,), jnp.int32),
            wide_rows, wide_rows, pltpu.VMEM((256, 128), F32),
            low_rows, low_rows, low_rows, low_rows, low_rows,
            sum_scratch(), sum_scratch(), sum_scratch(),
            pltpu.VMEM((4, 128, 128), BF16),
            pltpu.VMEM((32, 128, 128), BF16),
            pltpu.VMEM((8, 8, 256), F32),
            pltpu.VMEM((4, 256, 128), BF16),
            pltpu.VMEM((32, 8, 256), F32),
            pltpu.VMEM((32, 256, 128), BF16),
            pltpu.VMEM((4, 128, 128), BF16),
            pltpu.VMEM((4, 128, 128), BF16),
            pltpu.VMEM((4, 256, 128), BF16),
            pltpu.VMEM((4, 256, 128), BF16),
            pltpu.VMEM((256, 768), BF16),
            pltpu.VMEM((8, 1024), F32), pltpu.VMEM((8, 8, 1024), F32), pltpu.VMEM((4, 8, 1024), F32),
            pltpu.VMEM((8, 256), F32), pltpu.VMEM((8, 8, 256), F32), pltpu.VMEM((4, 8, 256), F32),
            job_scratch(1024, 1024, UP_STAGES),
            job_scratch(1024, 1024, DOWN_STAGES),
            job_scratch(1024, 256, Q_STAGES),
            job_scratch(1024, 256, K_STAGES),
            job_scratch(1024, 256, V_STAGES),
            job_scratch(256, 1024, O_STAGES),
            pltpu.SemaphoreType.DMA((240,)),
            pltpu.SemaphoreType.DMA((240,)),
            pltpu.SemaphoreType.DMA((6,)),
            pltpu.SemaphoreType.DMA((8,)),
        ],
        compiler_params=pltpu.CompilerParams(
            collective_id=0, has_side_effects=True, vmem_limit_bytes=VMEM_BYTES
        ),
    )(*args)


def widen_kernel(
    up, down, qkv, o, result, input_grad, vector, last,
    up_out, down_out, qkv_out, o_out, result_out, input_out,
    first_gain, first_shift, bias, output_bias, second_gain, second_shift, up_bias, down_bias,
):
    up_out[...] = up[...].astype(F32)
    down_out[...] = down[...].astype(F32)
    qkv_out[...] = qkv[...].astype(F32)
    o_out[...] = o[...].astype(F32)
    result_out[...] = result[...]
    input_out[...] = input_grad[...]

    @pl.when(pl.program_id(0) == 0)
    def _():
        first_gain[...] = jnp.concatenate([last[row : row + 1, :] for row in range(4)], axis=1)
        first_shift[...] = jnp.concatenate([last[row : row + 1, :] for row in range(4, 8)], axis=1)
        bias[0:1, :] = vector[5:6, 0:256]
        bias[1:2, :] = vector[5:6, 256:512]
        for target, row in (
            (second_gain, 0), (second_shift, 1), (output_bias, 2), (down_bias, 3), (up_bias, 4),
        ):
            target[...] = vector[row : row + 1, :]


def widen(up, down, qkv, o, result, input_grad, vector, last):
    steps = 8
    tall = pl.BlockSpec((1024 // steps, 1024), lambda step: (step, 0))
    short = pl.BlockSpec((256 // steps, 1024), lambda step: (step, 0))
    three = pl.BlockSpec((3, 1024 // steps, 256), lambda step: (0, step, 0))
    line = pl.BlockSpec((1, 1024), lambda step: (0, 0))

    def whole(shape):
        return pl.BlockSpec(shape, lambda step: (0, 0))

    row = jax.ShapeDtypeStruct((1, 1024), F32)
    return pl.pallas_call(
        widen_kernel,
        grid=(steps,),
        out_shape=[
            jax.ShapeDtypeStruct((1024, 1024), F32),
            jax.ShapeDtypeStruct((1024, 1024), F32),
            jax.ShapeDtypeStruct((3, 1024, 256), F32),
            jax.ShapeDtypeStruct((256, 1024), F32),
            jax.ShapeDtypeStruct((256, 1024), F32),
            jax.ShapeDtypeStruct((256, 1024), F32),
            row, row, jax.ShapeDtypeStruct((2, 256), F32), row, row, row, row, row,
        ],
        in_specs=[tall, tall, three, short, short, short, whole((8, 1024)), whole((8, 256))],
        out_specs=[
            tall, tall, three, short, short, short,
            line, line, whole((2, 256)), line, line, line, line, line,
        ],
        compiler_params=pltpu.CompilerParams(vmem_limit_bytes=VMEM_BYTES),
    )(up, down, qkv, o, result, input_grad, vector, last)


def per_device(
    inputs,
    first_gain,
    first_shift,
    attend_weight,
    attend_bias,
    output_weight,
    output_bias,
    second_gain,
    second_shift,
    up_weight,
    up_bias,
    down_weight,
    down_bias,
    image_of,
    cotangent,
):
    result, input_grad, vector, last, up, down, qkv, o = layer(
        inputs, cotangent, first_gain[None], first_shift[None], attend_weight, attend_bias,
        output_weight, output_bias[None], second_gain[None], second_shift[None],
        up_weight, up_bias[None], down_weight, down_bias[None], image_of,
    )
    (
        up, down, qkv, o, result, input_grad, first_gain_grad, first_shift_grad, bias_grad,
        output_bias_grad, second_gain_grad, second_shift_grad, up_bias_grad, down_bias_grad,
    ) = widen(up, down, qkv, o, result, input_grad, vector, last)
    return (
        result, input_grad, first_gain_grad[0], first_shift_grad[0], qkv, bias_grad, o,
        output_bias_grad[0], second_gain_grad[0], second_shift_grad[0], up, up_bias_grad[0], down,
        down_bias_grad[0],
    )


def solution(mesh):
    in_specs = (
        P("dp", None), P(), P(), P(None, None, "mp"), P(None, "mp"), P("mp", None), P(), P(), P(),
        P(None, "mp"), P("mp"), P("mp", None), P(), P(), P("dp", None),
    )
    out_specs = (
        P("dp", None), P("dp", None), P(), P(), P(None, None, "mp"), P(None, "mp"), P("mp", None),
        P(), P(), P(), P(None, "mp"), P("mp"), P("mp", None), P(),
    )
    return jax.shard_map(
        per_device, mesh=mesh, in_specs=in_specs, out_specs=out_specs, check_vma=False
    )
```

time: 1700 us -> 180 us (0.11); the launches traced: 1680 us -> 179 us
  waiting for transfers between devices: 1090 us -> 0 us
  blocking collectives: 158 us -> 0 us
  local copies, waits for them, and re-layouts: 137 us -> 0 us
  Pallas kernels: 57.8 us -> 178 us
  matrix products: 118 us -> 0 us
  other arithmetic: 87.3 us -> 0 us
  loops' own time: 17.2 us -> 0 us
    all_gather x4 -> x0, waiting for transfers between devices: 534 us -> none  [the longest x1 157 us: per_device(): lax.all_gather(fresh[0], 'dp', axis=0, tiled=True)]
    reduce_scatter x2 -> x0, waiting for transfers between devices: 307 us -> none  [the longest x1 168 us: per_device(): lax.psum_scatter(key_terms.astype(jnp.bfloat16), 'dp', scatter_dimension=...]
    psum x3 -> x0, waiting for transfers between devices: 245 us -> none  [the longest x1 174 us: per_device(): lax.psum(attend_weight_grad.astype(jnp.bfloat16), 'dp').astype(jnp.float32)]
    psum x1 -> x0, blocking collectives: 158 us -> none  [per_device(): lax.psum(first_gain_grad.astype(jnp.bfloat16), 'dp').astype(jnp.float32)]
    pallas_call x1 -> x2, Pallas kernels: 57.8 us -> 178 us  [the longest x1 168 us: layer(): pl.pallas_call(layer_kernel, out_shape=[jax.ShapeDtypeStruct((256, 1024),...]
    dot_general x61 -> x0, matrix products: 118 us -> none  [the longest x14 27.1 us: masked_scores(): jnp.einsum('qhd,khd->hqk', query_heads, keys_blk, preferred_element_type=...]
    convert_element_type x6 -> x0, local copies, waits for them, and re-layouts: 52.5 us -> none  [the longest x2 25.4 us: per_device(): key_terms.astype(jnp.bfloat16)]
    unnamed x87 -> x0, local copies, waits for them, and re-layouts: 34 us -> none
  transfers between devices with their start and end apart: 9 -> 0, of which waited for: 9 -> 0; matrix products, arithmetic and copies ran while one was open for 6% -> 0% of each run, Pallas kernels for 0% -> 0%
where the time goes in v3:
time: 180 us; the launch traced here: 179 us
  Pallas kernels  178 us (99%)
    pallas_call x1, Pallas kernels, layer(): pl.pallas_call(layer_kernel, out_shape=[jax.ShapeDtypeStruct((256, 1024),...  168 us
    pallas_call x1, Pallas kernels, widen(): pl.pallas_call(widen_kernel, grid=(steps,), out_shape=[jax.ShapeDtypeStru...  10 us

profile of v3, /device:TPU:0, one launch (start us, length us, event | category | flops | bytes accessed | tf_op | source)
XLA Modules:
  0.0 178.6 jit_solution(13692635265732667547)
XLA Ops:
  0.7 167.7 %shard_map.254 = (f32[256,1024]{1,0:T(8,128)}, f32[256,1024]{1,0:T(8,128)}, f32[8,1024]{1,0:T(8,128)}, f32[8,256]{1,0:T(8,128)}, bf16[1024,1024]{1,0:T(8,128)(2,...) custom-call(f32[256,1024]{1,0:T(8,128)} %x_hbm.1, f32[256,1024]{1,0:T(8,128)} %cot_hbm.1, ...), custom_call_target="tpu_custom_call" | custom-call | tf_op jit(solution)/shard_map/pallas_call | solution.py:909
  168.3 10.0 %shard_map.255 = (f32[1024,1024]{1,0:T(8,128)}, f32[1024,1024]{1,0:T(8,128)}, f32[3,1024,256]{2,1,0:T(8,128)}, f32[256,1024]{1,0:T(8,128)}, f32[256,1024]{1,0:T(...) custom-call(bf16[1024,1024]{1,0:T(8,128)(2,1)} %get-tuple-element.36, ...), custom_call_target="tpu_custom_call" | custom-call | tf_op jit(solution)/shard_map/pallas_call | solution.py:1010

commit v4 on v3

--- a/solution.py
+++ b/solution.py
@@ -91,6 +91,7 @@
     near += [me.at(dx=step, dz=1) for step in (1, 2, 3)]
     near += [me.at(dy=step) for step in (1, 2, 3)]
     near += [me.at(dy=step, dz=1) for step in (1, 2, 3)]
+    near += [me.at(dx=step, dhigh=1) for step in (1, 2, 3)]
     return near + [me.at(dz=1), me.at(dhigh=1), me.at(dcore=1)]
 
 
@@ -192,28 +193,46 @@
         self.own = pl.ds(pl.multiple_of(me.core * 128, 128), 128)
         self.other = pl.ds(pl.multiple_of((1 - me.core) * 128, 128), 128)
 
+    def cols(self, side):
+        return pl.ds(side * 512, 512)
+
     def begin(self, tile):
-        @pl.loop(0, 4)
-        def _(step):
-            cols = cols_of(step)
-            self.part[:, cols] = tile(cols).astype(BF16)
-
-        self.first = self.links.send(self.part.at[self.other], self.pair, self.me.at(dcore=1))
-
-    def cross(self):
-        self.first.wait_recv()
-        self.half[...] = (self.part[self.own, :].astype(F32) + self.pair[...].astype(F32)).astype(BF16)
-        self.second = self.links.send(self.half, self.far, self.me.at(dhigh=1))
+        self.first, self.second, self.third = [], [], []
+        for side in range(2):
+
+            @pl.loop(2 * side, 2 * side + 2)
+            def _(step):
+                cols = cols_of(step)
+                self.part[:, cols] = tile(cols).astype(BF16)
+
+            cols = self.cols(side)
+            self.first.append(
+                self.links.send(
+                    self.part.at[self.other, cols], self.pair.at[:, cols], self.me.at(dcore=1)
+                )
+            )
+
+    def cross(self, side):
+        cols = self.cols(side)
+        self.first[side].wait_recv()
+        value = self.part[self.own, cols].astype(F32) + self.pair[:, cols].astype(F32)
+        self.half[:, cols] = value.astype(BF16)
+        self.second.append(
+            self.links.send(self.half.at[:, cols], self.far.at[:, cols], self.me.at(dhigh=1))
+        )
 
     def back(self):
-        self.second.wait_recv()
-        self.full[self.own, :] = (self.half[...].astype(F32) + self.far[...].astype(F32)).astype(BF16)
-        self.third = self.links.send(
-            self.full.at[self.own], self.full.at[self.own], self.me.at(dcore=1)
-        )
+        for side in range(2):
+            cols = self.cols(side)
+            self.second[side].wait_recv()
+            value = self.half[:, cols].astype(F32) + self.far[:, cols].astype(F32)
+            self.full[self.own, cols] = value.astype(BF16)
+            piece = self.full.at[self.own, cols]
+            self.third.append(self.links.send(piece, piece, self.me.at(dcore=1)))
 
     def end(self):
-        self.third.wait_recv()
+        for made in self.third:
+            made.wait_recv()
 
 
 def cols_of(step):
@@ -226,7 +245,7 @@
     return me.y, lambda step, dz=0: me.at(dy=step, dz=dz)
 
 
-def add_rows(target, base, rows, cols, sources):
+def add_rows(target, base, rows, cols, sources, shift=0):
     step = min(rows.size, 64)
 
     @pl.loop(0, rows.size // step)
@@ -236,15 +255,30 @@
         value = base[there, cols].astype(F32)
         for source in sources:
             value = value + source[here, :].astype(F32)
+        there = pl.ds(pl.multiple_of(rows.start + shift + index * step, 8), step)
         target[there, cols] = value.astype(BF16)
 
 
 def weight_sum(me, links, stages, parts, whole, slots, result, done_sem):
     row, rows, col, cols = 0, parts.shape[0], 0, parts.shape[1]
     pieces = []
+    shift = 0
+
+    def moved(place):
+        return pl.ds(pl.multiple_of(place.start + shift, 8), place.size)
+
     for index, ((kind, axis), slot) in enumerate(zip(stages, slots)):
-        target = whole if index == len(stages) - 1 else parts
+        target, add = (whole, shift) if index == len(stages) - 1 else (parts, 0)
         across = pl.ds(col, cols)
+        if kind == "summed":
+            spot, to = ring(me, axis)
+            shift = spot * rows
+
+            def chunk(step, rows=rows, spot=spot):
+                return pl.ds(lax.rem(spot + step, 4) * rows - spot * rows, rows)
+
+            pieces.append((chunk, across))
+            continue
 
         if kind == "pair":
             here = pl.ds(row, rows)
@@ -252,10 +286,10 @@
             own = pl.ds(pl.multiple_of(col + me.z * cols, 128), cols)
             other = pl.ds(pl.multiple_of(col + (1 - me.z) * cols, 128), cols)
             made = links.send(parts.at[here, other], slot, me.at(dz=1))
-            pieces.append((here, own))
+            pieces.append((moved(here), own))
             yield
             made.wait_recv()
-            add_rows(target, parts, here, own, [slot])
+            add_rows(target, parts, here, own, [slot], add)
             col = own.start
             continue
         spot, to = ring(me, axis)
@@ -267,7 +301,7 @@
                 place = lax.rem(spot + step, 4) * 2 + z
                 return pl.ds(pl.multiple_of(col + place * cols, 128), cols)
 
-            pieces.append((here, strip))
+            pieces.append((moved(here), strip))
             moves = []
             for step, dz in PLANE:
                 piece = parts.at[here, strip(step, lax.rem(me.z + dz, 2))]
@@ -276,14 +310,12 @@
             for made in moves:
                 made.wait_recv()
             mine = strip(0, me.z)
-            add_rows(target, parts, here, mine, [slot.at[index] for index in range(7)])
+            add_rows(target, parts, here, mine, [slot.at[index] for index in range(7)], add)
             continue
-        rows = rows // (8 if kind == "plane" else 4)
-
-        def chunk(step, z=None, row=row, rows=rows, spot=spot):
-            place = lax.rem(spot + step, 4)
-            place = place if z is None else place * 2 + z
-            return pl.ds(pl.multiple_of(row + place * rows, 8), rows)
+        rows = rows // 4
+
+        def chunk(step, row=row, rows=rows, spot=spot):
+            return pl.ds(pl.multiple_of(row + lax.rem(spot + step, 4) * rows, 8), rows)
 
         pieces.append((chunk, across))
         if kind == "ring":
@@ -307,9 +339,9 @@
             yield
             for made in near:
                 made.wait_recv()
-            add_rows(target, parts, chunk(0), across, [main_up, main_down])
+            add_rows(target, parts, chunk(0), across, [main_up, main_down], add)
             row = chunk(0).start
-        elif kind == "direct":
+        else:
             moves = [
                 links.send(parts.at[chunk(step), across], slot.at[step - 1], to(step))
                 for step in (1, 3, 2)
@@ -317,46 +349,35 @@
             yield
             for made in moves:
                 made.wait_recv()
-            add_rows(target, parts, chunk(0), across, [slot.at[step] for step in range(3)])
+            add_rows(target, parts, chunk(0), across, [slot.at[step] for step in range(3)], add)
             row = chunk(0).start
-        else:
-            moves = []
-            for step, dz in PLANE:
-                piece = parts.at[chunk(step, lax.rem(me.z + dz, 2)), across]
-                moves.append(links.send(piece, slot.at[step * 2 + dz - 1], to(step, dz)))
-            yield
-            for made in moves:
-                made.wait_recv()
-            mine = chunk(0, me.z)
-            add_rows(target, parts, mine, across, [slot.at[index] for index in range(7)])
-            row = mine.start
     for (kind, axis), (place, across) in zip(stages[::-1], pieces[::-1]):
         if kind == "pair":
             piece = whole.at[place, across]
             moves = [links.send(piece, piece, me.at(dz=1))]
             yield
-        elif kind in ("plane", "columns"):
+        elif kind == "columns":
             _, to = ring(me, axis)
-            piece = whole.at[place, across(0, me.z)] if kind == "columns" else whole.at[place(0, me.z), across]
+            piece = whole.at[place, across(0, me.z)]
             moves = [links.send(piece, piece, to(step, dz)) for step, dz in PLANE]
             yield
         elif kind == "direct":
             _, to = ring(me, axis)
-            piece = whole.at[place(0), across]
+            piece = whole.at[moved(place(0)), across]
             moves = [links.send(piece, piece, to(step)) for step in (1, 3, 2)]
             yield
         else:
             _, to = ring(me, axis)
             half = across.size // 2
-            piece = whole.at[place(0), across]
+            piece = whole.at[moved(place(0)), across]
             above = links.send(piece, piece, to(1))
             below = links.send(piece, piece, to(3))
             yield
             above.wait_recv()
-            piece = whole.at[place(3), pl.ds(across.start, half)]
+            piece = whole.at[moved(place(3)), pl.ds(across.start, half)]
             moves = [links.send(piece, piece, to(1))]
             below.wait_recv()
-            piece = whole.at[place(1), pl.ds(across.start + half, half)]
+            piece = whole.at[moved(place(1)), pl.ds(across.start + half, half)]
             moves.append(links.send(piece, piece, to(3)))
             yield
         for made in moves:
@@ -367,6 +388,41 @@
     copy.wait()
 
 
+def head_sum(me, links, parts, whole, slots, result, done_sem, wide_last):
+    count = parts.shape[0] // 8
+
+    def rows(step, z):
+        place = lax.rem(me.y + step, 4) * 2 + z
+        return pl.ds(pl.multiple_of(place * count, count), count)
+
+    moves = []
+    for step, dz in PLANE:
+        piece = parts.at[rows(step, lax.rem(me.z + dz, 2))]
+        moves.append(links.send(piece, slots.at[step * 2 + dz - 1], me.at(dy=step, dz=dz)))
+    yield
+    for made in moves:
+        made.wait_recv()
+    mine = rows(0, me.z)
+    value = parts[mine, :].astype(F32)
+    for index in range(7):
+        value = value + slots[index].astype(F32)
+    whole[me.x, mine, :] = value.astype(BF16)
+    for plane in (not wide_last, wide_last):
+        if plane:
+            piece = whole.at[:, mine] if wide_last else whole.at[me.x, mine]
+            moves = [links.send(piece, piece, me.at(dy=step, dz=dz)) for step, dz in PLANE]
+        else:
+            piece = whole.at[me.x, mine] if wide_last else whole.at[me.x]
+            moves = [links.send(piece, piece, me.at(dx=step)) for step in (1, 3, 2)]
+        yield
+        for made in moves:
+            made.wait_recv()
+    copy = pltpu.make_async_copy(whole, result, done_sem)
+    copy.start()
+    yield
+    copy.wait()
+
+
 PLANE = [(1, 0), (3, 0), (0, 1), (1, 1), (3, 1), (2, 0), (2, 1)]
 
 
@@ -390,10 +446,77 @@
     total[...] = line[0] + line[1] + line[2] + line[3]
 
 
-def advance(jobs):
-    for job in list(jobs):
-        if next(job, "done") == "done":
-            jobs.remove(job)
+def x_share(me, links, slots):
+    half = pl.ds(pl.multiple_of(me.core * 128, 128), 128)
+    piece = slots.at[me.x, half]
+    return [links.send(piece, piece, me.at(dx=step)) for step in (1, 3, 2)]
+
+
+def core_share(me, links, slots, moves):
+    half = pl.ds(pl.multiple_of(me.core * 128, 128), 128)
+    passed = []
+    for step, made in zip((3, 1, 2), moves):
+        made.wait_recv()
+        piece = slots.at[lax.rem(me.x + step, 4), half]
+        passed.append(links.send(piece, piece, me.at(dcore=1)))
+    return passed
+
+
+PLAN = {
+    "norm crossed": ("up", "first",),
+    "norm back": ("up",),
+    "heads sent": ("o",),
+    "query one": ("up",),
+    "query two": ("down",),
+    "query three": ("up", "o",),
+    "query four": ("up", "down",),
+    "far wait": ("o", "up", "down",),
+    "key one": ("down",),
+    "vectors": ("o",),
+    "key two": ("first", "vectors",),
+    "key three": ("up",),
+    "key four": ("down", "vectors", "first",),
+    "head sums": ("kv", "q",),
+    "low wait": ("down", "kv", "up",),
+    "low back": ("q", "kv", "o", "o",),
+    "last vectors": ("last",),
+    "input ready": ("vectors", "q", "last", "kv", "kv", "up", "up",),
+    "end": ("q", "down", "down", "last", "q",),
+}
+
+
+def share(me, links, slots):
+    moves = x_share(me, links, slots)
+    yield
+    passed = core_share(me, links, slots, moves)
+    yield
+    for made in passed:
+        made.wait_recv()
+
+
+class Jobs:
+    def __init__(self):
+        self.live = {}
+
+    def add(self, name, job):
+        self.live[name] = job
+
+    def step(self, name):
+        if name in self.live and next(self.live[name], "done") == "done":
+            del self.live[name]
+
+    def drain(self, name):
+        while name in self.live:
+            self.step(name)
+
+    def at(self, place):
+        for name in PLAN.get(place, ()):
+            self.step(name)
+
+    def finish(self):
+        while self.live:
+            for name in list(self.live):
+                self.step(name)
 
 
 def list_mates(image_ref, next_of, mates, own):
@@ -415,28 +538,25 @@
         lax.fori_loop(0, 16, list_one, first)
 
 
-UP_STAGES = [("ring", "x"), ("direct", "y"), ("pair", None)]
-DOWN_STAGES = [("ring", "y"), ("direct", "x"), ("pair", None)]
+UP_STAGES = [("ring", "y"), ("direct", "x"), ("pair", None)]
+DOWN_STAGES = [("summed", "x"), ("direct", "y"), ("pair", None)]
 O_STAGES = [("direct", "x"), ("columns", "y")]
-Q_STAGES = [("direct", "y"), ("plane", "x")]
-K_STAGES = [("direct", "x"), ("plane", "y")]
-V_STAGES = [("direct", "y"), ("plane", "x")]
 
 
 def layer_kernel(
     x_hbm, cot_hbm, gain_one_ref, shift_one_ref, weight_hbm, attend_bias_ref, output_hbm,
     output_bias_ref, gain_two_ref, shift_two_ref, up_hbm, up_bias_ref, down_hbm, down_bias_ref,
     image_ref,
-    result_out, input_out, vector_out, last_out, up_out, down_out, qkv_out, o_out,
+    result_out, input_out, vector_out, last_out, up_out, down_out, kv_out, q_out, o_out,
     x_ref, cot_ref, weight_ref, up_ref, down_ref,
-    first_low, kv, query_pair, kv_send, query_send, query_own, top, total, mixed,
+    first_all, down_all, activated_all, kv, query_pair, kv_send, query_send, query_own, top, total, mixed,
     head_send, head_recv, attended, output_all, next_of, mates,
-    hidden, xhat_two, inverse_two, second_low, down_grad, activated, pre_grad,
+    hidden, xhat_two, inverse_two, second_low, activated, pre_grad,
     branch_low, norm_parts, unit_parts, low_parts,
     grad_send, grad_pair, stats_all, grad_own, rows_all, query_grad_all,
-    qg_send, qg_recv, kvg_send, kvg_recv, stacked,
+    qg_own, qg_send, qg_recv, kvg_send, kvg_recv, stacked, flat,
     vector, plane_one, line_one, last, plane_two, line_two,
-    job_up, job_down, job_q, job_k, job_v, job_o,
+    job_up, job_down, job_kv, job_q, job_o,
     send_sem, recv_sem, load_sem, done_sem,
 ):
     me = Place()
@@ -444,8 +564,8 @@
     at = me.high * 2 + me.core
     loads = []
     for source, target in (
-        (x_hbm, x_ref), (weight_hbm, weight_ref), (output_hbm, output_all.at[at]), (up_hbm, up_ref),
-        (down_hbm, down_ref), (cot_hbm, cot_ref),
+        (x_hbm, x_ref), (weight_hbm, weight_ref), (output_hbm, output_all.at[at]),
+        (cot_hbm, cot_ref), (up_hbm, up_ref), (down_hbm, down_ref),
     ):
         load = pltpu.make_async_copy(source, target, load_sem.at[len(loads)])
         load.start()
@@ -454,10 +574,11 @@
     own = me.group
     loads[0].wait()
     normed, _ = row_norm(x_ref[...])
-    first_low[...] = (normed * gain_one_ref[...] + shift_one_ref[...]).astype(BF16)
+    first_low = (normed * gain_one_ref[...] + shift_one_ref[...]).astype(BF16)
+    first_all[me.x] = first_low
     loads[1].wait()
-    keys = dot_nn(first_low[...], weight_ref[1])
-    values = dot_nn(first_low[...], weight_ref[2]) + attend_bias_ref[1:2, :]
+    keys = dot_nn(first_low, weight_ref[1])
+    values = dot_nn(first_low, weight_ref[2]) + attend_bias_ref[1:2, :]
     for head in range(4):
         part = slice(head * HEAD_DIM, (head + 1) * HEAD_DIM)
         kv_send[head] = jnp.concatenate([keys[:, part], values[:, part]], axis=1).astype(BF16)
@@ -466,7 +587,11 @@
     for step in (1, 3, 2):
         head = lax.rem(me.x + step, 4)
         kv_moves.append(links.send(kv_send.at[head], kv.at[own * 4 + me.x], me.at(dx=step)))
-    queries = dot_nn(first_low[...], weight_ref[0]) + attend_bias_ref[0:1, :]
+    loads[2].wait()
+    quarter = pl.ds(pl.multiple_of(me.x * 64, 64), 64)
+    piece = output_all.at[at, quarter]
+    output_high = links.send(piece, piece, me.at(dhigh=1))
+    queries = dot_nn(first_low, weight_ref[0]) + attend_bias_ref[0:1, :]
     pack_heads(queries.astype(BF16).astype(F32) * (HEAD_DIM**-0.5), query_send)
     for step in (1, 3, 2):
         head = lax.rem(me.x + step, 4)
@@ -475,6 +600,10 @@
         )
     kv[own * 4 + me.x] = kv_send[me.x]
     query_pair[own * 4 + me.x] = query_send[me.x]
+    output_core = links.send(output_all.at[at], output_all.at[at], me.at(dcore=1))
+    loads[3].wait()
+    down_all[me.x] = cot_ref[...].astype(BF16)
+    down_moves = x_share(me, links, down_all)
     for made in kv_moves:
         made.wait_recv()
     gather = Gather(me, links, kv)
@@ -526,26 +655,21 @@
         def _(side):
             attend(gather.slot(3 - 2 * side, z))
 
+    across = (1 - me.high) * 2 + me.core
+    output_high.wait_recv()
+    piece = output_all.at[across, quarter]
+    output_moves = [links.send(piece, piece, me.at(dx=step)) for step in (1, 3, 2)]
     attend(own)
     gather.pass_z()
     attend(gather.slot(0, gather.other))
     gather.pass_own()
     attend_near(me.z)
     gather.pass_other()
+    gather.end_own()
+    attend(gather.slot(2, me.z))
     gather.end_near()
     attend_near(gather.other)
-    gather.end_own()
-    loads[2].wait()
-    quarter = pl.ds(pl.multiple_of(me.x * 64, 64), 64)
-    piece = output_all.at[at, quarter]
-    output_high = links.send(piece, piece, me.at(dhigh=1))
-    output_core = links.send(output_all.at[at], output_all.at[at], me.at(dcore=1))
-    attend(gather.slot(2, me.z))
     gather.end_other()
-    across = (1 - me.high) * 2 + me.core
-    output_high.wait_recv()
-    piece = output_all.at[across, quarter]
-    output_moves = [links.send(piece, piece, me.at(dx=step)) for step in (1, 3, 2)]
     query_gather = Gather(me, links, query_pair)
     query_gather.begin()
     attend(gather.slot(2, gather.other))
@@ -556,28 +680,33 @@
         top[block] = top[block] + jnp.log(sums)
         back = pltpu.roll(out[:128, :], 64, 1)
         head_send[block] = jnp.where(lanes_below(back.shape), back, out[128:, :]).astype(BF16)
-    head_moves = []
+    head_moves, high_moves = [], []
     for step in (1, 3, 2):
-        to = lax.rem(me.x + step, 4)
-        head_moves.append(links.send(head_send.at[to], head_recv.at[me.x], me.at(dx=step)))
+        piece = head_send.at[lax.rem(me.x + step, 4)]
+        head_moves.append(links.send(piece, head_recv.at[me.x], me.at(dx=step)))
+        high_moves.append(links.send(piece, head_recv.at[me.x + 4], me.at(dx=step, dhigh=1)))
+    high_moves.append(
+        links.send(head_send.at[me.x], head_recv.at[me.x + 4], me.at(dhigh=1))
+    )
     head_recv[me.x] = head_send[me.x]
     for made in output_moves:
         made.wait_recv()
     output_pass = links.send(output_all.at[across], output_all.at[across], me.at(dcore=1))
+    down_pass = core_share(me, links, down_all, down_moves)
     for block in range(4):
         stats_all[own, block : block + 1, :] = top[block].T[0:1, :]
     for made in head_moves:
         made.wait_recv()
-    attended[at] = unpack_heads(head_recv)
-    here = attended.at[at]
-    attended_high = links.send(here, here, me.at(dhigh=1))
-    attended_core = links.send(here, here, me.at(dcore=1))
+    attended[at] = unpack_heads(head_recv.at[0:4])
+    attended_core = links.send(attended.at[at], attended.at[at], me.at(dcore=1))
     query_gather.pass_z()
+    for made in high_moves:
+        made.wait_recv()
+    attended[across] = unpack_heads(head_recv.at[4:8])
+    attended_pass = links.send(attended.at[across], attended.at[across], me.at(dcore=1))
     query_gather.pass_own()
     output_core.wait_recv()
     output_pass.wait_recv()
-    attended_high.wait_recv()
-    attended_pass = links.send(attended.at[across], attended.at[across], me.at(dcore=1))
     query_gather.pass_other()
     attended_core.wait_recv()
     attended_pass.wait_recv()
@@ -594,16 +723,14 @@
     xhat_two[...] = normed
     inverse_two[...] = spread(inverse)
     second_low[...] = (normed * gain_two_ref[...] + shift_two_ref[...]).astype(BF16)
+    loads[4].wait()
     loads[5].wait()
-    down_grad[...] = cot_ref[...].astype(BF16)
-    loads[3].wait()
-    loads[4].wait()
 
     @pl.loop(0, 4)
     def _(step):
         cols = cols_of(step)
         pre = dot_nn(second_low[...], up_ref[:, cols]) + up_bias_ref[:, cols]
-        back = dot_nt(down_grad[...], down_ref[cols, :])
+        back = dot_nt(down_all[me.x], down_ref[cols, :])
         chance = 0.5 + 0.5 * lax.erf(pre * (0.5**0.5))
         density = jnp.exp(-0.5 * pre * pre) * 0.3989422804014327
         activated[:, cols] = (pre * chance).astype(BF16)
@@ -611,33 +738,48 @@
         pre_grad[:, cols] = low
         vector[4:5, cols] = jnp.sum(low.astype(F32), axis=0, keepdims=True)
 
+    act_moves = []
+    for step in (1, 3, 2):
+        piece = activated.at[:, cols_of(lax.rem(me.x + step, 4))]
+        act_moves.append(links.send(piece, activated_all.at[me.x], me.at(dx=step)))
     norm_sum = ModelSum(me, links, *norm_parts)
     norm_sum.begin(lambda cols: dot_nt(pre_grad[...], up_ref[cols, :]))
+
+    for side in range(2):
+
+        @pl.loop(2 * side, 2 * side + 2)
+        def _(step):
+            cols = cols_of(step)
+            job_up[0][cols, :] = dot_tn(second_low[:, cols], pre_grad[...]).astype(BF16)
+
+        norm_sum.cross(side)
+
+    jobs = Jobs()
+    jobs.add("first", share(me, links, first_all))
+    jobs.add("up", weight_sum(me, links, UP_STAGES, *job_up, up_out, done_sem.at[0]))
+    query_gather.end_near()
+    query_gather.end_own()
+    query_gather.end_other()
+    jobs.at("norm crossed")
+    unit_sum = ModelSum(me, links, *unit_parts)
+    unit_sum.begin(lambda cols: dot_nn(activated[...], down_ref[:, cols]))
+    vector[3:4, :] = jnp.sum(down_all[me.x].astype(F32), axis=0, keepdims=True)
+    activated_all[me.x] = activated[:, cols_of(me.x)]
+    for made in down_pass + act_moves:
+        made.wait_recv()
 
     @pl.loop(0, 4)
     def _(step):
         cols = cols_of(step)
-        job_down[0][cols, :] = dot_tn(activated[:, cols], down_grad[...]).astype(BF16)
-
-    downs = [weight_sum(me, links, DOWN_STAGES, *job_down, down_out, done_sem.at[1])]
-    norm_sum.cross()
-    query_gather.end_near()
-    query_gather.end_own()
-    query_gather.end_other()
-    advance(downs)
-
-    @pl.loop(0, 4)
-    def _(step):
-        cols = cols_of(step)
-        job_up[0][cols, :] = dot_tn(second_low[:, cols], pre_grad[...]).astype(BF16)
-
-    ups = [weight_sum(me, links, UP_STAGES, *job_up, up_out, done_sem.at[0])]
-    advance(ups)
-    unit_sum = ModelSum(me, links, *unit_parts)
-    unit_sum.begin(lambda cols: dot_nn(activated[...], down_ref[:, cols]))
-    vector[3:4, :] = jnp.sum(down_grad[...].astype(F32), axis=0, keepdims=True)
-    advance(downs)
+        value = dot_tn(activated_all[0], down_all[0, :, cols])
+        for spot in range(1, 4):
+            value = value + dot_tn(activated_all[spot], down_all[spot, :, cols])
+        job_down[0][:, cols] = value.astype(BF16)
+
+    jobs.add("down", weight_sum(me, links, DOWN_STAGES, *job_down, down_out, done_sem.at[1]))
+    jobs.at("partner wait")
     norm_sum.back()
+    jobs.at("norm back")
     norm_sum.end()
     grad = norm_sum.full[...].astype(F32)
     xhat = xhat_two[...]
@@ -659,13 +801,14 @@
         head = lax.rem(me.x + step, 4)
         moves.append(links.send(grad_send.at[head], grad_pair.at[own * 4 + me.x], me.at(dx=step)))
     grad_pair[own * 4 + me.x] = grad_send[me.x]
-    advance(ups)
 
     @pl.loop(0, 4)
     def _(step):
         cols = cols_of(step)
         job_o[0][:, cols] = dot_tn(attended[at], branch_low[:, cols]).astype(BF16)
 
+    jobs.add("o", weight_sum(me, links, O_STAGES, *job_o, o_out, done_sem.at[2]))
+    jobs.at("heads sent")
     for made in moves:
         made.wait_recv()
     gather = Gather(me, links, grad_pair)
@@ -699,8 +842,9 @@
                 keys.append(key)
             return acc + dot_nn(jnp.concatenate(changes, axis=1), jnp.concatenate(keys, axis=0))
 
-        acc = lax.fori_loop(0, 2, some, jnp.zeros((256, 128), F32))
-        qg_send[block] = pack_rows(acc * (HEAD_DIM**-0.5)).astype(BF16)
+        acc = lax.fori_loop(0, 2, some, jnp.zeros((256, 128), F32)) * (HEAD_DIM**-0.5)
+        qg_own[block] = acc.astype(BF16)
+        qg_send[block] = pack_rows(acc).astype(BF16)
 
     query_moves = []
 
@@ -725,34 +869,35 @@
             rows_all[spot, 0:1, :] = stats_all[slot, pl.ds(block, 1), :]
             rows_all[spot, 1:2, :] = stats_all[slot, pl.ds(block + 4, 1), :]
 
+    jobs.at("gather begun")
     send_query(2)
+    jobs.at("query one")
+    send_query(1)
     gather.pass_z()
-    advance(downs)
-    send_query(1)
     gather.pass_own()
-    outs = [weight_sum(me, links, O_STAGES, *job_o, o_out, done_sem.at[5])]
-    advance(outs)
-    advance(ups)
+    jobs.at("query two")
     for made in stats_moves:
         made.wait_recv()
     pair_up(own)
     pair_up(gather.slot(0, gather.other))
     send_query(3)
     gather.pass_other()
+    gather.end_own()
+    jobs.at("query three")
     pair_up(gather.slot(1, me.z))
     pair_up(gather.slot(3, me.z))
     send_query(0)
-    gather.end_own()
-    advance(downs)
+    jobs.at("query four")
     gather.end_near()
     pair_up(gather.slot(2, me.z))
     pair_up(gather.slot(1, gather.other))
     pair_up(gather.slot(3, gather.other))
+    jobs.at("far wait")
     gather.end_other()
     pair_up(gather.slot(2, gather.other))
-    advance(ups)
-    advance(downs)
-    advance(outs)
+    unit_sum.cross(0)
+    unit_sum.cross(1)
+    jobs.at("gathered")
 
     def key_pass(block):
         both = kv[own * 4 + block].astype(F32)
@@ -792,54 +937,63 @@
             kvg_recv[me.x] = kvg_send[me.x]
 
     send_key(2)
-    advance(ups)
+    jobs.at("key one")
+    vector[5:8, :] = jnp.zeros((3, 1024), F32)
+    jobs.add("vectors", vector_sum(me, links, vector, plane_one, line_one, vector_out))
+    jobs.at("vectors")
+    send_key(1)
+    jobs.at("key two")
     for made in query_moves:
         made.wait_recv()
     stacked[:, 0:256] = unpack_heads(qg_recv)
-    job_q[0][...] = dot_tn(first_low[...], stacked[:, 0:256]).astype(BF16)
-    jobs = [weight_sum(me, links, Q_STAGES, *job_q, qkv_out.at[0], done_sem.at[2])]
-    advance(jobs)
-    advance(outs)
-    send_key(1)
-    advance(downs)
     send_key(3)
-    advance(ups)
+    jobs.at("key three")
     send_key(0)
-    advance(jobs)
-    advance(outs)
+    unit_sum.back()
+    jobs.at("key four")
+
+    jobs.drain("first")
+
+    def own_grads(block):
+        return jnp.concatenate([kvg_send[block], qg_own[block]], axis=1)
+
+    @pl.loop(0, 4)
+    def _(step):
+        cols = cols_of(step)
+        value = dot_tn(first_all[0, :, cols], own_grads(0))
+        for spot in range(1, 4):
+            value = value + dot_tn(first_all[spot, :, cols], own_grads(spot))
+        job_kv[0][cols, :] = value[:, :128].astype(BF16)
+        flat[cols, :] = value[:, 128:]
+
+    job_q[0][...] = jnp.where(
+        lanes_below((512, 128)), flat[0:512, :], pltpu.roll(flat[512:1024, :], 64, 1)
+    ).astype(BF16)
+    jobs.add("kv", head_sum(me, links, *job_kv, kv_out, done_sem.at[3], False))
+    jobs.add("q", head_sum(me, links, *job_q, q_out, done_sem.at[4], True))
+    jobs.at("head sums")
     for made in key_moves:
         made.wait_recv()
 
-    heads = [kvg_recv[head].astype(F32) for head in range(4)]
-    stacked[:, 256:512] = jnp.concatenate([value[:, :64] for value in heads], axis=1).astype(BF16)
-    stacked[:, 512:768] = jnp.concatenate([value[:, 64:] for value in heads], axis=1).astype(BF16)
+    back = [kvg_recv[head].astype(F32) for head in range(4)]
+    stacked[:, 256:512] = jnp.concatenate([value[:, :64] for value in back], axis=1).astype(BF16)
+    stacked[:, 512:768] = jnp.concatenate([value[:, 64:] for value in back], axis=1).astype(BF16)
     low_sum = ModelSum(me, links, *low_parts)
     low_sum.begin(
         lambda cols: dot_nt(stacked[:, 0:256], weight_ref[0, cols, :])
         + dot_nt(stacked[:, 256:512], weight_ref[1, cols, :])
         + dot_nt(stacked[:, 512:768], weight_ref[2, cols, :])
     )
-    job_k[0][...] = dot_tn(first_low[...], stacked[:, 256:512]).astype(BF16)
-    job_v[0][...] = dot_tn(first_low[...], stacked[:, 512:768]).astype(BF16)
-    pairs = [
-        weight_sum(me, links, K_STAGES, *job_k, qkv_out.at[1], done_sem.at[3]),
-        weight_sum(me, links, V_STAGES, *job_v, qkv_out.at[2], done_sem.at[4]),
-    ]
-    advance(pairs)
-    low_sum.cross()
-    unit_sum.cross()
-    vector[5:6, 0:256] = jnp.sum(stacked[:, 0:256].astype(F32), axis=0, keepdims=True)
-    vector[5:6, 256:512] = jnp.sum(stacked[:, 512:768].astype(F32), axis=0, keepdims=True)
-    vector[5:6, 512:1024] = jnp.zeros((1, 512), F32)
-    vector[6:8, :] = jnp.zeros((2, 1024), F32)
-    vectors = [vector_sum(me, links, vector, plane_one, line_one, vector_out)]
-    advance(vectors)
-    advance(jobs)
-    advance(downs)
-    advance(ups)
+    low_sum.cross(0)
+    last[8:9, :] = jnp.sum(stacked[:, 0:256].astype(F32), axis=0, keepdims=True)
+    last[9:10, :] = jnp.sum(stacked[:, 512:768].astype(F32), axis=0, keepdims=True)
+    last[10:16, :] = jnp.zeros((6, 256), F32)
+    low_sum.cross(1)
+    jobs.at("low crossed")
     xhat, inverse = row_norm(x_ref[...])
+    jobs.at("low wait")
     low_sum.back()
-    advance(pairs)
+    jobs.at("low back")
     low_sum.end()
     grad = low_sum.full[...].astype(F32)
     gain_grad = jnp.sum(grad * xhat, axis=0, keepdims=True)
@@ -848,8 +1002,8 @@
         cols = slice(part * 256, (part + 1) * 256)
         last[part : part + 1, :] = gain_grad[:, cols]
         last[part + 4 : part + 5, :] = shift_grad[:, cols]
-    vectors.append(vector_sum(me, links, last, plane_two, line_two, last_out))
-    advance(vectors)
+    jobs.add("last", vector_sum(me, links, last, plane_two, line_two, last_out))
+    jobs.at("last vectors")
     scaled = grad * gain_one_ref[...]
     cot_ref[...] = cot_ref[...] + (
         scaled
@@ -858,14 +1012,13 @@
     ) * inverse
     input_done = pltpu.make_async_copy(cot_ref, input_out, done_sem.at[6])
     input_done.start()
-    unit_sum.back()
     unit_sum.end()
     hidden[...] = hidden[...] + unit_sum.full[...].astype(F32) + down_bias_ref[...]
     result_done = pltpu.make_async_copy(hidden, result_out, done_sem.at[7])
     result_done.start()
-    jobs = pairs + vectors + jobs + ups + downs + outs
-    while jobs:
-        advance(jobs)
+    jobs.at("input ready")
+    jobs.at("end")
+    jobs.finish()
     input_done.wait()
     result_done.wait()
     links.finish()
@@ -882,16 +1035,24 @@
         elif kind == "direct":
             rows = rows // 4
             slots.append(pltpu.VMEM((3, rows, cols), BF16))
-        elif kind == "plane":
-            rows = rows // 8
-            slots.append(pltpu.VMEM((7, rows, cols), BF16))
+        elif kind == "summed":
+            slots.append(pltpu.SMEM((1,), jnp.int32))
         elif kind == "columns":
             cols = cols // 8
             slots.append(pltpu.VMEM((7, rows, cols), BF16))
         else:
             cols = cols // 2
             slots.append(pltpu.VMEM((rows, cols), BF16))
-    return [pltpu.VMEM((height, width), BF16), pltpu.VMEM((height, width), BF16), slots]
+    full = height * 4 if stages[0][0] == "summed" else height
+    return [pltpu.VMEM((height, width), BF16), pltpu.VMEM((full, width), BF16), slots]
+
+
+def head_scratch(rows):
+    return [
+        pltpu.VMEM((rows, 128), BF16),
+        pltpu.VMEM((4, rows, 128), BF16),
+        pltpu.VMEM((7, rows // 8, 128), BF16),
+    ]
 
 
 def sum_scratch():
@@ -912,19 +1073,22 @@
             jax.ShapeDtypeStruct((256, 1024), F32),
             jax.ShapeDtypeStruct((256, 1024), F32),
             jax.ShapeDtypeStruct((8, 1024), F32),
-            jax.ShapeDtypeStruct((8, 256), F32),
+            jax.ShapeDtypeStruct((16, 256), F32),
             jax.ShapeDtypeStruct((1024, 1024), BF16),
             jax.ShapeDtypeStruct((1024, 1024), BF16),
-            jax.ShapeDtypeStruct((3, 1024, 256), BF16),
+            jax.ShapeDtypeStruct((4, 1024, 128), BF16),
+            jax.ShapeDtypeStruct((4, 512, 128), BF16),
             jax.ShapeDtypeStruct((256, 1024), BF16),
         ],
         in_specs=[hbm, hbm, vmem, vmem, hbm, vmem, hbm, vmem, vmem, vmem, hbm, vmem, hbm, vmem, smem],
-        out_specs=[hbm] * 2 + [vmem] * 2 + [hbm] * 4,
+        out_specs=[hbm] * 2 + [vmem] * 2 + [hbm] * 5,
         scratch_shapes=[
             wide_rows, wide_rows,
             pltpu.VMEM((3, 1024, 256), BF16),
             pltpu.VMEM((1024, 1024), BF16), pltpu.VMEM((1024, 1024), BF16),
-            low_rows,
+            pltpu.VMEM((4, 256, 1024), BF16),
+            pltpu.VMEM((4, 256, 1024), BF16),
+            pltpu.VMEM((4, 256, 256), BF16),
             pltpu.VMEM((32, 256, 128), BF16),
             pltpu.VMEM((32, 128, 128), BF16),
             pltpu.VMEM((4, 256, 128), BF16),
@@ -934,13 +1098,13 @@
             pltpu.VMEM((4, 256, 128), F32),
             pltpu.VMEM((4, 256, 128), F32),
             pltpu.VMEM((4, 128, 128), BF16),
-            pltpu.VMEM((4, 128, 128), BF16),
+            pltpu.VMEM((8, 128, 128), BF16),
             pltpu.VMEM((4, 256, 256), BF16),
             pltpu.VMEM((4, 256, 1024), BF16),
             pltpu.SMEM((32,), jnp.int32),
             pltpu.SMEM((64,), jnp.int32),
             wide_rows, wide_rows, pltpu.VMEM((256, 128), F32),
-            low_rows, low_rows, low_rows, low_rows, low_rows,
+            low_rows, low_rows, low_rows, low_rows,
             sum_scratch(), sum_scratch(), sum_scratch(),
             pltpu.VMEM((4, 128, 128), BF16),
             pltpu.VMEM((32, 128, 128), BF16),
@@ -948,18 +1112,19 @@
             pltpu.VMEM((4, 256, 128), BF16),
             pltpu.VMEM((32, 8, 256), F32),
             pltpu.VMEM((32, 256, 128), BF16),
+            pltpu.VMEM((4, 256, 128), BF16),
             pltpu.VMEM((4, 128, 128), BF16),
             pltpu.VMEM((4, 128, 128), BF16),
             pltpu.VMEM((4, 256, 128), BF16),
             pltpu.VMEM((4, 256, 128), BF16),
             pltpu.VMEM((256, 768), BF16),
+            pltpu.VMEM((1024, 128), F32),
             pltpu.VMEM((8, 1024), F32), pltpu.VMEM((8, 8, 1024), F32), pltpu.VMEM((4, 8, 1024), F32),
-            pltpu.VMEM((8, 256), F32), pltpu.VMEM((8, 8, 256), F32), pltpu.VMEM((4, 8, 256), F32),
+            pltpu.VMEM((16, 256), F32), pltpu.VMEM((8, 16, 256), F32), pltpu.VMEM((4, 16, 256), F32),
             job_scratch(1024, 1024, UP_STAGES),
-            job_scratch(1024, 1024, DOWN_STAGES),
-            job_scratch(1024, 256, Q_STAGES),
-            job_scratch(1024, 256, K_STAGES),
-            job_scratch(1024, 256, V_STAGES),
+            job_scratch(256, 1024, DOWN_STAGES),
+            head_scratch(1024),
+            head_scratch(512),
             job_scratch(256, 1024, O_STAGES),
             pltpu.SemaphoreType.DMA((240,)),
             pltpu.SemaphoreType.DMA((240,)),
@@ -973,13 +1138,19 @@
 
 
 def widen_kernel(
-    up, down, qkv, o, result, input_grad, vector, last,
+    up, down, kv, q, o, result, input_grad, vector, last,
     up_out, down_out, qkv_out, o_out, result_out, input_out,
     first_gain, first_shift, bias, output_bias, second_gain, second_shift, up_bias, down_bias,
 ):
     up_out[...] = up[...].astype(F32)
     down_out[...] = down[...].astype(F32)
-    qkv_out[...] = qkv[...].astype(F32)
+    pairs = [kv[head].astype(F32) for head in range(4)]
+    qkv_out[1] = jnp.concatenate([pair[:, :HEAD_DIM] for pair in pairs], axis=1)
+    qkv_out[2] = jnp.concatenate([pair[:, HEAD_DIM:] for pair in pairs], axis=1)
+    pairs = [q[head].astype(F32) for head in range(4)]
+    upper = jnp.concatenate([pair[:, :HEAD_DIM] for pair in pairs], axis=1)
+    lower = jnp.concatenate([pair[:, HEAD_DIM:] for pair in pairs], axis=1)
+    qkv_out[0] = jnp.where(pl.program_id(0) < pl.num_programs(0) // 2, upper, lower)
     o_out[...] = o[...].astype(F32)
     result_out[...] = result[...]
     input_out[...] = input_grad[...]
@@ -988,15 +1159,14 @@
     def _():
         first_gain[...] = jnp.concatenate([last[row : row + 1, :] for row in range(4)], axis=1)
         first_shift[...] = jnp.concatenate([last[row : row + 1, :] for row in range(4, 8)], axis=1)
-        bias[0:1, :] = vector[5:6, 0:256]
-        bias[1:2, :] = vector[5:6, 256:512]
+        bias[...] = last[8:10, :]
         for target, row in (
             (second_gain, 0), (second_shift, 1), (output_bias, 2), (down_bias, 3), (up_bias, 4),
         ):
             target[...] = vector[row : row + 1, :]
 
 
-def widen(up, down, qkv, o, result, input_grad, vector, last):
+def widen(up, down, kv, q, o, result, input_grad, vector, last):
     steps = 8
     tall = pl.BlockSpec((1024 // steps, 1024), lambda step: (step, 0))
     short = pl.BlockSpec((256 // steps, 1024), lambda step: (step, 0))
@@ -1019,13 +1189,18 @@
             jax.ShapeDtypeStruct((256, 1024), F32),
             row, row, jax.ShapeDtypeStruct((2, 256), F32), row, row, row, row, row,
         ],
-        in_specs=[tall, tall, three, short, short, short, whole((8, 1024)), whole((8, 256))],
+        in_specs=[
+            tall, tall,
+            pl.BlockSpec((4, 1024 // steps, 128), lambda step: (0, step, 0)),
+            pl.BlockSpec((4, 1024 // steps, 128), lambda step: (0, lax.rem(step, steps // 2), 0)),
+            short, short, short, whole((8, 1024)), whole((16, 256)),
+        ],
         out_specs=[
             tall, tall, three, short, short, short,
             line, line, whole((2, 256)), line, line, line, line, line,
         ],
         compiler_params=pltpu.CompilerParams(vmem_limit_bytes=VMEM_BYTES),
-    )(up, down, qkv, o, result, input_grad, vector, last)
+    )(up, down, kv, q, o, result, input_grad, vector, last)
 
 
 def per_device(
@@ -1045,7 +1220,7 @@
     image_of,
     cotangent,
 ):
-    result, input_grad, vector, last, up, down, qkv, o = layer(
+    result, input_grad, vector, last, up, down, kv, q, o = layer(
         inputs, cotangent, first_gain[None], first_shift[None], attend_weight, attend_bias,
         output_weight, output_bias[None], second_gain[None], second_shift[None],
         up_weight, up_bias[None], down_weight, down_bias[None], image_of,
@@ -1053,7 +1228,7 @@
     (
         up, down, qkv, o, result, input_grad, first_gain_grad, first_shift_grad, bias_grad,
         output_bias_grad, second_gain_grad, second_shift_grad, up_bias_grad, down_bias_grad,
-    ) = widen(up, down, qkv, o, result, input_grad, vector, last)
+    ) = widen(up, down, kv, q, o, result, input_grad, vector, last)
     return (
         result, input_grad, first_gain_grad[0], first_shift_grad[0], qkv, bias_grad, o,
         output_bias_grad[0], second_gain_grad[0], second_shift_grad[0], up, up_bias_grad[0], down,

time: 180 us -> 164 us (0.911)
  Pallas kernels: 178 us -> 162 us
    pallas_call x1, Pallas kernels: 168 us -> 152 us  [layer(): pl.pallas_call(layer_kernel, out_shape=[jax.ShapeDtypeStruct((256, 1024),...]
where the time goes in v4:
time: 164 us; the launch traced here: 163 us
  Pallas kernels  162 us (99%)
    pallas_call x1, Pallas kernels, layer(): pl.pallas_call(layer_kernel, out_shape=[jax.ShapeDtypeStruct((256, 1024),...  152 us
    pallas_call x1, Pallas kernels, widen(): pl.pallas_call(widen_kernel, grid=(steps,), out_shape=[jax.ShapeDtypeStru...  10.7 us

profile of v4, /device:TPU:0, one launch (start us, length us, event | category | flops | bytes accessed | tf_op | source)
XLA Modules:
  0.0 163.1 jit_solution(8661392327881014732)
XLA Ops:
  0.7 151.5 %shard_map.254 = (f32[256,1024]{1,0:T(8,128)}, f32[256,1024]{1,0:T(8,128)}, f32[8,1024]{1,0:T(8,128)}, f32[16,256]{1,0:T(8,128)}, bf16[1024,1024]{1,0:T(8,128)(2...) custom-call(f32[256,1024]{1,0:T(8,128)} %x_hbm.1, ...), custom_call_target="tpu_custom_call" | custom-call | tf_op jit(solution)/shard_map/pallas_call | solution.py:1070
  152.2 10.7 %shard_map.255 = (f32[1024,1024]{1,0:T(8,128)}, f32[1024,1024]{1,0:T(8,128)}, f32[3,1024,256]{2,1,0:T(8,128)}, f32[256,1024]{1,0:T(8,128)}, f32[256,1024]{1,0:T(...) custom-call(bf16[1024,1024]{1,0:T(8,128)(2,1)} %get-tuple-element.37, ...), custom_call_target="tpu_custom_call" | custom-call | tf_op jit(solution)/shard_map/pallas_call | solution.py:1180
